TPU v7x, 32 devices: a whole 2x2x4 slice. The times are simulated.
32 devices in a mesh: seq: 8 (over y, x, core), batch: 4 (over z).
Axes of the slice: x: 2, y: 2, z: 4, core: 2. Of those that a mesh axis runs over, the one named last changes fastest.
Arguments:
- tokens: bfloat16 [8, 512, 2048], P('batch', 'seq'), may hold values from -6 to 6
- grad_out: bfloat16 [8, 512, 2048], P('batch', 'seq'), may hold values from -6 to 6
- resets: int32 [8], P('batch'), may hold values from 1 to 512, as said below
- w_proj: bfloat16 [2048, 12288], P(('seq', 'batch')), may hold values from -0.125 to 0.125
- w_small: bfloat16 [2048, 32], P(('seq', 'batch')), may hold values from -0.125 to 0.125
- w_out: bfloat16 [4096, 2048], P(('seq', 'batch')), may hold values from -0.1875 to 0.1875
- w_gu: bfloat16 [2048, 11264], P(('seq', 'batch')), may hold values from -0.125 to 0.125
- w_down: bfloat16 [5632, 2048], P(('seq', 'batch')), may hold values from -0.078125 to 0.078125
- norm_in: float32 [2048], replicated, may hold values from 0.5 to 1.5
- norm_ff: float32 [2048], replicated, may hold values from 0.5 to 1.5
- norm_head: float32 [256], replicated, may hold values from 0.5 to 1.5
- conv_w: float32 [4, 8192], replicated, may hold values from -2.5 to 2.5
- a_log: float32 [16], replicated, may hold values from 0 to 2.77
- dt_bias: float32 [16], replicated, may hold values from -8 to -3
Outputs:
- block_out: bfloat16 [8, 512, 2048], P('batch', 'seq')
- d_tokens: bfloat16 [8, 512, 2048], P('batch', 'seq')
- g_proj: float32 [2048, 12288], P(('seq', 'batch'))
- g_small: float32 [2048, 32], P(('seq', 'batch'))
- g_out: float32 [4096, 2048], P(None, ('seq', 'batch'))
- g_gu: float32 [2048, 11264], P(('seq', 'batch'))
- g_down: float32 [5632, 2048], P(None, ('seq', 'batch'))
- g_norm_in: float32 [2048], replicated
- g_norm_ff: float32 [2048], replicated
- g_norm_head: float32 [256], replicated
- g_conv: float32 [4, 8192], replicated
- g_alog: float32 [16], replicated
- g_dt: float32 [16], replicated
Inputs may be any that keep to these rules, and one draw needn't show every extreme that they name: resets[r] is the position in row r where a second sequence begins, where the state and the short convolution restart; it lies within the first or the last 64 positions of its row, and exactly one row has resets = 512, that row being a single sequence.
All inputs are finite; a program needn't handle non-finite values.
Results may differ from a plain program's by a relative error of at most 0.014.
Values may be sent and summed in bfloat16 or wider, within the bound.
No kernel may reach another device: no remote copies, remote signals or barrier semaphores. Data moves between devices by JAX's collectives and lax.ppermute only.
A program may use at most 960 MiB of HBM per device.

v0:
```python
from functools import partial

import jax
import jax.numpy as jnp
from jax import lax
from jax.sharding import PartitionSpec as P

D = 2048
H = 16
DK = 128
DV = 256
FF = 5632
CH = 64
KW = 2048
VW = 4096
CW = 8192


EPS_NORM = 1e-06
EPS_HEAD = 1e-05
EPS_UNIT = 1e-06
highest = lax.Precision.HIGHEST


def passed_along(block, axis, distance):
    devices = range(lax.axis_size(axis))
    route = [(i - distance, i) for i in devices if i - distance in devices]
    return lax.ppermute(block, axis, route)


def entering(value, axis, combine, identity, reverse):
    devices, here = (lax.axis_size(axis), lax.axis_index(axis))
    everything = jax.tree.map(
        lambda part, kind: lax.all_gather(part.astype(kind), axis),
        value,
        jax.tree.map(lambda a: jnp.bfloat16 if a.dtype == jnp.float32 else a.dtype, value),
    )
    start = jax.tree.map(
        lambda part, zero: jnp.broadcast_to(jnp.asarray(zero, part.dtype), part.shape),
        value,
        identity,
    )

    def step(k, before):
        at = devices - 1 - k if reverse else k
        reached = at > here if reverse else at < here
        new = combine(
            before, jax.tree.map(lambda part, own: part[at].astype(own.dtype), everything, value)
        )
        return jax.tree.map(lambda a, b: jnp.where(reached, a, b), new, before)

    return lax.fori_loop(0, devices, step, start)


def matmul_high(left_op, right_op):
    return jnp.matmul(left_op, right_op, precision=highest)


def contract_rows(left_op, right_op):
    return lax.dot_general(
        left_op, right_op, (((0,), (0,)), ((), ())), preferred_element_type=jnp.float32
    )


def contract_cols(left_op, right_op):
    return lax.dot_general(
        left_op, right_op, (((1,), (1,)), ((), ())), preferred_element_type=jnp.float32
    )


def rms_scale(values, scale_gain):
    return (
        values
        * lax.rsqrt(jnp.mean(values * values, axis=-1, keepdims=True) + EPS_NORM)
        * scale_gain
    )


def unit_rows(values):
    return values * lax.rsqrt(jnp.sum(values * values, axis=-1, keepdims=True) + EPS_UNIT)


def head_norm(mixer_out, gate_head, norm_head):
    scaled = (
        mixer_out
        * lax.rsqrt(jnp.mean(mixer_out * mixer_out, axis=-1, keepdims=True) + EPS_HEAD)
        * norm_head
    )
    return scaled * jax.nn.silu(gate_head)


def glu_hidden(gate_half, up_half):
    return jax.nn.silu(gate_half) * up_half


def front_piece(extended, small_pre, conv_w, a_log, dt_bias, valid_taps):
    batch_rows, ext_len, channels = extended.shape
    tap_count = conv_w.shape[0]
    span_len = ext_len - tap_count + 1
    conv_out = jnp.zeros((batch_rows, span_len, channels), jnp.float32)
    for tap_pos in range(tap_count):
        conv_out = (
            conv_out
            + conv_w[tap_pos]
            * extended[:, tap_pos : tap_pos + span_len]
            * valid_taps[tap_pos][..., None]
        )
    active = jax.nn.silu(conv_out)
    query_rows = unit_rows(active[..., :KW].reshape(batch_rows, span_len, H, DK)) * DK ** (-0.5)
    key_rows = unit_rows(active[..., KW : 2 * KW].reshape(batch_rows, span_len, H, DK))
    value_rows = active[..., 2 * KW :].reshape(batch_rows, span_len, H, DV)
    beta_gate = jax.nn.sigmoid(small_pre[..., :H])
    log_decay = -jnp.exp(a_log) * jax.nn.softplus(small_pre[..., H:] + dt_bias)
    return (query_rows, key_rows, value_rows, beta_gate, log_decay)


def group_view(array):
    batch_rows, span_len, head_count = array.shape[:3]
    shaped = array.reshape((batch_rows, span_len // CH, CH, head_count) + array.shape[3:])
    return jnp.moveaxis(shaped, 3, 2)


def group_pieces(query_rows, key_rows, value_rows, beta_gate, log_decay, segment):
    query_blk = group_view(query_rows)
    key_blk = group_view(key_rows)
    value_blk = group_view(value_rows)
    rate_blk = group_view(beta_gate)
    cumulated = jnp.cumsum(group_view(log_decay), axis=-1)
    seg_blk = segment[:, :, None, :]
    order_pos = jnp.arange(CH)
    same_seg = seg_blk[..., :, None] == seg_blk[..., None, :]
    causal = ((order_pos[:, None] >= order_pos[None, :]) & same_seg).astype(jnp.float32)
    strict = ((order_pos[:, None] > order_pos[None, :]) & same_seg).astype(jnp.float32)
    spread = cumulated[..., :, None] - cumulated[..., None, :]
    ratios = jnp.exp(spread * causal) * causal
    start_fade = jnp.exp(cumulated) * (seg_blk == 0).astype(jnp.float32)
    key_key = jnp.einsum("bnhtk,bnhsk->bnhts", key_blk, key_blk, precision=highest)
    query_key = jnp.einsum("bnhtk,bnhsk->bnhts", query_blk, key_blk, precision=highest)
    system = jnp.eye(CH, dtype=jnp.float32) + rate_blk[..., :, None] * ratios * strict * key_key
    right_side = jnp.concatenate(
        [rate_blk[..., None] * value_blk, (rate_blk * start_fade)[..., None] * key_blk], axis=-1
    )
    solved = jax.scipy.linalg.solve_triangular(system, right_side, lower=True)
    base_values = solved[..., :DV]
    write_keys = solved[..., DV:]
    readings = ratios * query_key
    query_eff = start_fade[..., None] * query_blk - jnp.einsum(
        "bnhts,bnhsk->bnhtk", readings, write_keys, precision=highest
    )
    local_out = jnp.einsum("bnhts,bnhsv->bnhtv", readings, base_values, precision=highest)
    last_seg = (seg_blk == seg_blk[..., -1:]).astype(jnp.float32)
    end_fade = jnp.exp(cumulated[..., -1:] - cumulated) * last_seg
    faded_keys = end_fade[..., None] * key_blk
    trans_blk = start_fade[..., -1][..., None, None] * jnp.eye(DK, dtype=jnp.float32) - jnp.einsum(
        "bnhsk,bnhsj->bnhkj", faded_keys, write_keys, precision=highest
    )
    part_blk = jnp.einsum("bnhsk,bnhsv->bnhkv", faded_keys, base_values, precision=highest)
    return (query_eff, local_out, trans_blk, part_blk)


def span_summary(trans_blk, part_blk):
    total_trans = trans_blk[:, 0]
    total_part = part_blk[:, 0]
    return (total_trans, total_part)


def read_states(query_eff, local_out, trans_blk, part_blk, state):
    outputs = [
        jnp.einsum("bhtk,bhkv->bhtv", query_eff[:, 0], state, precision=highest) + local_out[:, 0]
    ]
    stacked = jnp.stack(outputs, 1)
    batch_rows, block_n, head_count, block_len, value_size = stacked.shape
    return jnp.moveaxis(stacked, 2, 3).reshape(
        batch_rows, block_n * block_len, head_count, value_size
    )


def join_pairs(earlier, later):
    return (matmul_high(later[0], earlier[0]), matmul_high(later[0], earlier[1]) + later[1])


def mixer_weights(w_proj, w_small, w_out):
    return (
        lax.all_gather(w_proj, ("seq", "batch"), axis=0, tiled=True),
        lax.all_gather(w_small, ("seq", "batch"), axis=0, tiled=True),
        lax.all_gather(w_out, ("seq", "batch"), axis=0, tiled=True),
    )


def shards(
    tokens,
    grad_out,
    resets,
    w_proj,
    w_small,
    w_out,
    w_gu,
    w_down,
    norm_in,
    norm_ff,
    norm_head,
    conv_w,
    a_log,
    dt_bias,
):
    batch_rows = tokens.shape[0]
    span_len = tokens.shape[1]
    tok_rows = batch_rows * span_len
    halo_len = conv_w.shape[0] - 1
    positions = lax.axis_index("seq") * span_len + jnp.arange(span_len, dtype=jnp.int32)
    starts = resets[:, None]
    seg_start = jnp.where(positions[None, :] >= starts, starts, 0)
    valid_taps = tuple(
        (
            (positions[None, :] - halo_len + tap_pos >= seg_start).astype(jnp.float32)
            for tap_pos in range(halo_len + 1)
        )
    )
    restart = (positions[None, :] == starts).astype(jnp.int32)
    segment = jnp.cumsum(restart.reshape(batch_rows, span_len // CH, CH), axis=-1)
    identity_pair = (
        jnp.broadcast_to(jnp.eye(DK, dtype=jnp.float32), (batch_rows, H, DK, DK)),
        jnp.zeros((batch_rows, H, DK, DV), jnp.float32),
    )
    flat_in = tokens.reshape(tok_rows, D).astype(jnp.float32)
    full_proj, full_small, full_out = mixer_weights(w_proj, w_small, w_out)
    normed_in, pull_norm_in = jax.vjp(rms_scale, flat_in, norm_in)
    h_in = normed_in.astype(jnp.bfloat16)
    projected = jnp.dot(h_in, full_proj, preferred_element_type=jnp.float32)
    conv_in = projected[:, :CW].astype(jnp.bfloat16).reshape(batch_rows, span_len, CW)
    gate_head = projected[:, CW:].reshape(batch_rows, span_len, H, DV)
    small_pre = jnp.dot(h_in, full_small, preferred_element_type=jnp.float32).reshape(
        batch_rows, span_len, 2 * H
    )
    before = passed_along(conv_in[:, span_len - halo_len :], "seq", 1)
    extended = jnp.concatenate([before, conv_in], axis=1).astype(jnp.float32)
    fronts, pull_front = jax.vjp(
        partial(front_piece, valid_taps=valid_taps), extended, small_pre, conv_w, a_log, dt_bias
    )
    pieces, pull_pieces = jax.vjp(partial(group_pieces, segment=segment), *fronts)
    summary, pull_summary = jax.vjp(span_summary, pieces[2], pieces[3])
    incoming = entering(summary, "seq", join_pairs, identity_pair, False)
    mixer_out, pull_read = jax.vjp(
        read_states, pieces[0], pieces[1], pieces[2], pieces[3], incoming[1]
    )
    heads_out, pull_head = jax.vjp(head_norm, mixer_out, gate_head, norm_head)
    z_rows = heads_out.reshape(tok_rows, VW).astype(jnp.bfloat16)
    residual = flat_in + jnp.dot(z_rows, full_out, preferred_element_type=jnp.float32)
    normed_ff, pull_norm_ff = jax.vjp(rms_scale, residual, norm_ff)
    h_ff = normed_ff.astype(jnp.bfloat16)
    kept_gu, kept_down = (
        lax.all_gather(w_gu, ("seq", "batch"), axis=0, tiled=True),
        lax.all_gather(w_down, ("seq", "batch"), axis=0, tiled=True),
    )
    gate_up = jnp.dot(h_ff, kept_gu, preferred_element_type=jnp.float32)
    hidden_full, pull_glu = jax.vjp(glu_hidden, gate_up[:, :FF], gate_up[:, FF:])
    hidden = hidden_full.astype(jnp.bfloat16)
    block_out = residual + jnp.dot(hidden, kept_down, preferred_element_type=jnp.float32)
    d_out = grad_out.reshape(tok_rows, D)
    back_gu, back_down = (kept_gu, kept_down)
    d_hidden = contract_cols(d_out, back_down)
    d_gate, d_up = pull_glu(d_hidden)
    d_gate_up = jnp.concatenate([d_gate, d_up], axis=1).astype(jnp.bfloat16)
    ffn_grads = lax.psum_scatter(
        jnp.concatenate([contract_rows(h_ff, d_gate_up), contract_rows(d_out, hidden)], axis=1),
        ("seq", "batch"),
        scatter_dimension=0,
        tiled=True,
    )
    d_h_ff = contract_cols(d_gate_up, back_gu)
    d_resid_norm, g_norm_ff = pull_norm_ff(d_h_ff)
    d_residual = d_out.astype(jnp.float32) + d_resid_norm
    d_branch = d_residual.astype(jnp.bfloat16)
    full_proj, full_small, full_out = mixer_weights(w_proj, w_small, w_out)
    d_heads = contract_cols(d_branch, full_out).reshape(batch_rows, span_len, H, DV)
    d_mixer, d_gate_head, g_norm_head = pull_head(d_heads)
    d_query_eff, d_local_out, d_trans, d_part, d_start = pull_read(d_mixer)
    reverse_in = (jnp.swapaxes(summary[0], -1, -2), d_start)
    state_grad = entering(reverse_in, "seq", join_pairs, identity_pair, True)[1]
    d_sum_trans = matmul_high(state_grad, jnp.swapaxes(incoming[1], -1, -2))
    d_trans_more, d_part_more = pull_summary((d_sum_trans, state_grad))
    d_fronts = pull_pieces((d_query_eff, d_local_out, d_trans + d_trans_more, d_part + d_part_more))
    d_extended, d_small_pre, g_conv, g_alog, g_dt = pull_front(d_fronts)
    spill = passed_along(d_extended[:, :halo_len].astype(jnp.bfloat16), "seq", -1).astype(
        jnp.float32
    )
    d_conv_in = jnp.concatenate(
        [d_extended[:, halo_len:span_len], d_extended[:, span_len:] + spill], axis=1
    )
    d_projected = jnp.concatenate(
        [d_conv_in.reshape(tok_rows, CW), d_gate_head.reshape(tok_rows, VW)], axis=1
    ).astype(jnp.bfloat16)
    d_small_rows = d_small_pre.reshape(tok_rows, 2 * H)
    h_in_full = h_in.astype(jnp.float32)
    small_term = lax.dot_general(
        h_in_full, d_small_rows, (((0,), (0,)), ((), ())), precision=highest
    )
    mixer_grads = lax.psum_scatter(
        jnp.concatenate(
            [contract_rows(h_in, d_projected), small_term, contract_rows(d_branch, z_rows)], axis=1
        ),
        ("seq", "batch"),
        scatter_dimension=0,
        tiled=True,
    )
    d_h_in = contract_cols(d_projected, full_proj) + lax.dot_general(
        d_small_rows, full_small.astype(jnp.float32), (((1,), (1,)), ((), ())), precision=highest
    )
    d_flat, g_norm_in = pull_norm_in(d_h_in)
    d_tokens = (d_residual + d_flat).astype(jnp.bfloat16).reshape(batch_rows, span_len, D)
    small_grads = lax.psum(
        (g_norm_in, g_norm_ff, g_norm_head, g_conv, g_alog, g_dt), ("seq", "batch")
    )
    g_proj = mixer_grads[:, : CW + VW]
    g_small = mixer_grads[:, CW + VW : CW + VW + 2 * H]
    g_out = jnp.transpose(mixer_grads[:, CW + VW + 2 * H :])
    g_gu = ffn_grads[:, : 2 * FF]
    g_down = jnp.transpose(ffn_grads[:, 2 * FF :])
    return (
        block_out.astype(jnp.bfloat16).reshape(batch_rows, span_len, D),
        d_tokens,
        g_proj,
        g_small,
        g_out,
        g_gu,
        g_down,
        small_grads[0],
        small_grads[1],
        small_grads[2],
        small_grads[3],
        small_grads[4],
        small_grads[5],
    )


def solution(mesh):
    in_specs = (
        P("batch", "seq", None),
        P("batch", "seq", None),
        P("batch"),
        P(("seq", "batch"), None),
        P(("seq", "batch"), None),
        P(("seq", "batch"), None),
        P(("seq", "batch"), None),
        P(("seq", "batch"), None),
        P(),
        P(),
        P(),
        P(),
        P(),
        P(),
    )
    out_specs = (
        P("batch", "seq", None),
        P("batch", "seq", None),
        P(("seq", "batch"), None),
        P(("seq", "batch"), None),
        P(None, ("seq", "batch")),
        P(("seq", "batch"), None),
        P(None, ("seq", "batch")),
        P(),
        P(),
        P(),
        P(),
        P(),
        P(),
    )
    return jax.shard_map(shards, mesh=mesh, in_specs=in_specs, out_specs=out_specs, check_vma=False)
```

profile of v0, /device:TPU:0, one launch (start us, length us, event | category | flops | bytes accessed | tf_op | source)
XLA Modules:
  0.0 4646.2 jit_solution(3494414573478290518)
XLA Ops:
  8.0 75.1 %all-gather.4 = bf16[32,64,32]{1,2,0:T(8,128)(2,1)S(1)} all-gather(bf16[1,64,32]{1,2,0:T(8,128)(2,1)} %bitcast.559), channel_id=1, replica_groups=mesh['seq'=8,'batch'=4] {'seq','batch'}, dimensions={0}, use_global_device_ids=true | all-gather | bytes 135168 | tf_op jit(solution)/shard_map/all_gather | solution.py:185
  88.6 203.9 %all-gather.14.cloned.1.call-done = bf16[2048,12288]{1,0:T(8,128)(2,1)} async-done(((bf16[64,12288]{1,0:T(8,128)(2,1)}), bf16[2048,12288]{1,0:T(8,128)(2,1)}) %all-gather.14.cloned.1.call-update) | async-done | bytes 50331664 | tf_op jit(solution)/shard_map/all_gather | solution.py:184
  292.5 17.9 fusion.210
  334.4 158.1 %custom-call.10 = f32[2,16,1,64,64]{3,4,2,1,0:T(8,128)S(1)} custom-call(f32[2,16,1,64,64]{4,3,2,1,0:T(8,128)} %select_bitcast_fusion), custom_call_target="InvertDiagBlocksLowerTriangular" | custom-call | tf_op jit(solution)/shard_map/jvp(jit(_solve_triangular))/vmap(vmap())/triangular_solve | solution.py:143
  529.7 38.3 all-gather.22.cloned.1.call-done
  568.0 92.4 %all-gather.24.cloned.1.call-done = bf16[16,16,128,256]{3,2,1,0:T(8,128)(2,1)} async-done(((bf16[2,16,128,256]{3,2,1,0:T(8,128)(2,1)}), bf16[16,16,128,256]{3,2,1,0:T(8,128)(2,1)}) %all-gather.24.cloned.1.call-update) | async-done | bytes 16777232 | tf_op jit(solution)/shard_map/all_gather | solution.py:34
  660.4 111.2 %while.30 = (s32[]{:T(128)}, f32[2,16,128,256]{3,2,1,0:T(8,128)}, s32[]{:T(128)}, bf16[8,2,16,128,128]{4,3,2,1,0:T(8,128)(2,1)}, bf16[8,2,16,128,256]{4,3,2,1,0:T(8,128)(2,1)}, /*index=5*/s32[]{:T(128)}, s32[]{:T(128)}) while((s32[]{:T(128)}, f32[2,16,128,256]{3,2,1,0:T(8,128)}, s32[]{:T(128)}, ...), condition=%wide.region_6.7_spmd.clone, body=%wide.region_5.6_spmd.clone.sunk | while | flops 1615855616 | bytes 24119912 | solution.py:52
  691.6 9.7 fusion.254
  797.6 236.7 %all-gather.18.cloned.1.call-done = bf16[2048,11264]{1,0:T(8,128)(2,1)} async-done(((bf16[64,11264]{1,0:T(8,128)(2,1)}), bf16[2048,11264]{1,0:T(8,128)(2,1)}) %all-gather.18.cloned.1.call-update) | async-done | bytes 46137360 | tf_op jit(solution)/shard_map/all_gather | solution.py:252
  1034.3 20.9 fusion.201
  1055.2 124.6 %all-gather.20.cloned.1.call-done = bf16[5632,2048]{1,0:T(8,128)(2,1)} async-done(((bf16[176,2048]{1,0:T(8,128)(2,1)}), bf16[5632,2048]{1,0:T(8,128)(2,1)}) %all-gather.20.cloned.1.call-update) | async-done | bytes 23068688 | tf_op jit(solution)/shard_map/all_gather | solution.py:253
  1179.8 15.6 fusion.34
  1195.4 25.1 multiply_reduce_fusion.5
  1222.2 13.2 fusion.157
  1256.5 19.9 convolution_bitcast_fusion
  1276.4 36.6 fusion.58
  1313.0 90.1 %pad_maximum_fusion = f32[2048,16896]{1,0:T(8,128)} fusion(f32[2048,5632]{1,0:T(8,128)} %convolution_bitcast_fusion, f32[2048,11264]{1,0:T(8,128)} %fusion.58), kind=kLoop, calls=%fused_computation.20 | loop fusion | flops 34603008 | bytes 276824064 | tf_op jit(solution)/shard_map/concatenate | solution.py:265
  1421.9 13.7 fusion.155
  1435.6 113.1 %while.31 = (s32[]{:T(128)}, f32[2,16,128,256]{3,2,1,0:T(8,128)}, s32[]{:T(128)}, bf16[8,2,16,128,128]{4,3,2,1,0:T(8,128)(2,1)}, bf16[8,2,16,128,256]{4,3,2,1,0:...) while((s32[]{:T(128)}, f32[2,16,128,256]{3,2,1,0:T(8,128)}, s32[]{:T(128)}, ...), condition=%wide.region_12.13_spmd.clone, body=%wide.region_11.12_spmd.clone.sunk | while | flops 1615855616 | bytes 24119972 | solution.py:52
  1453.1 10.2 fusion.257
  1467.9 9.4 fusion.257
  1496.1 9.7 fusion.257
  1538.7 9.6 fusion.257
  1625.8 11.6 multiply_reduce_fusion.3
  1657.5 38.9 fusion.49
  1696.4 180.3 %concatenate.29 = f32[2048,16416]{1,0:T(8,128)} concatenate(f32[2048,12288]{1,0:T(8,128)} %fusion.49, f32[2048,32]{1,0:T(8,128)} %convolution_bitcast_fusion.1, f32[2048,4096]{1,0:T(8,128)} %fusion.155), dimensions={1} | concatenate | bytes 268959744 | tf_op jit(solution)/shard_map/concatenate | solution.py:299
  1878.1 12.7 fusion.36
  1891.9 23.9 fusion.50
  1919.2 42.4 all-reduce.18
  1961.6 1373.3 %all-reduce.24.cloned.1.call-done = f32[2048,16896]{1,0:T(8,128)} async-done(((f32[2048,16896]{1,0:T(8,128)}), f32[2048,16896]{1,0:T(8,128)}) %all-reduce.24.cloned.1.call-update) | async-done | bytes 138412048
  3341.5 1168.1 %reduce-scatter.2.cloned.1.call-done = f32[64,16416]{1,0:T(8,128)} async-done(((f32[2048,16416]{1,0:T(8,128)}), f32[64,16416]{1,0:T(8,128)}) %reduce-scatter.2.cloned.1.call-update) | async-done | bytes 4202512 | tf_op jit(solution)/shard_map/reduce_scatter | solution.py:298
  4517.4 120.6 %all-reduce.22.cloned.1.call-done = f32[4,8192]{1,0:T(4,128)} async-done(((f32[4,8192]{1,0:T(4,128)}), f32[4,8192]{1,0:T(4,128)}) %all-reduce.22.cloned.1.call-update) | async-done | bytes 131088 | tf_op jit(solution)/shard_map/psum | solution.py:311
  (507 shorter events, 427.2 us)
Async XLA Ops:
  7.2 285.3 %all-gather.14.cloned.1.call-start = ((), (), s32[]{:S(2)}) async-start(), calls=%async_computation.1 | async-start | bytes 51904512 | tf_op jit(solution)/shard_map/all_gather | solution.py:184
  8.0 560.0 %all-gather.22.cloned.1.call-start = ((), (), s32[]{:S(2)}) async-start(), calls=%async_computation.7 | async-start | bytes 9437184 | tf_op jit(solution)/shard_map/all_gather | solution.py:34
  86.6 246.4 %copy-start.71 = (f32[2,16,64]{2,1,0:T(8,128)}, f32[2,16,64]{2,1,0:T(8,128)S(1)}, u32[]{:S(2)}) copy-start(f32[2,16,64]{2,1,0:T(8,128)S(1)} %get-tuple-element.434) | copy-start | bytes 24580
  87.0 689.3 %copy-start.41 = (f32[2,1,16,64]{3,2,1,0:T(8,128)}, f32[2,1,16,64]{3,2,1,0:T(8,128)S(1)}, u32[]{:S(2)}) copy-start(f32[2,1,16,64]{3,2,1,0:T(8,128)S(1)} %reduce_window_sum.35) | copy-start | bytes 24580
  87.2 245.7 %copy-start.111 = (pred[64,64]{1,0:T(8,128)(4,1)}, pred[64,64]{1,0:T(8,128)(4,1)S(1)}, u32[]{:S(2)}) copy-start(pred[64,64]{1,0:T(8,128)(4,1)S(1)} %get-tuple-element.471) | copy-start | bytes 12292
  87.4 418.0 %copy-start.75 = (f32[128,128]{0,1:T(8,128)}, f32[128,128]{0,1:T(8,128)S(1)}, u32[]{:S(2)}) copy-start(f32[128,128]{0,1:T(8,128)S(1)} %get-tuple-element.472) | copy-start | bytes 196612
  87.6 227.0 %copy-start.125 = (f32[2,64]{1,0:T(2,128)}, f32[2,64]{1,0:T(2,128)S(1)}, u32[]{:S(2)}) copy-start(f32[2,64]{1,0:T(2,128)S(1)} %get-tuple-element.446) | copy-start | bytes 1540
  87.6 227.0 %copy-start.127 = (f32[2,64]{1,0:T(2,128)}, f32[2,64]{1,0:T(2,128)S(1)}, u32[]{:S(2)}) copy-start(f32[2,64]{1,0:T(2,128)S(1)} %get-tuple-element.447) | copy-start | bytes 1540
  87.6 227.0 %copy-start.129 = (f32[2,64]{1,0:T(2,128)}, f32[2,64]{1,0:T(2,128)S(1)}, u32[]{:S(2)}) copy-start(f32[2,64]{1,0:T(2,128)S(1)} %get-tuple-element.448) | copy-start | bytes 1540
  87.6 227.0 %copy-start.131 = (f32[2,64]{1,0:T(2,128)}, f32[2,64]{1,0:T(2,128)S(1)}, u32[]{:S(2)}) copy-start(f32[2,64]{1,0:T(2,128)S(1)} %get-tuple-element.449) | copy-start | bytes 1540
  87.7 238.5 %copy-start.94 = (f32[2,16,64]{2,1,0:T(8,128)}, f32[2,16,64]{2,1,0:T(8,128)S(1)}, u32[]{:S(2)}) copy-start(f32[2,16,64]{2,1,0:T(8,128)S(1)} %get-tuple-element.408) | copy-start | bytes 24580
  87.8 423.8 %copy-start.73 = (f32[2,16,64]{2,1,0:T(8,128)}, f32[2,16,64]{2,1,0:T(8,128)S(1)}, u32[]{:S(2)}) copy-start(f32[2,16,64]{2,1,0:T(8,128)S(1)} %get-tuple-element.438) | copy-start | bytes 24580
  87.8 438.4 %copy-start.91 = (f32[2,16,64]{2,1,0:T(8,128)}, f32[2,16,64]{2,1,0:T(8,128)S(1)}, u32[]{:S(2)}) copy-start(f32[2,16,64]{2,1,0:T(8,128)S(1)} %get-tuple-element.439) | copy-start | bytes 24580
  88.2 244.7 %copy-start.68 = (f32[2,64,64]{2,1,0:T(8,128)}, f32[2,64,64]{2,1,0:T(8,128)S(1)}, u32[]{:S(2)}) copy-start(f32[2,64,64]{2,1,0:T(8,128)S(1)} %get-tuple-element.445) | copy-start | bytes 98308
  88.2 688.1 %copy-start.54 = (f32[2,64,64]{2,1,0:T(8,128)}, f32[2,64,64]{2,1,0:T(8,128)S(1)}, u32[]{:S(2)}) copy-start(f32[2,64,64]{2,1,0:T(8,128)S(1)} %get-tuple-element.444) | copy-start | bytes 98308
  88.5 226.1 %copy-start.79 = (f32[1,8192]{1,0:T(1,128)}, f32[1,8192]{1,0:T(1,128)S(1)}, u32[]{:S(2)}) copy-start(f32[1,8192]{1,0:T(1,128)S(1)} %get-tuple-element.428) | copy-start | bytes 98308
  310.8 3.1 collective-permute-start
  511.2 149.1 %all-gather.24.cloned.1.call-start = ((), (), s32[]{:S(2)}) async-start(), calls=%async_computation.8 | async-start | bytes 18874368 | tf_op jit(solution)/shard_map/all_gather | solution.py:34
  518.8 269.7 %all-gather.16.cloned.1.call-start = ((), (), s32[]{:S(2)}) async-start(), calls=%async_computation.2 | async-start | bytes 17301504 | tf_op jit(solution)/shard_map/all_gather | solution.py:186
  519.4 514.9 %all-gather.18.cloned.1.call-start = ((), (), s32[]{:S(2)}) async-start(), calls=%async_computation.3 | async-start | bytes 47579136 | tf_op jit(solution)/shard_map/all_gather | solution.py:252
  520.0 659.8 %all-gather.20.cloned.1.call-start = ((), (), s32[]{:S(2)}) async-start(), calls=%async_computation.4 | async-start | bytes 23789568 | tf_op jit(solution)/shard_map/all_gather | solution.py:253
  520.6 915.0 %all-gather.26.cloned.1.call-start = ((), (), s32[]{:S(2)}) async-start(), calls=%async_computation.9 | async-start | bytes 9437184 | tf_op jit(solution)/shard_map/all_gather | solution.py:34
  520.7 263.1 %copy-start.93 = (f32[2,2,8,128]{3,1,2,0:T(2,128)}, f32[2,2,8,128]{3,1,2,0:T(2,128)S(1)}, u32[]{:S(2)}) copy-start(f32[2,2,8,128]{3,1,2,0:T(2,128)S(1)} %copy.275) | copy-start | bytes 49156
  526.2 250.1 %copy-start.11 = (f32[2,16,64,64]{3,2,1,0:T(8,128)}, f32[2,16,64,64]{3,2,1,0:T(8,128)S(1)}, u32[]{:S(2)}) copy-start(f32[2,16,64,64]{3,2,1,0:T(8,128)S(1)} %fusion.89) | copy-start | bytes 1572868
  529.6 241.9 %copy-start.46 = (f32[2,16,64,128]{3,2,1,0:T(8,128)}, f32[2,16,64,128]{3,2,1,0:T(8,128)S(1)}, u32[]{:S(2)}) copy-start(f32[2,16,64,128]{3,2,1,0:T(8,128)S(1)} %fusion.76) | copy-start | bytes 3145732
  529.6 905.9 %all-gather.28.cloned.1.call-start = ((), (), s32[]{:S(2)}) async-start(), calls=%async_computation.10 | async-start | bytes 18874368 | tf_op jit(solution)/shard_map/all_gather | solution.py:34
  788.5 245.8 %copy-start.70 = (f32[2048]{0:T(1024)S(1)}, f32[2048]{0:T(1024)}, u32[]{:S(2)}) copy-start(f32[2048]{0:T(1024)} %param.27) | copy-start | bytes 24580
  797.6 478.8 %copy-start.9 = (f32[128,2048]{1,0:T(8,128)}, f32[128,2048]{1,0:T(8,128)S(1)}, u32[]{:S(2)}) copy-start(f32[128,2048]{1,0:T(8,128)S(1)} %get-tuple-element.455) | copy-start | bytes 3145732
  1256.5 2078.5 %all-reduce.24.cloned.1.call-start = ((), (), s32[]{:S(2)}) async-start(), calls=%async_computation.11 | async-start | bytes 276824064
  1403.2 3106.4 %reduce-scatter.2.cloned.1.call-start = ((), (), s32[]{:S(2)}) async-start(), calls=%async_computation.5 | async-start | bytes 139493376 | tf_op jit(solution)/shard_map/reduce_scatter | solution.py:298
  1646.8 9.4 collective-permute-start.1
  1876.8 2761.1 %all-reduce.22.cloned.1.call-start = ((), (), s32[]{:S(2)}) async-start(), calls=%async_computation.6 | async-start | bytes 262144 | tf_op jit(solution)/shard_map/psum | solution.py:311
  (131 other events, 3116.8 us)
Sparse Core Ops, SparseCore 0:
  11.0 281.4 all-gather.13
  511.4 56.5 all-gather.21
  570.5 89.8 all-gather.23
  663.2 114.8 all-gather.15
  780.8 253.4 all-gather.17
  1037.0 142.7 all-gather.19
  1181.7 52.5 all-gather.25
  1256.6 87.3 all-gather.27
  1403.3 1931.6 all-reduce.23
  3341.2 1168.3 reduce-scatter.1
  4515.7 122.1 all-reduce.21
where the time goes:
time: 4660 us; the launch traced here: 4650 us
  waiting for transfers between devices  3360 us (72%)
  matrix products  502 us (11%)
  local copies, waits for them, and re-layouts  330 us (7%)
  other arithmetic  315 us (7%)
  blocking collectives  117 us (3%)
    unnamed x12, waiting for transfers between devices  1380 us
    reduce_scatter x1, waiting for transfers between devices, shards(): lax.psum_scatter(jnp.concatenate([contract_rows(h_in, d_projected), small...  1170 us
    all_gather x1, waiting for transfers between devices, shards(): lax.all_gather(w_gu, ('seq', 'batch'), axis=0, tiled=True)  237 us
    all_gather x1, waiting for transfers between devices, mixer_weights(): lax.all_gather(w_proj, ('seq', 'batch'), axis=0, tiled=True)  204 us
    concatenate x1, local copies, waits for them, and re-layouts, shards(): jnp.concatenate([contract_rows(h_in, d_projected), small_term, contract_r...  180 us
    another operation x2, other arithmetic, group_pieces(): solved = jax.scipy.linalg.solve_triangular(system, right_side, lower=True)  160 us
    dot_general x17, matrix products, matmul_high(): return jnp.matmul(left_op, right_op, precision=highest)  157 us
    all_gather x4, waiting for transfers between devices, entering(): lax.all_gather(part.astype(kind), axis)  131 us
  transfers between devices with their start and end apart: 13, of which 9 were waited for; matrix products, arithmetic and copies ran while one was open for 20% of the time, Pallas kernels for 0%

commit v1 on v0

v1 whole, which is shorter than its diff:
```python
from functools import partial

import jax
import jax.numpy as jnp
from jax import lax
from jax.experimental import pallas as pl
from jax.experimental.pallas import tpu as pltpu
from jax.sharding import PartitionSpec as P

D = 2048
H = 16
DK = 128
DV = 256
FF = 5632
CH = 64
KW = 2048
VW = 4096
CW = 8192
TAPS = 4
LANES = 128

EPS_NORM = 1e-06
EPS_HEAD = 1e-05
EPS_UNIT = 1e-06
f32 = jnp.float32
bf16 = jnp.bfloat16
VMEM_BYTES = 32 * 1024 * 1024
KERNEL_COST = pl.CostEstimate(flops=60_000_000_000, bytes_accessed=40_000_000, transcendentals=0)


def dot_in(left, right, contract, precision):
    return lax.dot_general(
        left,
        right,
        (((contract[0],), (contract[1],)), ((), ())),
        precision=precision,
        preferred_element_type=f32,
    )


def fine(left, right, contract=(1, 0)):
    return dot_in(left, right, contract, lax.Precision.HIGHEST)


def coarse(left, right, contract=(1, 0)):
    return dot_in(left, right, contract, lax.Precision.HIGHEST)


def position_masks(reset, chunk):
    rows = lax.broadcasted_iota(jnp.int32, (CH, CH), 0)
    cols = lax.broadcasted_iota(jnp.int32, (CH, CH), 1)
    time = lax.broadcasted_iota(jnp.int32, (CH, 1), 0)
    offset = reset - chunk * CH
    cut = jnp.where(offset < 0, CH, offset)
    apart = (rows >= cut) & (cols < cut)
    causal = jnp.where((rows >= cols) & ~apart, 1.0, 0.0)
    strict = jnp.where((rows > cols) & ~apart, 1.0, 0.0)
    in_first = jnp.where(time < cut, 1.0, 0.0)
    last_first = jnp.where(CH - 1 < cut, 1.0, 0.0)
    in_last = jnp.where((time >= cut) | (cut > CH - 1), 1.0, 0.0)
    begin = jnp.where(time >= offset, offset, -chunk * CH)
    taps = [jnp.where(time - (TAPS - 1) + j >= begin, 1.0, 0.0) for j in range(TAPS)]
    return causal, strict, in_first, last_first, in_last, taps


def gates(small, aux):
    beta = jax.nn.sigmoid(small)
    shifted = small + aux[1:2]
    soft = jnp.maximum(shifted, 0.0) + jnp.log1p(jnp.exp(-jnp.abs(shifted)))
    return beta, -aux[0:1] * soft, shifted


def running(values, reverse=False):
    rows = lax.broadcasted_iota(jnp.int32, (CH, CH), 0)
    cols = lax.broadcasted_iota(jnp.int32, (CH, CH), 1)
    keep = (cols >= rows) if reverse else (cols <= rows)
    return fine(jnp.where(keep, 1.0, 0.0), values)


def as_rows(total):
    pick_row = lax.broadcasted_iota(jnp.int32, (LANES, LANES), 0)
    pick_col = lax.broadcasted_iota(jnp.int32, (LANES, LANES), 1)
    return fine(jnp.where(pick_row == pick_col, 1.0, 0.0), total, (1, 1))


def inverse_unit_lower(strict_part):
    rows = lax.broadcasted_iota(jnp.int32, (CH, CH), 0)
    cols = lax.broadcasted_iota(jnp.int32, (CH, CH), 1)
    eye = jnp.where(rows == cols, 1.0, 0.0)
    diag = jnp.where(rows // 16 == cols // 16, strict_part, 0.0)
    inv = eye - diag
    power = diag
    for _ in range(3):
        power = fine(power, power)
        inv = inv + fine(inv, power)
    for size in (16, 32):
        off = jnp.where((rows // size != cols // size) & (rows // (2 * size) == cols // (2 * size)), strict_part, 0.0)
        inv = inv - fine(fine(inv, off), inv)
    return inv


def conv_taps(ext_ref, row, conv_w, taps):
    out = None
    for j in range(TAPS):
        part = conv_w[j : j + 1] * (ext_ref[row, 8 - (TAPS - 1) + j : 8 - (TAPS - 1) + j + CH, :] * taps[j])
        out = part if out is None else out + part
    return out


def unit(values):
    return lax.rsqrt(jnp.sum(values * values, axis=-1, keepdims=True) + EPS_UNIT)


def head_parts(active, head, heads):
    q = active[:, head * DK : (head + 1) * DK]
    k = active[:, heads * DK + head * DK : heads * DK + (head + 1) * DK]
    v = active[:, 2 * heads * DK + head * DV : 2 * heads * DK + (head + 1) * DV]
    return q, k, v


def decay_terms(total, total_rows, head, heads, masks):
    causal, strict, in_first, last_first, in_last, _ = masks
    lane = heads + head
    col = total[:, lane : lane + 1]
    row = total_rows[lane : lane + 1, :]
    ratios = jnp.exp(jnp.where(causal > 0, col - row, 0.0)) * causal
    last = col[CH - 1 : CH, :]
    start_fade = jnp.exp(col) * in_first
    start_last = jnp.exp(last) * last_first
    end_fade = jnp.exp(jnp.where(in_last > 0, last - col, 0.0)) * in_last
    return ratios, start_fade, start_last, end_fade


def forward_kernel(
    heads, pos_ref, reset_ref, proj, conv_w_ref, aux_ref, outs, state_out, inv_out, delta_out, ext, state
):
    chunk = pl.program_id(0)
    width = heads * (2 * DK + DV)

    @pl.when(chunk == 0)
    def _():
        ext[...] = jnp.zeros_like(ext)
        state[...] = jnp.zeros_like(state)

    state_out[0] = state[...]
    conv_w = conv_w_ref[...]
    aux = aux_ref[...]
    for row in range(proj.shape[0]):
        masks = position_masks(reset_ref[row], chunk)
        ext[row, 0:8, :] = ext[row, CH : CH + 8, :]
        ext[row, 8:, :] = proj[row, 0, :, :width].astype(bf16).astype(f32)
        conv = conv_taps(ext, row, conv_w, masks[5])
        active = conv * jax.nn.sigmoid(conv)
        beta_all, decay, _ = gates(proj[row, 0, :, width : width + LANES], aux)
        total = running(decay)
        total_rows = as_rows(total)
        for head in range(heads):
            at = row * heads + head
            q, k, v = head_parts(active, head, heads)
            q = q * (unit(q) * DK**-0.5)
            k = k * unit(k)
            beta = beta_all[:, head : head + 1]
            ratios, start_fade, start_last, end_fade = decay_terms(total, total_rows, head, heads, masks)
            both = jnp.concatenate([q, k], axis=0)
            pair = fine(both, k, (1, 1))
            inv = inverse_unit_lower(beta * (ratios * masks[1] * pair[CH:]))
            old = state[at]
            read = coarse(both, old)
            delta = coarse(inv, beta * (v - start_fade * read[CH:]))
            out = start_fade * read[:CH] + coarse(ratios * pair[:CH], delta)
            state[at] = start_last * old + coarse(end_fade * k, delta, (0, 0))
            outs[row, 0, :, head * DV : (head + 1) * DV] = out
            inv_out[0, at] = inv
            delta_out[0, at] = delta


def backward_kernel(
    heads,
    chunks,
    pos_ref,
    reset_ref,
    proj,
    tail,
    d_out,
    conv_w_ref,
    aux_ref,
    state_ref,
    inv_ref,
    delta_ref,
    d_proj,
    g_conv,
    g_decay,
    ext,
    dext,
    d_state,
):
    step = pl.program_id(0)
    chunk = chunks - 1 - step
    width = heads * (2 * DK + DV)

    @pl.when(step == 0)
    def _():
        dext[...] = jnp.zeros_like(dext)
        d_state[...] = jnp.zeros_like(d_state)
        g_conv[...] = jnp.zeros_like(g_conv)
        g_decay[...] = jnp.zeros_like(g_decay)

    conv_w = conv_w_ref[...]
    aux = aux_ref[...]
    lane_ids = lax.broadcasted_iota(jnp.int32, (CH, LANES), 1)
    ones = jnp.ones((CH, LANES), f32)
    for row in range(proj.shape[0]):
        masks = position_masks(reset_ref[row], chunk)
        taps = masks[5]
        ext[row, 0:8, :] = tail[row, 0].astype(bf16).astype(f32)
        ext[row, 8:, :] = proj[row, 0, :, :width].astype(bf16).astype(f32)
        conv = conv_taps(ext, row, conv_w, taps)
        sig = jax.nn.sigmoid(conv)
        active = conv * sig
        small = proj[row, 0, :, width : width + LANES]
        beta_all, decay, shifted = gates(small, aux)
        total = running(decay)
        total_rows = as_rows(total)
        d_beta_all = jnp.zeros((CH, LANES), f32)
        d_total = jnp.zeros((CH, LANES), f32)
        d_active = []
        for head in range(heads):
            at = row * heads + head
            a_q, a_k, v = head_parts(active, head, heads)
            q_scale = unit(a_q)
            k_scale = unit(a_k)
            q = a_q * (q_scale * DK**-0.5)
            k = a_k * k_scale
            beta = beta_all[:, head : head + 1]
            ratios, start_fade, start_last, end_fade = decay_terms(total, total_rows, head, heads, masks)
            both = jnp.concatenate([q, k], axis=0)
            pair = fine(both, k, (1, 1))
            key_key, query_key = pair[CH:], pair[:CH]
            old = state_ref[0, at]
            inv = inv_ref[0, at]
            delta = delta_ref[0, at]
            do = d_out[row, 0, :, head * DV : (head + 1) * DV]
            ds = d_state[at]
            read = coarse(both, old)
            readings = ratios * query_key
            faded = end_fade * k
            d_delta = coarse(readings, do, (0, 0)) + coarse(faded, ds)
            d_right = coarse(inv, d_delta, (0, 0))
            d_pair = coarse(jnp.concatenate([do, d_right], axis=0), delta, (1, 1))
            d_faded = coarse(delta, ds, (1, 1))
            d_read = jnp.concatenate([start_fade * do, -(beta * start_fade) * d_right], axis=0)
            d_both = coarse(d_read, old, (1, 1))
            d_state[at] = start_last * ds + coarse(both, d_read, (0, 0))
            d_v = beta * d_right
            d_read_pair = d_pair[:CH] * ratios
            d_sys = -d_pair[CH:] * (ratios * masks[1])
            d_key_key = beta * d_sys
            moved = d_key_key * key_key + d_read_pair * query_key
            recall = read[CH:]
            d_beta = jnp.sum(d_right * (v - start_fade * recall), axis=-1, keepdims=True) + jnp.sum(
                d_sys * key_key, axis=-1, keepdims=True
            )
            d_start = jnp.sum(do * read[:CH], axis=-1, keepdims=True) - beta * jnp.sum(
                d_right * recall, axis=-1, keepdims=True
            )
            d_end = jnp.sum(d_faded * k, axis=-1, keepdims=True) * end_fade
            d_last = jnp.sum(d_end, axis=0, keepdims=True) + start_last * jnp.sum(
                jnp.sum(ds * old, axis=-1, keepdims=True), axis=0, keepdims=True
            )
            last_row = lax.broadcasted_iota(jnp.int32, (CH, 1), 0) == CH - 1
            d_col = (
                jnp.sum(moved, axis=-1, keepdims=True)
                - fine(moved, ones, (0, 0))[:, 0:1]
                + d_start * start_fade
                - d_end
                + jnp.where(last_row, d_last, 0.0)
            )
            d_q = d_both[:CH] + coarse(d_read_pair, k)
            d_k = (
                d_both[CH:]
                + coarse(d_read_pair, q, (0, 0))
                + coarse(d_key_key, k)
                + coarse(d_key_key, k, (0, 0))
                + end_fade * d_faded
            )
            d_aq = (q_scale * DK**-0.5) * (d_q - a_q * (q_scale * q_scale * jnp.sum(a_q * d_q, axis=-1, keepdims=True)))
            d_ak = k_scale * (d_k - a_k * (k_scale * k_scale * jnp.sum(a_k * d_k, axis=-1, keepdims=True)))
            d_active.append((d_aq, d_ak, d_v))
            d_beta_all = jnp.where(lane_ids == head, d_beta, d_beta_all)
            d_total = jnp.where(lane_ids == heads + head, d_col, d_total)
        d_decay = running(d_total, reverse=True)
        d_shift = d_decay * (-aux[0:1]) * jax.nn.sigmoid(shifted)
        d_small = d_beta_all * beta_all * (1.0 - beta_all) + d_shift
        g_decay[0:1, :] += jnp.sum(d_decay * decay, axis=0, keepdims=True)
        g_decay[1:2, :] += jnp.sum(d_shift, axis=0, keepdims=True)
        d_act = jnp.concatenate([d_active[h][i] for i in range(3) for h in range(heads)], axis=1)
        d_conv = d_act * (sig * (1.0 + conv * (1.0 - sig)))
        d_in = None
        for j in range(TAPS):
            masked = d_conv * taps[j]
            g_conv[j : j + 1, :] += jnp.sum(
                masked * ext[row, 8 - (TAPS - 1) + j : 8 - (TAPS - 1) + j + CH, :], axis=0, keepdims=True
            )
            dext[row, j, 0:CH, :] = masked
            shift = TAPS - 1 - j
            part = conv_w[j : j + 1] * dext[row, j, shift : shift + CH, :]
            d_in = part if d_in is None else d_in + part
            dext[row, j, CH : CH + 8, :] = masked[0:8]
        d_proj[row, 0, :, :width] = d_in.astype(bf16)
        d_proj[row, 0, :, width : width + LANES] = d_small.astype(bf16)


def params():
    return pltpu.CompilerParams(dimension_semantics=("arbitrary",), vmem_limit_bytes=VMEM_BYTES)


def whole(array):
    return pl.BlockSpec(array.shape, lambda c, pos, rst: (0,) * array.ndim)


def mixer_forward(proj, pos, resets, conv_w, aux):
    rows_n, chunks, _, total = proj.shape
    width = total - LANES
    heads = width // (2 * DK + DV)
    units = rows_n * heads
    spec = lambda w: pl.BlockSpec((rows_n, 1, CH, w), lambda c, pos, rst: (0, pos[c], 0, 0))
    kept = lambda *s: pl.BlockSpec((1, units) + s, lambda c, pos, rst: (c, 0, 0, 0))
    return pl.pallas_call(
        partial(forward_kernel, heads),
        grid_spec=pltpu.PrefetchScalarGridSpec(
            num_scalar_prefetch=2,
            grid=(chunks,),
            in_specs=[spec(total), whole(conv_w), whole(aux)],
            out_specs=[spec(heads * DV), kept(DK, DV), kept(CH, CH), kept(CH, DV)],
            scratch_shapes=[pltpu.VMEM((rows_n, CH + 8, width), f32), pltpu.VMEM((units, DK, DV), f32)],
        ),
        out_shape=[
            jax.ShapeDtypeStruct((rows_n, chunks, CH, heads * DV), f32),
            jax.ShapeDtypeStruct((chunks, units, DK, DV), f32),
            jax.ShapeDtypeStruct((chunks, units, CH, CH), f32),
            jax.ShapeDtypeStruct((chunks, units, CH, DV), f32),
        ],
        cost_estimate=KERNEL_COST,
        compiler_params=params(),
        name="delta_forward",
    )(pos, resets, proj, conv_w, aux)


def mixer_backward(proj, d_out, pos, resets, conv_w, aux, states, invs, deltas):
    rows_n, chunks, _, total = proj.shape
    width = total - LANES
    heads = width // (2 * DK + DV)
    units = rows_n * heads
    back = lambda c: chunks - 1 - c
    spec = lambda w: pl.BlockSpec((rows_n, 1, CH, w), lambda c, pos, rst: (0, pos[back(c)], 0, 0))
    tail = pl.BlockSpec(
        (rows_n, 1, 8, width), lambda c, pos, rst: (0, pos[jnp.maximum(back(c) - 1, 0)], CH // 8 - 1, 0)
    )
    kept = lambda *s: pl.BlockSpec((1, units) + s, lambda c, pos, rst: (back(c), 0, 0, 0))
    return pl.pallas_call(
        partial(backward_kernel, heads, chunks),
        grid_spec=pltpu.PrefetchScalarGridSpec(
            num_scalar_prefetch=2,
            grid=(chunks,),
            in_specs=[spec(total), tail, spec(heads * DV), whole(conv_w), whole(aux)]
            + [kept(DK, DV), kept(CH, CH), kept(CH, DV)],
            out_specs=[
                spec(total),
                pl.BlockSpec((8, width), lambda c, pos, rst: (0, 0)),
                pl.BlockSpec((8, LANES), lambda c, pos, rst: (0, 0)),
            ],
            scratch_shapes=[
                pltpu.VMEM((rows_n, CH + 8, width), f32),
                pltpu.VMEM((rows_n, TAPS, CH + 8, width), f32),
                pltpu.VMEM((units, DK, DV), f32),
            ],
        ),
        out_shape=[
            jax.ShapeDtypeStruct((rows_n, chunks, CH, total), bf16),
            jax.ShapeDtypeStruct((8, width), f32),
            jax.ShapeDtypeStruct((8, LANES), f32),
        ],
        cost_estimate=KERNEL_COST,
        compiler_params=params(),
        name="delta_backward",
    )(pos, resets, proj, proj, d_out, conv_w, aux, states, invs, deltas)


def swap(value, axis, bit):
    return lax.ppermute(value, axis, [(i, i ^ bit) for i in range(lax.axis_size(axis))])


def routes(axis):
    bits = [1 << i for i in range(lax.axis_size(axis).bit_length() - 1)]
    return [bits[1:] + bits[:1], bits[:0:-1] + bits[:1]]


def slot_of(relative, chunks):
    return (relative >> 1) | ((relative & 1) * (chunks // 2))


def gather_rows(rows, axis):
    size = lax.axis_size(axis)
    orders = routes(axis)
    laid = []
    for row in range(rows.shape[0]):
        order = orders[row % 2]
        held = rows[row][None]
        names = [0]
        for bit in order[:-1]:
            held = jnp.concatenate([held, swap(held, axis, bit)], axis=0)
            names = names + [n ^ bit for n in names]
        other = swap(held, axis, order[-1])
        place = {name: i for i, name in enumerate(names)}
        for part in (held, other):
            if names == sorted(names):
                laid.append(part)
            else:
                laid.extend(part[place[n]][None] for n in sorted(names))
    whole_rows = jnp.concatenate(laid, axis=0)
    return whole_rows.reshape((rows.shape[0], size) + rows.shape[1:])


def scatter_rows(parts, axis):
    size = lax.axis_size(axis)
    orders = routes(axis)
    out = []
    for row in range(parts.shape[0]):
        order = orders[row % 2][::-1]
        half = size // 2
        held = parts[row, :half].astype(f32) + swap(parts[row, half:], axis, order[0]).astype(f32)
        names = list(range(0, size, 2))
        for bit in order[1:]:
            keep = [n for n in names if not n & bit]
            sent = jnp.stack([held[names.index(n ^ bit)] for n in keep]).astype(bf16)
            kept = jnp.stack([held[names.index(n)] for n in keep])
            held = kept + swap(sent, axis, bit).astype(f32)
            names = keep
        out.append(held[0])
    return jnp.stack(out)


def after(value, *earlier):
    return lax.optimization_barrier((value,) + earlier)[0]


def sum_all(value, axes):
    for axis in axes:
        for i in range(lax.axis_size(axis).bit_length() - 1):
            value = value + swap(value, axis, 1 << i)
    return value


def mm(left, right):
    return jnp.dot(left, right, preferred_element_type=f32)


def contract_rows(left, right):
    return lax.dot_general(left, right, (((0,), (0,)), ((), ())), preferred_element_type=f32)


def contract_cols(left, right):
    return lax.dot_general(left, right, (((1,), (1,)), ((), ())), preferred_element_type=f32)


def rms_scale(values, scale_gain):
    return values * lax.rsqrt(jnp.mean(values * values, axis=-1, keepdims=True) + EPS_NORM) * scale_gain


def head_norm(mixer_out, gate_head, norm_head):
    scaled = (
        mixer_out * lax.rsqrt(jnp.mean(mixer_out * mixer_out, axis=-1, keepdims=True) + EPS_HEAD) * norm_head
    )
    return scaled * jax.nn.silu(gate_head)


def head_norms(mixer_out, gate_head, norm_head):
    parts = [slice(i, i + DV) for i in range(0, gate_head.shape[-1], DV)]
    return jnp.concatenate([head_norm(mixer_out[:, p], gate_head[:, p], norm_head) for p in parts], axis=1)


def glu_hidden(gate_half, up_half):
    return jax.nn.silu(gate_half) * up_half


def exchanged(packed):
    return lax.all_to_all(packed, "seq", split_axis=0, concat_axis=0, tiled=True)


def stacked(blocks):
    full = lax.all_gather(blocks, "batch", axis=0, tiled=False)
    return full.reshape(-1, blocks.shape[-1])


def summed(partial_grad):
    own = lax.psum_scatter(partial_grad, "batch", scatter_dimension=0, tiled=True)
    return own.reshape(lax.axis_size("seq"), -1, own.shape[-1])


def shards(
    tokens,
    grad_out,
    resets,
    w_proj,
    w_small,
    w_out,
    w_gu,
    w_down,
    norm_in,
    norm_ff,
    norm_head,
    conv_w,
    a_log,
    dt_bias,
):
    size = lax.axis_size("seq")
    groups = lax.axis_size("batch")
    me = lax.axis_index("seq")
    batch_rows, span_len, _ = tokens.shape
    own_rows = w_proj.shape[0]
    heads = H // size
    ff = FF // size
    key_w, val_w = heads * DK, heads * DV
    conv_cols = 2 * key_w + val_w
    tok_rows = batch_rows * span_len
    shape_in = (batch_rows, span_len, D)
    everyone = (batch_rows, size, span_len)

    def shuffled(array):
        lead = array.shape[:-1]
        return array.reshape(lead + (size, groups, own_rows)).swapaxes(-3, -2).reshape(lead + (D,))

    def restored(array):
        lead = array.shape[:-1]
        return array.reshape(lead + (groups, size, own_rows)).swapaxes(-3, -2).reshape(lead + (D,))

    small = jnp.concatenate(
        [w_small[:, :H].reshape(own_rows, size, heads), w_small[:, H:].reshape(own_rows, size, heads)], axis=-1
    )
    small = jnp.pad(small, ((0, 0), (0, 0), (0, LANES - 2 * heads)))
    packed_mix = jnp.concatenate(
        [
            w_proj[:, :KW].reshape(own_rows, size, key_w),
            w_proj[:, KW : 2 * KW].reshape(own_rows, size, key_w),
            w_proj[:, 2 * KW : CW].reshape(own_rows, size, val_w),
            small,
        ],
        axis=-1,
    ).transpose(1, 0, 2)
    out_w = lax.all_gather(shuffled(w_out), "batch", axis=0, tiled=True)
    moved_mix = exchanged(packed_mix)
    mix_w = stacked(after(moved_mix, out_w))
    packed_gate, packed_gu = after(
        (
            w_proj[:, CW:].reshape(own_rows, size, val_w).transpose(1, 0, 2),
            w_gu.reshape(own_rows, 2, size, ff).transpose(2, 0, 1, 3).reshape(size, own_rows, 2 * ff),
        ),
        moved_mix,
    )
    gate_w = stacked(after(exchanged(packed_gate), mix_w))
    gu_w = stacked(after(exchanged(packed_gu), mix_w))
    down_w = lax.all_gather(after(shuffled(w_down), mix_w), "batch", axis=0, tiled=True)

    order = jnp.arange(size, dtype=jnp.int32) ^ me.astype(jnp.int32)
    slots = slot_of(order, size)
    conv_l = jnp.concatenate(
        [
            lax.dynamic_slice_in_dim(conv_w, me * key_w, key_w, 1),
            lax.dynamic_slice_in_dim(conv_w, KW + me * key_w, key_w, 1),
            lax.dynamic_slice_in_dim(conv_w, 2 * KW + me * val_w, val_w, 1),
        ],
        axis=1,
    )
    at_heads = (heads, LANES - 2 * heads)
    aux = jnp.pad(
        jnp.stack(
            [
                lax.dynamic_slice_in_dim(jnp.exp(a_log), me * heads, heads),
                lax.dynamic_slice_in_dim(dt_bias, me * heads, heads),
            ]
        ),
        ((0, 6), at_heads),
    )

    flat_in = shuffled(tokens).astype(f32)
    gain_in, gain_ff = shuffled(norm_in), shuffled(norm_ff)
    normed_in, pull_norm_in = jax.vjp(rms_scale, flat_in, gain_in)
    h_in = gather_rows(normed_in.astype(bf16), "seq").reshape(-1, D)
    proj = mm(h_in, mix_w).reshape(everyone + (conv_cols + LANES,))
    mixed, states, invs, deltas = mixer_forward(proj, slots, resets, conv_l, aux)
    gate = mm(h_in, gate_w)
    heads_out, pull_head = jax.vjp(head_norms, mixed.reshape(-1, val_w), gate, norm_head)
    z_rows = heads_out.astype(bf16)
    residual = flat_in + scatter_rows(mm(z_rows, out_w).astype(bf16).reshape(everyone + (D,)), "seq")

    normed_ff, pull_norm_ff = jax.vjp(rms_scale, residual, gain_ff)
    h_ff = gather_rows(normed_ff.astype(bf16), "seq").reshape(-1, D)
    d_own = shuffled(grad_out)
    d_out = gather_rows(d_own, "seq").reshape(-1, D)
    gate_up = mm(h_ff, gu_w)
    hidden_full, pull_glu = jax.vjp(glu_hidden, gate_up[:, :ff], gate_up[:, ff:])
    hidden = hidden_full.astype(bf16)
    block_out = residual + scatter_rows(mm(hidden, down_w).astype(bf16).reshape(everyone + (D,)), "seq")
    down_grad = contract_rows(d_out, hidden).astype(bf16)
    down_own = summed(down_grad)
    d_hidden = contract_cols(after(d_out, down_grad), down_w)
    d_gate_up = jnp.concatenate(pull_glu(d_hidden), axis=1).astype(bf16)
    d_h_ff = scatter_rows(contract_cols(d_gate_up, gu_w).astype(bf16).reshape(everyone + (D,)), "seq")
    gu_grad = contract_rows(h_ff, d_gate_up).astype(bf16)
    gu_own = summed(gu_grad)
    d_resid_norm, g_norm_ff = pull_norm_ff(d_h_ff)
    d_residual = d_own.astype(f32) + d_resid_norm

    d_branch = gather_rows(after(d_residual.astype(bf16), gu_grad, down_own), "seq").reshape(-1, D)
    d_heads = contract_cols(d_branch, out_w)
    d_mixed, d_gate, g_norm_head = pull_head(d_heads)
    d_gate = d_gate.astype(bf16)
    out_grad = jnp.concatenate(
        [contract_rows(h_in, d_gate).astype(bf16), contract_rows(d_branch, z_rows).astype(bf16)], axis=1
    )
    d_mixed = after(d_mixed, out_grad)
    d_proj, g_conv_l, g_decay = mixer_backward(
        proj, d_mixed.reshape(everyone + (val_w,)), slots, resets, conv_l, aux, states, invs, deltas
    )
    d_proj, gu_own = lax.optimization_barrier((d_proj.reshape(-1, conv_cols + LANES), gu_own))
    out_own = summed(out_grad)
    mix_grad = contract_rows(h_in, d_proj).astype(bf16)
    mix_own = summed(after(mix_grad, out_own))
    d_proj = after(d_proj, mix_grad)
    down_grads = exchanged(down_own)
    gu_grads = exchanged(gu_own)
    out_grads = exchanged(out_own)
    mix_grads = exchanged(mix_own)
    d_h_in = scatter_rows(
        (contract_cols(d_proj, mix_w) + contract_cols(d_gate, gate_w)).astype(bf16).reshape(everyone + (D,)), "seq"
    )
    d_flat, g_norm_in = pull_norm_in(d_h_in)
    d_tokens = restored((d_residual + d_flat).astype(bf16))

    local = jnp.concatenate([g_conv_l[:TAPS].reshape(-1), g_decay[:2, heads : 2 * heads].reshape(-1)])
    shared = gather_rows(sum_all(local, ("batch",))[None], "seq")[0][slots]
    g_conv_all = shared[:, : TAPS * conv_cols].reshape(size, TAPS, conv_cols).transpose(1, 0, 2)
    g_conv = jnp.concatenate(
        [
            g_conv_all[:, :, :key_w].reshape(TAPS, KW),
            g_conv_all[:, :, key_w : 2 * key_w].reshape(TAPS, KW),
            g_conv_all[:, :, 2 * key_w :].reshape(TAPS, VW),
        ],
        axis=1,
    )
    g_alog = shared[:, TAPS * conv_cols : TAPS * conv_cols + heads].reshape(H)
    g_dt = shared[:, TAPS * conv_cols + heads :].reshape(H)
    gains = sum_all(jnp.concatenate([g_norm_in, g_norm_ff, g_norm_head]), ("seq", "batch"))

    def columns_of(grads, first, width):
        return grads[:, :, first : first + width].astype(f32).transpose(1, 0, 2).reshape(own_rows, size * width)

    g_proj = jnp.concatenate(
        [
            columns_of(mix_grads, 0, key_w),
            columns_of(mix_grads, key_w, key_w),
            columns_of(mix_grads, 2 * key_w, val_w),
            columns_of(out_grads, 0, val_w),
        ],
        axis=1,
    )
    g_small = jnp.concatenate(
        [columns_of(mix_grads, conv_cols, heads), columns_of(mix_grads, conv_cols + heads, heads)], axis=1
    )
    g_out = out_grads[:, :, val_w:].astype(f32).transpose(0, 2, 1).reshape(VW, own_rows)
    g_gu = gu_grads.astype(f32).reshape(size, own_rows, 2, ff).transpose(1, 2, 0, 3)
    g_down = down_grads.astype(f32).transpose(0, 2, 1).reshape(FF, own_rows)
    return (
        restored(block_out.astype(bf16)),
        d_tokens,
        g_proj,
        g_small,
        g_out,
        g_gu.reshape(own_rows, 2 * FF),
        g_down,
        restored(gains[:D]),
        restored(gains[D : 2 * D]),
        gains[2 * D :],
        g_conv,
        g_alog,
        g_dt,
    )


def solution(mesh):
    rows = P(("seq", "batch"), None)
    cols = P(None, ("seq", "batch"))
    act = P("batch", "seq", None)
    in_specs = (act, act, P("batch"), rows, rows, rows, rows, rows) + (P(),) * 6
    out_specs = (act, act, rows, rows, cols, rows, cols) + (P(),) * 6
    return jax.shard_map(shards, mesh=mesh, in_specs=in_specs, out_specs=out_specs, check_vma=False)
```

time: 4660 us -> 807 us (0.17)
  waiting for transfers between devices: 3360 us -> 208 us
  matrix products: 502 us -> 92.6 us
  other arithmetic: 315 us -> 69.9 us
  local copies, waits for them, and re-layouts: 330 us -> 193 us
  Pallas kernels: 0 us -> 133 us
  blocking collectives: 117 us -> 0 us
  starting transfers between devices: 5.01 us -> 88.4 us
    unnamed x12 -> x9, waiting for transfers between devices: 1380 us -> 0.15 us
    reduce_scatter x1 -> x4, waiting for transfers between devices: 1170 us -> 6.33 us  [summed(): lax.psum_scatter(partial_grad, 'batch', scatter_dimension=0, tiled=True)]
    all_gather x8 -> x5, waiting for transfers between devices: 696 us -> 80.6 us  [the longest x3 42 us: stacked(): full = lax.all_gather(blocks, 'batch', axis=0, tiled=False)]
    dot_general x54 -> x15, matrix products: 492 us -> 92.6 us  [the longest x5 31.4 us: contract_rows(): lax.dot_general(left, right, (((0,), (0,)), ((), ())), preferred_element_...]
    concatenate x1 -> x5, local copies, waits for them, and re-layouts: 180 us -> 4.12 us  [the longest x4 4.12 us: gather_rows(): whole_rows = jnp.concatenate(laid, axis=0)]
    another operation x8 -> x10, other arithmetic: 168 us -> 12 us  [the longest x2 160 us: group_pieces(): solved = jax.scipy.linalg.solve_triangular(system, right_side, lower=True)]
    pallas_call x0 -> x2, Pallas kernels: none -> 133 us  [the longest x1 73.2 us: mixer_forward(): pl.pallas_call(partial(forward_kernel, heads), grid_spec=pltpu.PrefetchSc...]
    psum x1 -> x0, waiting for transfers between devices: 121 us -> none  [shards(): lax.psum((g_norm_in, g_norm_ff, g_norm_head, g_conv, g_alog, g_dt), ('seq...]
  transfers between devices with their start and end apart: 13 -> 74, of which waited for: 9 -> 28; matrix products, arithmetic and copies ran while one was open for 20% -> 39% of each run, Pallas kernels for 0% -> 17%
where the time goes in v1:
time: 807 us; the launch traced here: 800 us
  waiting for transfers between devices  208 us (26%)
  local copies, waits for them, and re-layouts  193 us (24%)
  Pallas kernels  133 us (16%)
  matrix products  92.6 us (11%)
  starting transfers between devices  88.4 us (11%)
  other arithmetic  69.9 us (9%)
  between operations  16.2 us (2%)
    ppermute x58, waiting for transfers between devices, swap(): lax.ppermute(value, axis, [(i, i ^ bit) for i in range(lax.axis_size(axis...  117 us
    unnamed x220, local copies, waits for them, and re-layouts  81.7 us
    pallas_call x1, Pallas kernels, mixer_forward(): pl.pallas_call(partial(forward_kernel, heads), grid_spec=pltpu.PrefetchSc...  73.2 us
    pallas_call x1, Pallas kernels, mixer_backward(): pl.pallas_call(partial(backward_kernel, heads, chunks), grid_spec=pltpu.P...  59.6 us
    ppermute x58, starting transfers between devices, swap(): lax.ppermute(value, axis, [(i, i ^ bit) for i in range(lax.axis_size(axis...  56.6 us
    all_gather x3, waiting for transfers between devices, stacked(): full = lax.all_gather(blocks, 'batch', axis=0, tiled=False)  42 us
    all_gather x1, waiting for transfers between devices, shards(): lax.all_gather(after(shuffled(w_down), mix_w), 'batch', axis=0, tiled=True)  38.6 us
    dot_general x5, matrix products, contract_rows(): lax.dot_general(left, right, (((0,), (0,)), ((), ())), preferred_element_...  31.4 us
  transfers between devices with their start and end apart: 74, of which 28 were waited for; matrix products, arithmetic and copies ran while one was open for 39% of the time, Pallas kernels for 17%

profile of v1, /device:TPU:0, one launch (start us, length us, event | category | flops | bytes accessed | tf_op | source)
XLA Modules:
  0.0 800.2 jit_solution(11832782767485925088)
XLA Ops:
  60.8 4.7 reshape.390
  83.5 13.8 %collective-permute-done.25 = bf16[2,64,2048]{2,1,0:T(8,128)(2,1)S(1)} collective-permute-done((bf16[2,64,2048]{2,1,0:T(8,128)(2,1)S(1)}, bf16[2,64,2048]{2,1,0:T(8,128)(2,1)S(1)}, u32[]{:S(2)}, u32[]{:S(2)}) %collective-permute-start.25) | collective-permute-done | bytes 524320 | tf_op jit(solution)/shard_map/ppermute | solution.py:390
  129.5 4.3 all-to-all-start.2
  133.8 26.6 %all-gather.13.cloned.1.call-done = bf16[32,64,1152]{2,1,0:T(8,128)(2,1)} async-done(((bf16[8,64,1152]{2,1,0:T(8,128)(2,1)}), bf16[32,64,1152]{2,1,0:T(8,128)(2,1)}) %all-gather.13.cloned.1.call-update) | async-done | bytes 4718608 | tf_op jit(solution)/shard_map/all_gather | solution.py:491
  160.8 8.8 %fusion.59.proj.tail = f32[2,8,64,1152]{3,2,1,0:T(8,128)S(1)} fusion(bf16[2,8,64,2048]{3,2,1,0:T(8,128)(2,1)} %bitcast.271, bf16[2048,1152,1,1]{1,0,3,2:T(8,128)(2,1)} %bitcast.285), kind=kOutput, calls=%fused_computation.281 | convolution fusion | flops 4831838208 | bytes 13631488 | tf_op jit(solution)/shard_map/dot_general | solution.py:455
  169.6 73.2 %delta_forward.1 = (f32[2,8,64,512]{3,2,1,0:T(8,128)S(1)}, f32[8,4,128,256]{3,2,1,0:T(8,128)S(1)}, f32[8,4,64,64]{3,2,1,0:T(8,128)S(1)}, f32[8,4,64,256]{3,2,1,0:T(8,128)S(1)}) custom-call(s32[8]{0:T(128)S(1)} %multiply_or_fusion.pos_ref, s32[2]{0:T(128)S(1)} %copy-done, f32[2,8,64,1152]{3,2,1,0:T(8,128)S(1)} %fusion.59.proj.tail, ...), custom_call_target="tpu_custom_call" | custom-call | flops 60000002048 | bytes 40000000 | tf_op jit(solution)/shard_map/delta_forward/pallas_call | solution.py:328
  255.2 5.4 fusion.60
  276.3 9.1 %collective-permute-done.10 = bf16[2,64,2048]{2,1,0:T(8,128)(2,1)S(1)} collective-permute-done((bf16[2,64,2048]{2,1,0:T(8,128)(2,1)S(1)}, bf16[2,64,2048]{2,1,0:T(8,128)(2,1)S(1)}, u32[]{:S(2)}, u32[]{:S(2)}) %collective-permute-start.10) | collective-permute-done | bytes 524320 | tf_op jit(solution)/shard_map/ppermute | solution.py:390
  320.4 6.4 collective-permute-done.13
  344.6 15.4 %all-gather.17.cloned.1.call-done = bf16[32,64,1408]{2,1,0:T(8,128)(2,1)} async-done(((bf16[8,64,1408]{2,1,0:T(8,128)(2,1)}), bf16[32,64,1408]{2,1,0:T(8,128)(2,1)}) %all-gather.17.cloned.1.call-update) | async-done | bytes 5767184 | tf_op jit(solution)/shard_map/all_gather | solution.py:491
  359.9 10.5 %fusion.61 = f32[1024,1408]{1,0:T(8,128)S(1)} fusion(bf16[1024,2048]{1,0:T(8,128)(2,1)} %bitcast.277, bf16[2048,1408]{1,0:T(8,128)(2,1)} %bitcast.283), kind=kOutput, calls=%fused_computation.283 | convolution fusion | flops 5905580032 | bytes 15728640 | tf_op jit(solution)/shard_map/dot_general | solution.py:455
  373.0 7.0 convolution_convert_fusion.5
  380.3 38.6 %all-gather.11.cloned.1.call-done = bf16[704,2048]{1,0:T(8,128)(2,1)} async-done(((bf16[176,2048]{1,0:T(8,128)(2,1)}), bf16[704,2048]{1,0:T(8,128)(2,1)}) %all-gather.11.cloned.1.call-update) | async-done | bytes 2883600 | tf_op jit(solution)/shard_map/all_gather | solution.py:562
  418.9 9.2 %fusion.2 = (bf16[1024,704]{1,0:T(8,128)(2,1)S(1)}, bf16[1024,704]{1,0:T(8,128)(2,1)S(1)}) fusion(f32[1024,1408]{1,0:T(8,128)} %copy-done.28, bf16[1024,2048]{1,0:T(8,128)(2,1)} %bitcast.37, bf16[704,2048]{1,0:T(8,128)(2,1)} %all-gather.11.cloned.1.call-done), kind=kOutput, calls=%fused_computation.12 | convolution fusion | flops 2962882560 | bytes 15728640 | tf_op jit(solution)/shard_map/dot_general | solution.py:463
  428.0 8.8 %convolution_convert_fusion.2 = bf16[1024,2048]{1,0:T(8,128)(2,1)S(1)} fusion(bf16[2048,1408]{1,0:T(8,128)(2,1)} %bitcast.284, bf16[1024,704]{1,0:T(8,128)(2,1)S(1)} %get-tuple-element.66, bf16[1024,704]{1,0:T(8,128)(2,1)S(1)} %get-tuple-element.65), kind=kOutput, calls=%fused_computation.6 | convolution fusion | flops 5913444352 | bytes 12845056 | tf_op jit(solution)/shard_map/dot_general | solution.py:463
  448.9 8.8 %convolution_convert_fusion.1 = bf16[2048,1408]{1,0:T(8,128)(2,1)} fusion(bf16[1024,2048]{1,0:T(8,128)(2,1)S(1)} %bitcast.278, bf16[1024,704]{1,0:T(8,128)(2,1)S(1)} %get-tuple-element.66, bf16[1024,704]{1,0:T(8,128)(2,1)S(1)} %get-tuple-element.65), kind=kOutput, calls=%fused_computation.3 | convolution fusion | flops 5914230784 | bytes 12845056 | tf_op jit(solution)/shard_map/dot_general | solution.py:459
  464.7 10.5 %collective-permute-done.31 = bf16[2,64,2048]{2,1,0:T(8,128)(2,1)S(1)} collective-permute-done((bf16[2,64,2048]{2,1,0:T(8,128)(2,1)S(1)}, bf16[2,64,2048]{2,1,0:T(8,128)(2,1)S(1)}, u32[]{:S(2)}, u32[]{:S(2)}) %collective-permute-start.31) | collective-permute-done | bytes 524320 | tf_op jit(solution)/shard_map/ppermute | solution.py:390
  514.6 10.6 %collective-permute-done.37 = bf16[2,64,2048]{2,1,0:T(8,128)(2,1)S(1)} collective-permute-done((bf16[2,64,2048]{2,1,0:T(8,128)(2,1)S(1)}, bf16[2,64,2048]{2,1,0:T(8,128)(2,1)S(1)}, u32[]{:S(2)}, u32[]{:S(2)}) %collective-permute-start.37) | collective-permute-done | bytes 524320 | tf_op jit(solution)/shard_map/ppermute | solution.py:390
  526.4 4.7 collective-permute-done.40
  557.0 59.6 %delta_backward.1 = (bf16[2,8,64,1152]{3,2,1,0:T(8,128)(2,1)S(1)}, f32[8,1024]{1,0:T(8,128)S(1)}, f32[8,128]{1,0:T(8,128)S(1)}) custom-call(s32[8]{0:T(128)S(1)} %multiply_or_fusion.pos_ref, s32[2]{0:T(128)S(1)} %copy-done, f32[2,8,64,1152]{3,2,1,0:T(8,128)S(1)} %copy-done.4, f32[2,8,64,1152]{3,2,1,0:T(8,128)S(1)} %copy-done.4, ...), custom_call_target="tpu_custom_call" | custom-call | flops 60000002048 | bytes 40000000 | tf_op jit(solution)/shard_map/delta_backward/pallas_call | solution.py:360
  626.7 5.2 collective-permute-done.54
  644.2 10.8 %convolution_convert_fusion = bf16[2048,1152]{1,0:T(8,128)(2,1)} fusion(bf16[1024,2048]{1,0:T(8,128)(2,1)} %bitcast.273, bf16[1024,1152]{1,0:T(8,128)(2,1)S(1)} %bitcast.231), kind=kOutput, calls=%fused_computation.2 | convolution fusion | flops 4834197504 | bytes 11272192 | tf_op jit(solution)/shard_map/dot_general | solution.py:459
  655.1 6.3 reduce-scatter.9.cloned.1.call-done
  663.7 7.7 fusion.63
  681.5 4.5 all-to-all-start.5
  693.0 22.8 %collective-permute-done.43 = bf16[2,64,2048]{2,1,0:T(8,128)(2,1)S(1)} collective-permute-done((bf16[2,64,2048]{2,1,0:T(8,128)(2,1)S(1)}, bf16[2,64,2048]{2,1,0:T(8,128)(2,1)S(1)}, u32[]{:S(2)}, u32[]{:S(2)}) %collective-permute-start.43) | collective-permute-done | bytes 524320 | tf_op jit(solution)/shard_map/ppermute | solution.py:390
  718.1 6.1 collective-permute-done.44
  743.4 5.3 reshape.456
  748.6 5.5 copy.316
  754.1 4.8 reshape.447
  765.7 4.5 all-to-all-start.3
  770.3 4.9 fusion.18
  (563 shorter events, 359.8 us)
Async XLA Ops:
  7.2 64.3 %all-gather.9.cloned.1.call-start = ((), (), s32[]{:S(2)}) async-start(), calls=%async_computation.11 | async-start | bytes 2621440 | tf_op jit(solution)/shard_map/all_gather | solution.py:550
  16.2 55.3 %collective-permute-start = (bf16[1,64,2048]{2,1,0:T(8,128)(2,1)}, bf16[1,64,2048]{2,1,0:T(8,128)(2,1)}, u32[]{:S(2)}, u32[]{:S(2)}) collective-permute-start(bf16[1,64,2048]{2,1,0:T(8,128)(2,1)} %get-tuple-element.137), channel_id=1, source_target_pairs={{0,8},{4,12},{8,0},{12,4},{16,24},{20,28},{24,16},{28,20},{1,9},{5... | collective-permute-start | bytes 786440 | tf_op jit(solution)/shard_map/ppermute | solution.py:390
  19.1 54.1 %collective-permute-start.3 = (bf16[1,64,2048]{2,1,0:T(8,128)(2,1)}, bf16[1,64,2048]{2,1,0:T(8,128)(2,1)}, u32[]{:S(2)}, u32[]{:S(2)}) collective-permute-start(bf16[1,64,2048]{2,1,0:T(8,128)(2,1)} %get-tuple-element.135), channel_id=1, source_target_pairs={{0,16},{4,20},{8,24},{12,28},{16,0},{20,4},{24,8},{28,12},{1,17},{... | collective-permute-start | bytes 786440 | tf_op jit(solution)/shard_map/ppermute | solution.py:390
  29.8 41.7 %all-to-all-start = ((bf16[8,64,1152]{2,1,0:T(8,128)(2,1)}), bf16[8,64,1152]{2,1,0:T(8,128)(2,1)}, u32[]{:S(2)}, u32[]{:S(2)}) async-start(bf16[8,64,1152]{2,1,0:T(8,128)(2,1)} %copy.244), calls=%async_computation | async-start | bytes 2359296 | tf_op jit(solution)/shard_map/all_to_all | solution.py:487
  34.1 126.4 %all-gather.13.cloned.1.call-start = ((), (), s32[]{:S(2)}) async-start(), calls=%async_computation.17 | async-start | bytes 5898240 | tf_op jit(solution)/shard_map/all_gather | solution.py:491
  41.9 33.8 %collective-permute-start.24 = (bf16[1,64,2048]{2,1,0:T(8,128)(2,1)}, bf16[1,64,2048]{2,1,0:T(8,128)(2,1)}, u32[]{:S(2)}, u32[]{:S(2)}) collective-permute-start(bf16[1,64,2048]{2,1,0:T(8,128)(2,1)} %slice.433), channel_id=1, source_target_pairs={{0,8},{4,12},{8,0},{12,4},{16,24},{20,28},{24,16},{28,20},{1,9},{5... | collective-permute-start | bytes 786440 | tf_op jit(solution)/shard_map/ppermute | solution.py:390
  45.3 32.3 %collective-permute-start.27 = (bf16[1,64,2048]{2,1,0:T(8,128)(2,1)S(1)}, bf16[1,64,2048]{2,1,0:T(8,128)(2,1)}, u32[]{:S(2)}, u32[]{:S(2)}) collective-permute-start(bf16[1,64,2048]{2,1,0:T(8,128)(2,1)S(1)} %slice.435), channel_id=1, source_target_pairs={{0,16},{4,20},{8,24},{12,28},{16,0},{20,4},{24,8},{28,12},{1,17},{... | collective-permute-start | bytes 786440 | tf_op jit(solution)/shard_map/ppermute | solution.py:390
  72.6 26.8 %collective-permute-start.1 = (bf16[2,64,2048]{2,1,0:T(8,128)(2,1)S(1)}, bf16[2,64,2048]{2,1,0:T(8,128)(2,1)S(1)}, u32[]{:S(2)}, u32[]{:S(2)}) collective-permute-start(bf16[2,64,2048]{2,1,0:T(8,128)(2,1)S(1)} %pad_maximum_fusion.15), channel_id=1, source_target_pairs={{0,16},{4,20},{8,24},{12,28},{16,0},{20,4},{24,8},{28,12},{1,17},{... | collective-permute-start | bytes 1572872 | tf_op jit(solution)/shard_map/ppermute | solution.py:390
  74.3 27.8 %collective-permute-start.4 = (bf16[2,64,2048]{2,1,0:T(8,128)(2,1)S(1)}, bf16[2,64,2048]{2,1,0:T(8,128)(2,1)S(1)}, u32[]{:S(2)}, u32[]{:S(2)}) collective-permute-start(bf16[2,64,2048]{2,1,0:T(8,128)(2,1)S(1)} %pad_maximum_fusion.16), channel_id=1, source_target_pairs={{0,8},{4,12},{8,0},{12,4},{16,24},{20,28},{24,16},{28,20},{1,9},{5... | collective-permute-start | bytes 1572872 | tf_op jit(solution)/shard_map/ppermute | solution.py:390
  76.8 20.6 %collective-permute-start.25 = (bf16[2,64,2048]{2,1,0:T(8,128)(2,1)S(1)}, bf16[2,64,2048]{2,1,0:T(8,128)(2,1)S(1)}, u32[]{:S(2)}, u32[]{:S(2)}) collective-permute-start(bf16[2,64,2048]{2,1,0:T(8,128)(2,1)S(1)} %pad_maximum_fusion.21), channel_id=1, source_target_pairs={{0,16},{4,20},{8,24},{12,28},{16,0},{20,4},{24,8},{28,12},{1,17},{... | collective-permute-start | bytes 1572872 | tf_op jit(solution)/shard_map/ppermute | solution.py:390
  78.6 25.8 %collective-permute-start.28 = (bf16[2,64,2048]{2,1,0:T(8,128)(2,1)S(1)}, bf16[2,64,2048]{2,1,0:T(8,128)(2,1)S(1)}, u32[]{:S(2)}, u32[]{:S(2)}) collective-permute-start(bf16[2,64,2048]{2,1,0:T(8,128)(2,1)S(1)} %pad_maximum_fusion.22), channel_id=1, source_target_pairs={{0,8},{4,12},{8,0},{12,4},{16,24},{20,28},{24,16},{28,20},{1,9},{5... | collective-permute-start | bytes 1572872 | tf_op jit(solution)/shard_map/ppermute | solution.py:390
  106.6 166.3 %collective-permute-start.29 = (bf16[4,64,2048]{2,1,0:T(8,128)(2,1)}, bf16[4,64,2048]{2,1,0:T(8,128)(2,1)}, u32[]{:S(2)}, u32[]{:S(2)}) collective-permute-start(bf16[4,64,2048]{2,1,0:T(8,128)(2,1)} %pad_maximum_fusion.10), channel_id=1, source_target_pairs={{0,4},{4,0},{8,12},{12,8},{16,20},{20,16},{24,28},{28,24},{1,5},{5... | collective-permute-start | bytes 3145736 | tf_op jit(solution)/shard_map/ppermute | solution.py:390
  129.5 119.9 %all-to-all-start.2 = ((bf16[8,64,1408]{2,1,0:T(8,128)(2,1)}), bf16[8,64,1408]{2,1,0:T(8,128)(2,1)}, u32[]{:S(2)}, u32[]{:S(2)}) async-start(bf16[8,64,1408]{2,1,0:T(8,128)(2,1)} %reshape.390), calls=%async_computation.2 | async-start | bytes 2883584 | tf_op jit(solution)/shard_map/all_to_all | solution.py:487
  133.8 121.3 %all-gather.15.cloned.1.call-start = ((), (), s32[]{:S(2)}) async-start(), calls=%async_computation.18 | async-start | bytes 2621440 | tf_op jit(solution)/shard_map/all_gather | solution.py:491
  160.5 199.4 %all-gather.17.cloned.1.call-start = ((), (), s32[]{:S(2)}) async-start(), calls=%async_computation.19 | async-start | bytes 7208960 | tf_op jit(solution)/shard_map/all_gather | solution.py:491
  254.6 164.3 %all-gather.11.cloned.1.call-start = ((), (), s32[]{:S(2)}) async-start(), calls=%async_computation.12 | async-start | bytes 3604480 | tf_op jit(solution)/shard_map/all_gather | solution.py:562
  330.9 166.6 %reduce-scatter.5.cloned.1.call-start = ((), (), s32[]{:S(2)}) async-start(), calls=%async_computation.13 | async-start | bytes 3604480 | tf_op jit(solution)/shard_map/reduce_scatter | solution.py:496
  380.0 264.2 %reduce-scatter.7.cloned.1.call-start = ((), (), s32[]{:S(2)}) async-start(), calls=%async_computation.14 | async-start | bytes 7208960 | tf_op jit(solution)/shard_map/reduce_scatter | solution.py:496
  438.3 19.9 %collective-permute-start.30 = (bf16[4,64,2048]{2,1,0:T(8,128)(2,1)}, bf16[4,64,2048]{2,1,0:T(8,128)(2,1)}, u32[]{:S(2)}, u32[]{:S(2)}) collective-permute-start(bf16[4,64,2048]{2,1,0:T(8,128)(2,1)} %get-tuple-element.85), channel_id=1, source_target_pairs={{0,4},{4,0},{8,12},{12,8},{16,20},{20,16},{24,28},{28,24},{1,5},{5... | collective-permute-start | bytes 3145736 | tf_op jit(solution)/shard_map/ppermute | solution.py:390
  448.1 53.4 %collective-permute-start.21 = (bf16[4,64,2048]{2,1,0:T(8,128)(2,1)}, bf16[4,64,2048]{2,1,0:T(8,128)(2,1)}, u32[]{:S(2)}, u32[]{:S(2)}) collective-permute-start(bf16[4,64,2048]{2,1,0:T(8,128)(2,1)} %get-tuple-element.89), channel_id=1, source_target_pairs={{0,4},{4,0},{8,12},{12,8},{16,20},{20,16},{24,28},{28,24},{1,5},{5... | collective-permute-start | bytes 3145736 | tf_op jit(solution)/shard_map/ppermute | solution.py:390
  448.1 53.4 %collective-permute-start.18 = (bf16[4,64,2048]{2,1,0:T(8,128)(2,1)}, bf16[4,64,2048]{2,1,0:T(8,128)(2,1)}, u32[]{:S(2)}, u32[]{:S(2)}) collective-permute-start(bf16[4,64,2048]{2,1,0:T(8,128)(2,1)} %get-tuple-element.88), channel_id=1, source_target_pairs={{0,4},{4,0},{8,12},{12,8},{16,20},{20,16},{24,28},{28,24},{1,5},{5... | collective-permute-start | bytes 3145736 | tf_op jit(solution)/shard_map/ppermute | solution.py:390
  457.7 203.7 %reduce-scatter.9.cloned.1.call-start = ((), (), s32[]{:S(2)}) async-start(), calls=%async_computation.15 | async-start | bytes 5242880 | tf_op jit(solution)/shard_map/reduce_scatter | solution.py:496
  508.9 109.4 %collective-permute-start.22 = (bf16[2,64,2048]{2,1,0:T(8,128)(2,1)}, bf16[2,64,2048]{2,1,0:T(8,128)(2,1)}, u32[]{:S(2)}, u32[]{:S(2)}) collective-permute-start(bf16[2,64,2048]{2,1,0:T(8,128)(2,1)} %pad_maximum_fusion.20), channel_id=1, source_target_pairs={{0,8},{4,12},{8,0},{12,4},{16,24},{20,28},{24,16},{28,20},{1,9},{5... | collective-permute-start | bytes 1572872 | tf_op jit(solution)/shard_map/ppermute | solution.py:390
  511.2 112.7 %collective-permute-start.19 = (bf16[2,64,2048]{2,1,0:T(8,128)(2,1)}, bf16[2,64,2048]{2,1,0:T(8,128)(2,1)}, u32[]{:S(2)}, u32[]{:S(2)}) collective-permute-start(bf16[2,64,2048]{2,1,0:T(8,128)(2,1)} %stack.144), channel_id=1, source_target_pairs={{0,16},{4,20},{8,24},{12,28},{16,0},{20,4},{24,8},{28,12},{1,17},{... | collective-permute-start | bytes 1572872 | tf_op jit(solution)/shard_map/ppermute | solution.py:390
  639.4 38.5 %all-to-all-start.6 = ((bf16[8,64,704]{2,1,0:T(8,128)(2,1)}), bf16[8,64,704]{2,1,0:T(8,128)(2,1)S(1)}, u32[]{:S(2)}, u32[]{:S(2)}) async-start(bf16[8,64,704]{2,1,0:T(8,128)(2,1)} %bitcast.43), calls=%async_computation.10 | async-start | bytes 1572864 | tf_op jit(solution)/shard_map/all_to_all | solution.py:487
  643.6 122.1 %reduce-scatter.11.cloned.1.call-start = ((), (), s32[]{:S(2)}) async-start(), calls=%async_computation.16 | async-start | bytes 5898240 | tf_op jit(solution)/shard_map/reduce_scatter | solution.py:496
  643.7 36.9 %collective-permute-start.57 = (f32[4,4100]{1,0:T(4,128)S(1)}, f32[4,4100]{1,0:T(4,128)S(1)}, u32[]{:S(2)}, u32[]{:S(2)}) collective-permute-start(f32[4,4100]{1,0:T(4,128)S(1)} %pad_maximum_fusion.29), channel_id=1, source_target_pairs={{0,4},{4,0},{8,12},{12,8},{16,20},{20,16},{24,28},{28,24},{1,5},{5... | collective-permute-start | bytes 196808 | tf_op jit(solution)/shard_map/ppermute | solution.py:390
  681.5 53.7 %all-to-all-start.5 = ((bf16[8,64,1408]{2,1,0:T(8,128)(2,1)}), bf16[8,64,1408]{2,1,0:T(8,128)(2,1)}, u32[]{:S(2)}, u32[]{:S(2)}) async-start(bf16[8,64,1408]{2,1,0:T(8,128)(2,1)} %bitcast.47), calls=%async_computation.9 | async-start | bytes 2883584 | tf_op jit(solution)/shard_map/all_to_all | solution.py:487
  689.3 26.5 %collective-permute-start.43 = (bf16[2,64,2048]{2,1,0:T(8,128)(2,1)S(1)}, bf16[2,64,2048]{2,1,0:T(8,128)(2,1)S(1)}, u32[]{:S(2)}, u32[]{:S(2)}) collective-permute-start(bf16[2,64,2048]{2,1,0:T(8,128)(2,1)S(1)} %stack.142), channel_id=1, source_target_pairs={{0,16},{4,20},{8,24},{12,28},{16,0},{20,4},{24,8},{28,12},{1,17},{... | collective-permute-start | bytes 1572872 | tf_op jit(solution)/shard_map/ppermute | solution.py:390
  691.4 26.2 %collective-permute-start.46 = (bf16[2,64,2048]{2,1,0:T(8,128)(2,1)S(1)}, bf16[2,64,2048]{2,1,0:T(8,128)(2,1)S(1)}, u32[]{:S(2)}, u32[]{:S(2)}) collective-permute-start(bf16[2,64,2048]{2,1,0:T(8,128)(2,1)S(1)} %pad_maximum_fusion.26), channel_id=1, source_target_pairs={{0,8},{4,12},{8,0},{12,4},{16,24},{20,28},{24,16},{28,20},{1,9},{5... | collective-permute-start | bytes 1572872 | tf_op jit(solution)/shard_map/ppermute | solution.py:390
  735.2 30.5 %all-to-all-start.4 = ((bf16[8,64,1024]{2,1,0:T(8,128)(2,1)}), bf16[8,64,1024]{2,1,0:T(8,128)(2,1)}, u32[]{:S(2)}, u32[]{:S(2)}) async-start(bf16[8,64,1024]{2,1,0:T(8,128)(2,1)} %bitcast.54), calls=%async_computation.8 | async-start | bytes 2097152 | tf_op jit(solution)/shard_map/all_to_all | solution.py:487
  765.7 21.4 %all-to-all-start.3 = ((bf16[8,64,1152]{2,1,0:T(8,128)(2,1)}), bf16[8,64,1152]{2,1,0:T(8,128)(2,1)}, u32[]{:S(2)}, u32[]{:S(2)}) async-start(bf16[8,64,1152]{2,1,0:T(8,128)(2,1)} %bitcast.254), calls=%async_computation.7 | async-start | bytes 2359296 | tf_op jit(solution)/shard_map/all_to_all | solution.py:487
  (122 other events, 1250.3 us)
Sparse Core Ops, SparseCore 0:
  24.7 45.5 all-gather.8
  71.9 88.5 all-gather.12
  162.6 44.4 all-gather.14
  254.7 105.1 all-gather.16
  361.3 57.4 all-gather.10
  421.6 54.8 reduce-scatter.4
  478.8 102.1 reduce-scatter.6
  583.2 78.1 reduce-scatter.8
  663.8 85.7 reduce-scatter.10

commit v2 on v1

--- a/solution.py
+++ b/solution.py
@@ -24,7 +24,7 @@
 EPS_UNIT = 1e-06
 f32 = jnp.float32
 bf16 = jnp.bfloat16
-VMEM_BYTES = 32 * 1024 * 1024
+VMEM_BYTES = 56 * 1024 * 1024
 KERNEL_COST = pl.CostEstimate(flops=60_000_000_000, bytes_accessed=40_000_000, transcendentals=0)
 
 
@@ -132,7 +132,7 @@
 
 
 def forward_kernel(
-    heads, pos_ref, reset_ref, proj, conv_w_ref, aux_ref, outs, state_out, inv_out, delta_out, ext, state
+    heads, pos_ref, reset_ref, proj, small_ref, conv_w_ref, aux_ref, outs, state_out, inv_out, delta_out, ext, state
 ):
     chunk = pl.program_id(0)
     width = heads * (2 * DK + DV)
@@ -145,13 +145,13 @@
     state_out[0] = state[...]
     conv_w = conv_w_ref[...]
     aux = aux_ref[...]
-    for row in range(proj.shape[0]):
+    for row in range(proj.shape[1]):
         masks = position_masks(reset_ref[row], chunk)
         ext[row, 0:8, :] = ext[row, CH : CH + 8, :]
-        ext[row, 8:, :] = proj[row, 0, :, :width].astype(bf16).astype(f32)
+        ext[row, 8:, :] = proj[0, row, 0].astype(bf16).astype(f32)
         conv = conv_taps(ext, row, conv_w, masks[5])
         active = conv * jax.nn.sigmoid(conv)
-        beta_all, decay, _ = gates(proj[row, 0, :, width : width + LANES], aux)
+        beta_all, decay, _ = gates(small_ref[0, row, 0], aux)
         total = running(decay)
         total_rows = as_rows(total)
         for head in range(heads):
@@ -169,7 +169,7 @@
             delta = coarse(inv, beta * (v - start_fade * read[CH:]))
             out = start_fade * read[:CH] + coarse(ratios * pair[:CH], delta)
             state[at] = start_last * old + coarse(end_fade * k, delta, (0, 0))
-            outs[row, 0, :, head * DV : (head + 1) * DV] = out
+            outs[0, row, 0, :, head * DV : (head + 1) * DV] = out
             inv_out[0, at] = inv
             delta_out[0, at] = delta
 
@@ -180,6 +180,7 @@
     pos_ref,
     reset_ref,
     proj,
+    small_ref,
     tail,
     d_out,
     conv_w_ref,
@@ -188,6 +189,7 @@
     inv_ref,
     delta_ref,
     d_proj,
+    d_small_ref,
     g_conv,
     g_decay,
     ext,
@@ -209,15 +211,15 @@
     aux = aux_ref[...]
     lane_ids = lax.broadcasted_iota(jnp.int32, (CH, LANES), 1)
     ones = jnp.ones((CH, LANES), f32)
-    for row in range(proj.shape[0]):
+    for row in range(proj.shape[1]):
         masks = position_masks(reset_ref[row], chunk)
         taps = masks[5]
-        ext[row, 0:8, :] = tail[row, 0].astype(bf16).astype(f32)
-        ext[row, 8:, :] = proj[row, 0, :, :width].astype(bf16).astype(f32)
+        ext[row, 0:8, :] = tail[0, row, 0].astype(bf16).astype(f32)
+        ext[row, 8:, :] = proj[0, row, 0].astype(bf16).astype(f32)
         conv = conv_taps(ext, row, conv_w, taps)
         sig = jax.nn.sigmoid(conv)
         active = conv * sig
-        small = proj[row, 0, :, width : width + LANES]
+        small = small_ref[0, row, 0]
         beta_all, decay, shifted = gates(small, aux)
         total = running(decay)
         total_rows = as_rows(total)
@@ -239,7 +241,7 @@
             old = state_ref[0, at]
             inv = inv_ref[0, at]
             delta = delta_ref[0, at]
-            do = d_out[row, 0, :, head * DV : (head + 1) * DV]
+            do = d_out[0, row, 0, :, head * DV : (head + 1) * DV]
             ds = d_state[at]
             read = coarse(both, old)
             readings = ratios * query_key
@@ -306,8 +308,8 @@
             part = conv_w[j : j + 1] * dext[row, j, shift : shift + CH, :]
             d_in = part if d_in is None else d_in + part
             dext[row, j, CH : CH + 8, :] = masked[0:8]
-        d_proj[row, 0, :, :width] = d_in.astype(bf16)
-        d_proj[row, 0, :, width : width + LANES] = d_small.astype(bf16)
+        d_proj[0, row, 0] = d_in.astype(bf16)
+        d_small_ref[0, row, 0] = d_small.astype(bf16)
 
 
 def params():
@@ -318,24 +320,30 @@
     return pl.BlockSpec(array.shape, lambda c, pos, rst: (0,) * array.ndim)
 
 
-def mixer_forward(proj, pos, resets, conv_w, aux):
-    rows_n, chunks, _, total = proj.shape
-    width = total - LANES
+def slot_spec(rows_n, width, chunk_of):
+    return pl.BlockSpec(
+        (1, rows_n, 1, CH, width), lambda c, pos, rst: (pos[chunk_of(c)] & 1, 0, pos[chunk_of(c)] >> 1, 0, 0)
+    )
+
+
+def mixer_forward(proj, small, pos, resets, conv_w, aux):
+    _, rows_n, half, _, width = proj.shape
+    chunks = 2 * half
     heads = width // (2 * DK + DV)
     units = rows_n * heads
-    spec = lambda w: pl.BlockSpec((rows_n, 1, CH, w), lambda c, pos, rst: (0, pos[c], 0, 0))
+    spec = lambda w: slot_spec(rows_n, w, lambda c: c)
     kept = lambda *s: pl.BlockSpec((1, units) + s, lambda c, pos, rst: (c, 0, 0, 0))
     return pl.pallas_call(
         partial(forward_kernel, heads),
         grid_spec=pltpu.PrefetchScalarGridSpec(
             num_scalar_prefetch=2,
             grid=(chunks,),
-            in_specs=[spec(total), whole(conv_w), whole(aux)],
+            in_specs=[spec(width), spec(LANES), whole(conv_w), whole(aux)],
             out_specs=[spec(heads * DV), kept(DK, DV), kept(CH, CH), kept(CH, DV)],
             scratch_shapes=[pltpu.VMEM((rows_n, CH + 8, width), f32), pltpu.VMEM((units, DK, DV), f32)],
         ),
         out_shape=[
-            jax.ShapeDtypeStruct((rows_n, chunks, CH, heads * DV), f32),
+            jax.ShapeDtypeStruct((2, rows_n, half, CH, heads * DV), f32),
             jax.ShapeDtypeStruct((chunks, units, DK, DV), f32),
             jax.ShapeDtypeStruct((chunks, units, CH, CH), f32),
             jax.ShapeDtypeStruct((chunks, units, CH, DV), f32),
@@ -343,18 +351,20 @@
         cost_estimate=KERNEL_COST,
         compiler_params=params(),
         name="delta_forward",
-    )(pos, resets, proj, conv_w, aux)
-
-
-def mixer_backward(proj, d_out, pos, resets, conv_w, aux, states, invs, deltas):
-    rows_n, chunks, _, total = proj.shape
-    width = total - LANES
+    )(pos, resets, proj, small, conv_w, aux)
+
+
+def mixer_backward(proj, small, d_out, pos, resets, conv_w, aux, states, invs, deltas):
+    _, rows_n, half, _, width = proj.shape
+    chunks = 2 * half
     heads = width // (2 * DK + DV)
     units = rows_n * heads
     back = lambda c: chunks - 1 - c
-    spec = lambda w: pl.BlockSpec((rows_n, 1, CH, w), lambda c, pos, rst: (0, pos[back(c)], 0, 0))
+    before = lambda c: jnp.maximum(back(c) - 1, 0)
+    spec = lambda w: slot_spec(rows_n, w, back)
     tail = pl.BlockSpec(
-        (rows_n, 1, 8, width), lambda c, pos, rst: (0, pos[jnp.maximum(back(c) - 1, 0)], CH // 8 - 1, 0)
+        (1, rows_n, 1, 8, width),
+        lambda c, pos, rst: (pos[before(c)] & 1, 0, pos[before(c)] >> 1, CH // 8 - 1, 0),
     )
     kept = lambda *s: pl.BlockSpec((1, units) + s, lambda c, pos, rst: (back(c), 0, 0, 0))
     return pl.pallas_call(
@@ -362,10 +372,11 @@
         grid_spec=pltpu.PrefetchScalarGridSpec(
             num_scalar_prefetch=2,
             grid=(chunks,),
-            in_specs=[spec(total), tail, spec(heads * DV), whole(conv_w), whole(aux)]
+            in_specs=[spec(width), spec(LANES), tail, spec(heads * DV), whole(conv_w), whole(aux)]
             + [kept(DK, DV), kept(CH, CH), kept(CH, DV)],
             out_specs=[
-                spec(total),
+                spec(width),
+                spec(LANES),
                 pl.BlockSpec((8, width), lambda c, pos, rst: (0, 0)),
                 pl.BlockSpec((8, LANES), lambda c, pos, rst: (0, 0)),
             ],
@@ -376,14 +387,232 @@
             ],
         ),
         out_shape=[
-            jax.ShapeDtypeStruct((rows_n, chunks, CH, total), bf16),
+            jax.ShapeDtypeStruct((2, rows_n, half, CH, width), bf16),
+            jax.ShapeDtypeStruct((2, rows_n, half, CH, LANES), bf16),
             jax.ShapeDtypeStruct((8, width), f32),
             jax.ShapeDtypeStruct((8, LANES), f32),
         ],
         cost_estimate=KERNEL_COST,
         compiler_params=params(),
         name="delta_backward",
-    )(pos, resets, proj, proj, d_out, conv_w, aux, states, invs, deltas)
+    )(pos, resets, proj, small, proj, d_out, conv_w, aux, states, invs, deltas)
+
+
+def local_call(body, name, inputs, specs, outs, bytes_accessed):
+    return pl.pallas_call(
+        body,
+        grid=(1,),
+        in_specs=specs,
+        out_specs=whole_specs(outs),
+        out_shape=outs,
+        cost_estimate=pl.CostEstimate(flops=1_000_000, bytes_accessed=bytes_accessed, transcendentals=0),
+        compiler_params=pltpu.CompilerParams(vmem_limit_bytes=VMEM_BYTES),
+        name=name,
+    )(*inputs)
+
+
+def term_specs(terms):
+    kept, got, steps = terms
+    rows_n = kept.shape[0]
+    first = pl.BlockSpec((rows_n, 1) + kept.shape[2:], lambda i: (0, 0, 0, 0))
+    flat = [step for row in steps for step in row]
+    return [kept, got] + flat, [first, first] + [pl.BlockSpec((1,) + s.shape[1:], lambda i: (0, 0, 0)) for s in flat]
+
+
+def row_total(refs, row, rows_n):
+    kept, got = refs[0], refs[1]
+    each = (len(refs) - 2) // rows_n
+    total = kept[row, 0].astype(f32) + got[row, 0].astype(f32)
+    for step in refs[2 + row * each : 2 + (row + 1) * each]:
+        total = total + step[0].astype(f32)
+    return total
+
+
+def in_order(values, groups):
+    size, batches = groups
+    own = values.shape[-1] // (size * batches)
+    return jnp.concatenate(
+        [
+            values[:, (b * size + s) * own : (b * size + s + 1) * own]
+            for s in range(size)
+            for b in range(batches)
+        ],
+        axis=1,
+    )
+
+
+def whole_specs(arrays):
+    zeros = lambda n: lambda i: (0,) * n
+    return [pl.BlockSpec(a.shape, zeros(len(a.shape))) for a in arrays]
+
+
+def add_and_norm(terms, base, gain):
+    inputs, specs = term_specs(terms)
+    rows_n, _, span, _ = terms[0].shape
+
+    def body(*refs):
+        base_ref, gain_ref, out_ref, norm_ref = refs[len(inputs) :]
+        for row in range(rows_n):
+            at = pl.ds(row * span, span)
+            total = base_ref[at, :].astype(f32) + row_total(refs[: len(inputs)], row, rows_n)
+            scale = lax.rsqrt(jnp.mean(total * total, axis=-1, keepdims=True) + EPS_NORM)
+            out_ref[at, :] = total
+            norm_ref[row] = (total * scale * gain_ref[...]).astype(bf16)
+
+    extra = [base, gain.reshape(1, D)]
+    return local_call(
+        body,
+        "add_and_norm",
+        inputs + extra,
+        specs + whole_specs(extra),
+        [jax.ShapeDtypeStruct((rows_n * span, D), f32), jax.ShapeDtypeStruct((rows_n, span, D), bf16)],
+        4_000_000,
+    )
+
+
+def norm_back(terms, base, through, gain, out_dtype, groups=None):
+    inputs, specs = term_specs(terms)
+    rows_n, _, span, _ = terms[0].shape
+    with_rows = groups is None
+
+    def body(*refs):
+        base_ref, through_ref, gain_ref = refs[len(inputs) : len(inputs) + 3]
+        outs = refs[len(inputs) + 3 :]
+        g_gain = jnp.zeros((1, D), f32)
+        for row in range(rows_n):
+            at = pl.ds(row * span, span)
+            d_norm = row_total(refs[: len(inputs)], row, rows_n)
+            x = base_ref[at, :].astype(f32)
+            scale = lax.rsqrt(jnp.mean(x * x, axis=-1, keepdims=True) + EPS_NORM)
+            e = d_norm * gain_ref[...]
+            lean = jnp.mean(e * x, axis=-1, keepdims=True)
+            total = through_ref[at, :].astype(f32) + scale * e - x * (scale * scale * scale * lean)
+            g_gain = g_gain + jnp.sum(d_norm * x * scale, axis=0, keepdims=True)
+            if with_rows:
+                outs[0][at, :] = total.astype(out_dtype)
+                outs[1][row] = total.astype(bf16)
+            else:
+                outs[0][at, :] = in_order(total, groups).astype(out_dtype)
+        outs[-1][...] = g_gain
+
+    extra = [base, through, gain.reshape(1, D)]
+    outs = [jax.ShapeDtypeStruct((rows_n * span, D), out_dtype)]
+    if with_rows:
+        outs.append(jax.ShapeDtypeStruct((rows_n, span, D), bf16))
+    return local_call(
+        body,
+        "norm_back",
+        inputs + extra,
+        specs + whole_specs(extra),
+        outs + [jax.ShapeDtypeStruct((1, D), f32)],
+        4_000_000,
+    )
+
+
+def add_in_order(terms, base, groups):
+    inputs, specs = term_specs(terms)
+    rows_n, _, span, _ = terms[0].shape
+
+    def body(*refs):
+        base_ref, out_ref = refs[len(inputs) :]
+        for row in range(rows_n):
+            at = pl.ds(row * span, span)
+            total = base_ref[at, :] + row_total(refs[: len(inputs)], row, rows_n)
+            out_ref[at, :] = in_order(total, groups).astype(bf16)
+
+    return local_call(
+        body,
+        "add_in_order",
+        inputs + [base],
+        specs + whole_specs([base]),
+        [jax.ShapeDtypeStruct((rows_n * span, D), bf16)],
+        3_000_000,
+    )[0]
+
+
+ROW_BLOCK = 256
+
+
+def gated_norm(mixed, gate, gain):
+    rows_n, width = mixed.shape
+
+    def body(mixed_ref, gate_ref, gain_ref, out_ref):
+        for at in range(0, width, DV):
+            x = mixed_ref[:, at : at + DV]
+            g = gate_ref[:, at : at + DV]
+            scale = lax.rsqrt(jnp.mean(x * x, axis=-1, keepdims=True) + EPS_HEAD)
+            out_ref[:, at : at + DV] = (x * scale * gain_ref[...] * (g * jax.nn.sigmoid(g))).astype(bf16)
+
+    block = pl.BlockSpec((ROW_BLOCK, width), lambda i: (i, 0))
+    return pl.pallas_call(
+        body,
+        grid=(rows_n // ROW_BLOCK,),
+        in_specs=[block, block, pl.BlockSpec((1, DV), lambda i: (0, 0))],
+        out_specs=block,
+        out_shape=jax.ShapeDtypeStruct((rows_n, width), bf16),
+        cost_estimate=pl.CostEstimate(flops=1_000_000, bytes_accessed=5_000_000, transcendentals=0),
+        compiler_params=params(),
+        name="gated_norm",
+    )(mixed, gate, gain.reshape(1, DV))
+
+
+def gated_norm_back(mixed, gate, gain, d_out):
+    rows_n, width = mixed.shape
+
+    def body(mixed_ref, gate_ref, gain_ref, d_ref, d_mixed_ref, d_gate_ref, g_gain_ref):
+        @pl.when(pl.program_id(0) == 0)
+        def _():
+            g_gain_ref[...] = jnp.zeros_like(g_gain_ref)
+
+        g_gain = jnp.zeros((1, DV), f32)
+        for at in range(0, width, DV):
+            x = mixed_ref[:, at : at + DV]
+            g = gate_ref[:, at : at + DV]
+            d = d_ref[:, at : at + DV]
+            scale = lax.rsqrt(jnp.mean(x * x, axis=-1, keepdims=True) + EPS_HEAD)
+            sig = jax.nn.sigmoid(g)
+            through = d * (g * sig)
+            unit_x = x * scale
+            e = through * gain_ref[...]
+            lean = jnp.mean(e * unit_x, axis=-1, keepdims=True)
+            d_mixed_ref[:, at : at + DV] = scale * (e - unit_x * lean)
+            d_gate_ref[:, at : at + DV] = (
+                d * (unit_x * gain_ref[...]) * (sig * (1.0 + g * (1.0 - sig)))
+            ).astype(bf16)
+            g_gain = g_gain + jnp.sum(through * unit_x, axis=0, keepdims=True)
+        g_gain_ref[0:1, :] += g_gain
+
+    block = pl.BlockSpec((ROW_BLOCK, width), lambda i: (i, 0))
+    return pl.pallas_call(
+        body,
+        grid=(rows_n // ROW_BLOCK,),
+        in_specs=[block, block, pl.BlockSpec((1, DV), lambda i: (0, 0)), block],
+        out_specs=[block, block, pl.BlockSpec((8, DV), lambda i: (0, 0))],
+        out_shape=[
+            jax.ShapeDtypeStruct((rows_n, width), f32),
+            jax.ShapeDtypeStruct((rows_n, width), bf16),
+            jax.ShapeDtypeStruct((8, DV), f32),
+        ],
+        cost_estimate=pl.CostEstimate(flops=1_000_000, bytes_accessed=9_000_000, transcendentals=0),
+        compiler_params=params(),
+        name="gated_norm_back",
+    )(mixed, gate, gain.reshape(1, DV), d_out)
+
+
+def laid_out(blocks, pieces, total):
+    size, rows_n, _ = blocks[0].shape
+
+    def body(*refs):
+        out_ref = refs[-1]
+        for which, first, width, start in pieces:
+            for s in range(size):
+                out_ref[:, start + s * width : start + (s + 1) * width] = refs[which][
+                    s, :, first : first + width
+                ].astype(f32)
+
+    return local_call(
+        body, "laid_out", blocks, whole_specs(blocks), [jax.ShapeDtypeStruct((rows_n, total), f32)], 5_000_000
+    )[0]
 
 
 def swap(value, axis, bit):
@@ -395,49 +624,55 @@
     return [bits[1:] + bits[:1], bits[:0:-1] + bits[:1]]
 
 
-def slot_of(relative, chunks):
-    return (relative >> 1) | ((relative & 1) * (chunks // 2))
-
-
-def gather_rows(rows, axis):
-    size = lax.axis_size(axis)
-    orders = routes(axis)
+def gather_rows(rows, axis, ordered=True):
     laid = []
-    for row in range(rows.shape[0]):
-        order = orders[row % 2]
-        held = rows[row][None]
+    for row, order in zip(rows, routes(axis) * rows.shape[0]):
+        held = row[None]
         names = [0]
-        for bit in order[:-1]:
-            held = jnp.concatenate([held, swap(held, axis, bit)], axis=0)
-            names = names + [n ^ bit for n in names]
-        other = swap(held, axis, order[-1])
-        place = {name: i for i, name in enumerate(names)}
-        for part in (held, other):
-            if names == sorted(names):
-                laid.append(part)
+        parts = []
+        for i, bit in enumerate(order[:-1]):
+            got = swap(held, axis, bit)
+            names = names + [n ^ (bit >> 1) for n in names]
+            if i < len(order) - 2:
+                held = jnp.concatenate([held, got], axis=0)
             else:
-                laid.extend(part[place[n]][None] for n in sorted(names))
-    whole_rows = jnp.concatenate(laid, axis=0)
-    return whole_rows.reshape((rows.shape[0], size) + rows.shape[1:])
-
-
-def scatter_rows(parts, axis):
-    size = lax.axis_size(axis)
-    orders = routes(axis)
-    out = []
-    for row in range(parts.shape[0]):
-        order = orders[row % 2][::-1]
-        half = size // 2
-        held = parts[row, :half].astype(f32) + swap(parts[row, half:], axis, order[0]).astype(f32)
-        names = list(range(0, size, 2))
-        for bit in order[1:]:
-            keep = [n for n in names if not n & bit]
-            sent = jnp.stack([held[names.index(n ^ bit)] for n in keep]).astype(bf16)
-            kept = jnp.stack([held[names.index(n)] for n in keep])
-            held = kept + swap(sent, axis, bit).astype(f32)
-            names = keep
-        out.append(held[0])
-    return jnp.stack(out)
+                parts = [held, got]
+        if ordered and names != sorted(names):
+            place = {name: i for i, name in enumerate(names)}
+            size = len(names) // 2
+            for n in sorted(names):
+                which, at = divmod(place[n], size)
+                laid.append(parts[which][at : at + 1])
+        else:
+            laid.extend(parts)
+    even = jnp.concatenate(laid, axis=0).reshape((rows.shape[0], -1) + rows.shape[1:])
+    return even, swap(even, axis, 1)
+
+
+def scatter_rows(keep, send, axis, ordered=True, earlier=()):
+    got = after(swap(send, axis, 1), *earlier)
+    rows_n, half, span, width = keep.shape
+    depth = half.bit_length() - 1
+    steps = []
+    for row, order in zip(range(rows_n), routes(axis) * rows_n):
+        bits = order[:-1]
+        axes = sorted(bits, reverse=True) if ordered else bits[::-1]
+        shape = (2,) * depth + (span, width)
+        terms = [keep[row].reshape(shape), got[row].reshape(shape)]
+        mine = []
+        for bit in bits[::-1]:
+            at = axes.index(bit)
+            sent = sum(lax.index_in_dim(t, 1, at, keepdims=False).astype(f32) for t in terms).astype(bf16)
+            back = swap(sent, axis, bit)
+            terms = [lax.index_in_dim(t, 0, at, keepdims=False) for t in terms] + [back]
+            axes = [b for b in axes if b != bit]
+            mine.append(back.reshape((-1, span, width)))
+        steps.append(mine)
+    return keep, got, steps
+
+
+def joined(halves):
+    return jnp.concatenate([h.reshape(-1, h.shape[-1]) for h in halves], axis=0)
 
 
 def after(value, *earlier):
@@ -451,6 +686,14 @@
     return value
 
 
+def gather_small(value, axis):
+    held = value[None]
+    size = lax.axis_size(axis)
+    for i in range(size.bit_length() - 1):
+        held = jnp.concatenate([held, swap(held, axis, 1 << i)], axis=0)
+    return held[jnp.arange(size, dtype=jnp.int32) ^ lax.axis_index(axis).astype(jnp.int32)]
+
+
 def mm(left, right):
     return jnp.dot(left, right, preferred_element_type=f32)
 
@@ -465,18 +708,6 @@
 
 def rms_scale(values, scale_gain):
     return values * lax.rsqrt(jnp.mean(values * values, axis=-1, keepdims=True) + EPS_NORM) * scale_gain
-
-
-def head_norm(mixer_out, gate_head, norm_head):
-    scaled = (
-        mixer_out * lax.rsqrt(jnp.mean(mixer_out * mixer_out, axis=-1, keepdims=True) + EPS_HEAD) * norm_head
-    )
-    return scaled * jax.nn.silu(gate_head)
-
-
-def head_norms(mixer_out, gate_head, norm_head):
-    parts = [slice(i, i + DV) for i in range(0, gate_head.shape[-1], DV)]
-    return jnp.concatenate([head_norm(mixer_out[:, p], gate_head[:, p], norm_head) for p in parts], axis=1)
 
 
 def glu_hidden(gate_half, up_half):
@@ -522,9 +753,10 @@
     ff = FF // size
     key_w, val_w = heads * DK, heads * DV
     conv_cols = 2 * key_w + val_w
-    tok_rows = batch_rows * span_len
-    shape_in = (batch_rows, span_len, D)
-    everyone = (batch_rows, size, span_len)
+    half = batch_rows * size // 2 * span_len
+    cut = 16 * ff // 11 // LANES * LANES
+    halves = (batch_rows, size // 2, span_len)
+    blocks = (2,) + halves
 
     def shuffled(array):
         lead = array.shape[:-1]
@@ -534,35 +766,50 @@
         lead = array.shape[:-1]
         return array.reshape(lead + (groups, size, own_rows)).swapaxes(-3, -2).reshape(lead + (D,))
 
-    small = jnp.concatenate(
-        [w_small[:, :H].reshape(own_rows, size, heads), w_small[:, H:].reshape(own_rows, size, heads)], axis=-1
-    )
-    small = jnp.pad(small, ((0, 0), (0, 0), (0, LANES - 2 * heads)))
+    out_w = lax.all_gather(w_out, "batch", axis=0, tiled=True)
     packed_mix = jnp.concatenate(
         [
             w_proj[:, :KW].reshape(own_rows, size, key_w),
             w_proj[:, KW : 2 * KW].reshape(own_rows, size, key_w),
             w_proj[:, 2 * KW : CW].reshape(own_rows, size, val_w),
-            small,
         ],
         axis=-1,
     ).transpose(1, 0, 2)
-    out_w = lax.all_gather(shuffled(w_out), "batch", axis=0, tiled=True)
     moved_mix = exchanged(packed_mix)
-    mix_w = stacked(after(moved_mix, out_w))
-    packed_gate, packed_gu = after(
+    own_in = shuffled(tokens).reshape(-1, D)
+    gain_in, gain_ff = shuffled(norm_in), shuffled(norm_ff)
+    h_in = joined(gather_rows(rms_scale(own_in.astype(f32), gain_in).astype(bf16).reshape(tokens.shape), "seq"))
+    mix_w = stacked(after(moved_mix, out_w, h_in))
+    packed_gate, packed_gu, w_small, d_own, own_down = after(
         (
             w_proj[:, CW:].reshape(own_rows, size, val_w).transpose(1, 0, 2),
             w_gu.reshape(own_rows, 2, size, ff).transpose(2, 0, 1, 3).reshape(size, own_rows, 2 * ff),
+            w_small,
+            shuffled(grad_out),
+            shuffled(w_down),
         ),
         moved_mix,
     )
-    gate_w = stacked(after(exchanged(packed_gate), mix_w))
-    gu_w = stacked(after(exchanged(packed_gu), mix_w))
-    down_w = lax.all_gather(after(shuffled(w_down), mix_w), "batch", axis=0, tiled=True)
-
-    order = jnp.arange(size, dtype=jnp.int32) ^ me.astype(jnp.int32)
-    slots = slot_of(order, size)
+    d_out = joined(gather_rows(d_own, "seq", False))
+    small_all = gather_small(gather_small(w_small, "seq"), "batch").reshape(D, 2 * H)
+    small_w = jnp.pad(
+        jnp.concatenate(
+            [
+                lax.dynamic_slice_in_dim(small_all, me * heads, heads, 1),
+                lax.dynamic_slice_in_dim(small_all, H + me * heads, heads, 1),
+            ],
+            axis=1,
+        ),
+        ((0, 0), (0, LANES - 2 * heads)),
+    )
+    out_w = shuffled(out_w)
+    moved_gate, moved_gu = exchanged(packed_gate), exchanged(packed_gu)
+    moved_gate, moved_gu, small_w, mix_w = lax.optimization_barrier((moved_gate, moved_gu, small_w, mix_w))
+    gate_w = stacked(moved_gate)
+    moved_first, moved_rest = moved_gu[:, :, :cut], moved_gu[:, :, cut:]
+    gu_first = stacked(moved_first)
+
+    slots = jnp.arange(size, dtype=jnp.int32) ^ me.astype(jnp.int32)
     conv_l = jnp.concatenate(
         [
             lax.dynamic_slice_in_dim(conv_w, me * key_w, key_w, 1),
@@ -582,63 +829,76 @@
         ((0, 6), at_heads),
     )
 
-    flat_in = shuffled(tokens).astype(f32)
-    gain_in, gain_ff = shuffled(norm_in), shuffled(norm_ff)
-    normed_in, pull_norm_in = jax.vjp(rms_scale, flat_in, gain_in)
-    h_in = gather_rows(normed_in.astype(bf16), "seq").reshape(-1, D)
-    proj = mm(h_in, mix_w).reshape(everyone + (conv_cols + LANES,))
-    mixed, states, invs, deltas = mixer_forward(proj, slots, resets, conv_l, aux)
+    proj = mm(h_in, mix_w).reshape(blocks + (conv_cols,))
+    small = mm(h_in, small_w).reshape(blocks + (LANES,))
+    proj, out_w, moved_rest, own_down = lax.optimization_barrier((proj, out_w, moved_rest, own_down))
+    gu_rest = stacked(moved_rest)
+    down_w = lax.all_gather(own_down, "batch", axis=0, tiled=True)
+    mixed, states, invs, deltas = mixer_forward(proj, small, slots, resets, conv_l, aux)
+    mixed = mixed.reshape(-1, val_w)
     gate = mm(h_in, gate_w)
-    heads_out, pull_head = jax.vjp(head_norms, mixed.reshape(-1, val_w), gate, norm_head)
-    z_rows = heads_out.astype(bf16)
-    residual = flat_in + scatter_rows(mm(z_rows, out_w).astype(bf16).reshape(everyone + (D,)), "seq")
-
-    normed_ff, pull_norm_ff = jax.vjp(rms_scale, residual, gain_ff)
-    h_ff = gather_rows(normed_ff.astype(bf16), "seq").reshape(-1, D)
-    d_own = shuffled(grad_out)
-    d_out = gather_rows(d_own, "seq").reshape(-1, D)
+    z_rows = gated_norm(mixed, gate, norm_head)
+
+    def parts(product, left):
+        send = product(left[half:]).astype(bf16).reshape(halves + (D,))
+        return product(left[:half]).astype(bf16).reshape(halves + (D,)), send
+
+    keep, send = parts(lambda rows: mm(rows, out_w), z_rows)
+    keep, send, d_out = after((keep, send, d_out), gu_first)
+    residual, normed_ff = add_and_norm(
+        scatter_rows(keep, send, "seq"), after(own_in, gu_rest), gain_ff
+    )
+
+    h_halves = gather_rows(normed_ff, "seq", False)
+    gu_w = jnp.concatenate([gu_first, gu_rest], axis=1)
+    h_ff = joined(h_halves)
     gate_up = mm(h_ff, gu_w)
     hidden_full, pull_glu = jax.vjp(glu_hidden, gate_up[:, :ff], gate_up[:, ff:])
-    hidden = hidden_full.astype(bf16)
-    block_out = residual + scatter_rows(mm(hidden, down_w).astype(bf16).reshape(everyone + (D,)), "seq")
+    hidden = after(hidden_full.astype(bf16), down_w)
     down_grad = contract_rows(d_out, hidden).astype(bf16)
     down_own = summed(down_grad)
     d_hidden = contract_cols(after(d_out, down_grad), down_w)
     d_gate_up = jnp.concatenate(pull_glu(d_hidden), axis=1).astype(bf16)
-    d_h_ff = scatter_rows(contract_cols(d_gate_up, gu_w).astype(bf16).reshape(everyone + (D,)), "seq")
-    gu_grad = contract_rows(h_ff, d_gate_up).astype(bf16)
+    keep, send = parts(lambda rows: contract_cols(rows, gu_w), d_gate_up)
+    terms = scatter_rows(keep, send, "seq", False)
+    gu_grad = contract_rows(after(h_ff, keep, send), d_gate_up).astype(bf16)
     gu_own = summed(gu_grad)
-    d_resid_norm, g_norm_ff = pull_norm_ff(d_h_ff)
-    d_residual = d_own.astype(f32) + d_resid_norm
-
-    d_branch = gather_rows(after(d_residual.astype(bf16), gu_grad, down_own), "seq").reshape(-1, D)
+    out_parts = parts(lambda rows: mm(rows, down_w), after(hidden, keep, send))
+    d_residual, d_branch, g_norm_ff = norm_back(terms, residual, d_own.reshape(-1, D), gain_ff, f32)
+
+    d_branch = joined(gather_rows(after(d_branch, gu_grad, down_own, out_parts), "seq"))
     d_heads = contract_cols(d_branch, out_w)
-    d_mixed, d_gate, g_norm_head = pull_head(d_heads)
-    d_gate = d_gate.astype(bf16)
+    d_mixed, d_gate, g_norm_head = gated_norm_back(mixed, gate, norm_head, d_heads)
     out_grad = jnp.concatenate(
         [contract_rows(h_in, d_gate).astype(bf16), contract_rows(d_branch, z_rows).astype(bf16)], axis=1
     )
     d_mixed = after(d_mixed, out_grad)
-    d_proj, g_conv_l, g_decay = mixer_backward(
-        proj, d_mixed.reshape(everyone + (val_w,)), slots, resets, conv_l, aux, states, invs, deltas
-    )
-    d_proj, gu_own = lax.optimization_barrier((d_proj.reshape(-1, conv_cols + LANES), gu_own))
+    d_proj, d_small, g_conv_l, g_decay = mixer_backward(
+        proj, small, d_mixed.reshape(blocks + (val_w,)), slots, resets, conv_l, aux, states, invs, deltas
+    )
+    d_proj, gu_own = lax.optimization_barrier((d_proj.reshape(-1, conv_cols), gu_own))
+    d_small = d_small.reshape(-1, LANES)
     out_own = summed(out_grad)
     mix_grad = contract_rows(h_in, d_proj).astype(bf16)
-    mix_own = summed(after(mix_grad, out_own))
-    d_proj = after(d_proj, mix_grad)
-    down_grads = exchanged(down_own)
-    gu_grads = exchanged(gu_own)
-    out_grads = exchanged(out_own)
-    mix_grads = exchanged(mix_own)
-    d_h_in = scatter_rows(
-        (contract_cols(d_proj, mix_w) + contract_cols(d_gate, gate_w)).astype(bf16).reshape(everyone + (D,)), "seq"
-    )
-    d_flat, g_norm_in = pull_norm_in(d_h_in)
-    d_tokens = restored((d_residual + d_flat).astype(bf16))
-
-    local = jnp.concatenate([g_conv_l[:TAPS].reshape(-1), g_decay[:2, heads : 2 * heads].reshape(-1)])
-    shared = gather_rows(sum_all(local, ("batch",))[None], "seq")[0][slots]
+    mix_own = summed(mix_grad)
+    d_proj, d_small, g_conv_l, gu_own, out_parts = after((d_proj, d_small, g_conv_l, gu_own, out_parts), mix_grad)
+    ff_grads = exchanged(jnp.concatenate([gu_own, down_own], axis=-1))
+    keep, send = parts(
+        lambda rows: contract_cols(rows[:, :conv_cols], mix_w)
+        + contract_cols(rows[:, conv_cols : conv_cols + val_w], gate_w)
+        + contract_cols(rows[:, conv_cols + val_w :], small_w),
+        jnp.concatenate([d_proj, d_gate, d_small], axis=1),
+    )
+    d_tokens, g_norm_in = norm_back(
+        scatter_rows(keep, send, "seq", earlier=(ff_grads, out_own)), own_in, d_residual, gain_in, bf16, (size, groups)
+    )
+    block_out = add_in_order(scatter_rows(*after(out_parts, keep, send), "seq", False), residual, (size, groups))
+
+    small_grad = contract_rows(d_small, h_in)[: 2 * heads]
+    local = jnp.concatenate(
+        [g_conv_l[:TAPS].reshape(-1), g_decay[:2, heads : 2 * heads].reshape(-1), small_grad.reshape(-1)]
+    )
+    shared = gather_small(sum_all(local, ("batch",)), "seq")
     g_conv_all = shared[:, : TAPS * conv_cols].reshape(size, TAPS, conv_cols).transpose(1, 0, 2)
     g_conv = jnp.concatenate(
         [
@@ -649,34 +909,34 @@
         axis=1,
     )
     g_alog = shared[:, TAPS * conv_cols : TAPS * conv_cols + heads].reshape(H)
-    g_dt = shared[:, TAPS * conv_cols + heads :].reshape(H)
-    gains = sum_all(jnp.concatenate([g_norm_in, g_norm_ff, g_norm_head]), ("seq", "batch"))
-
-    def columns_of(grads, first, width):
-        return grads[:, :, first : first + width].astype(f32).transpose(1, 0, 2).reshape(own_rows, size * width)
-
-    g_proj = jnp.concatenate(
-        [
-            columns_of(mix_grads, 0, key_w),
-            columns_of(mix_grads, key_w, key_w),
-            columns_of(mix_grads, 2 * key_w, val_w),
-            columns_of(out_grads, 0, val_w),
-        ],
-        axis=1,
-    )
-    g_small = jnp.concatenate(
-        [columns_of(mix_grads, conv_cols, heads), columns_of(mix_grads, conv_cols + heads, heads)], axis=1
-    )
+    g_dt = shared[:, TAPS * conv_cols + heads : TAPS * conv_cols + 2 * heads].reshape(H)
+    g_small = lax.dynamic_slice_in_dim(
+        shared[:, TAPS * conv_cols + 2 * heads :].reshape(size, 2, heads, D),
+        (lax.axis_index("batch") * size + me) * own_rows,
+        own_rows,
+        3,
+    )
+    g_small = g_small.transpose(3, 1, 0, 2).reshape(own_rows, 2 * H)
+    gains = sum_all(jnp.concatenate([g_norm_in[0], g_norm_ff[0], g_norm_head[0]]), ("seq", "batch"))
+
+    out_grads = exchanged(out_own)
+    mix_own, d_tokens, block_out, out_grads = lax.optimization_barrier((mix_own, d_tokens, block_out, out_grads))
+    g_gu = laid_out([ff_grads], [(0, 0, ff, 0), (0, ff, ff, FF)], 2 * FF)
+    g_down = ff_grads[:, :, 2 * ff :].astype(f32).transpose(0, 2, 1).reshape(FF, own_rows)
     g_out = out_grads[:, :, val_w:].astype(f32).transpose(0, 2, 1).reshape(VW, own_rows)
-    g_gu = gu_grads.astype(f32).reshape(size, own_rows, 2, ff).transpose(1, 2, 0, 3)
-    g_down = down_grads.astype(f32).transpose(0, 2, 1).reshape(FF, own_rows)
+    mix_grads = exchanged(mix_own)
+    g_proj = laid_out(
+        [mix_grads, out_grads],
+        [(0, 0, key_w, 0), (0, key_w, key_w, KW), (0, 2 * key_w, val_w, 2 * KW), (1, 0, val_w, CW)],
+        CW + VW,
+    )
     return (
-        restored(block_out.astype(bf16)),
-        d_tokens,
+        block_out.reshape(tokens.shape),
+        d_tokens.reshape(tokens.shape),
         g_proj,
         g_small,
         g_out,
-        g_gu.reshape(own_rows, 2 * FF),
+        g_gu,
         g_down,
         restored(gains[:D]),
         restored(gains[D : 2 * D]),

time: 807 us -> 757 us (0.938)
  local copies, waits for them, and re-layouts: 193 us -> 78.2 us
  waiting for transfers between devices: 208 us -> 250 us
  Pallas kernels: 133 us -> 169 us
  other arithmetic: 69.9 us -> 39.3 us
  matrix products: 92.6 us -> 117 us
    unnamed x220 -> x191, local copies, waits for them, and re-layouts: 81.7 us -> 20.9 us
    ppermute x58 -> x55, waiting for transfers between devices: 117 us -> 172 us  [swap(): lax.ppermute(value, axis, [(i, i ^ bit) for i in range(lax.axis_size(axis...]
    pallas_call x0 -> x8, Pallas kernels: none -> 31.3 us  [the longest x6 21.1 us: local_call(): pl.pallas_call(body, grid=(1,), in_specs=specs, out_specs=whole_specs(out...]
    reshape x12 -> x4, local copies, waits for them, and re-layouts: 19.2 us -> 3.45 us  [the longest x2 2.59 us: shards(): ff_grads[:, :, 2 * ff:].astype(f32).transpose(0, 2, 1).reshape(FF, own_rows)]
    dot_general x5 -> x10, matrix products: 30.5 us -> 44.7 us  [contract_cols(): lax.dot_general(left, right, (((1,), (1,)), ((), ())), preferred_element_...]
    another operation x14 -> x7, local copies, waits for them, and re-layouts: 19.4 us -> 6.01 us  [the longest x4 3.85 us: gather_rows(): zip(rows, routes(axis) * rows.shape[0])]
    all_gather x3 -> x4, waiting for transfers between devices: 42 us -> 29.1 us  [stacked(): full = lax.all_gather(blocks, 'batch', axis=0, tiled=False)]
    another operation x9 -> x0, other arithmetic: 11.9 us -> none
  transfers between devices with their start and end apart: 74 -> 71, of which waited for: 28 -> 38; matrix products, arithmetic and copies ran while one was open for 39% -> 28% of each run, Pallas kernels for 17% -> 22%
where the time goes in v2:
time: 757 us; the launch traced here: 751 us
  waiting for transfers between devices  250 us (33%)
  Pallas kernels  169 us (22%)
  matrix products  117 us (15%)
  starting transfers between devices  82 us (11%)
  local copies, waits for them, and re-layouts  78.2 us (10%)
  other arithmetic  39.3 us (5%)
  between operations  15.8 us (2%)
    ppermute x55, waiting for transfers between devices, swap(): lax.ppermute(value, axis, [(i, i ^ bit) for i in range(lax.axis_size(axis...  172 us
    pallas_call x1, Pallas kernels, mixer_forward(): pl.pallas_call(partial(forward_kernel, heads), grid_spec=pltpu.PrefetchSc...  75.6 us
    pallas_call x1, Pallas kernels, mixer_backward(): pl.pallas_call(partial(backward_kernel, heads, chunks), grid_spec=pltpu.P...  62.2 us
    ppermute x55, starting transfers between devices, swap(): lax.ppermute(value, axis, [(i, i ^ bit) for i in range(lax.axis_size(axis...  56.9 us
    dot_general x10, matrix products, contract_cols(): lax.dot_general(left, right, (((1,), (1,)), ((), ())), preferred_element_...  44.7 us
    dot_general x8, matrix products, mm(): return jnp.dot(left, right, preferred_element_type=f32)  38.8 us
    dot_general x6, matrix products, contract_rows(): lax.dot_general(left, right, (((0,), (0,)), ((), ())), preferred_element_...  33.6 us
    all_gather x4, waiting for transfers between devices, stacked(): full = lax.all_gather(blocks, 'batch', axis=0, tiled=False)  29.1 us
  transfers between devices with their start and end apart: 71, of which 38 were waited for; matrix products, arithmetic and copies ran while one was open for 28% of the time, Pallas kernels for 22%

profile of v2, /device:TPU:0, one launch (start us, length us, event | category | flops | bytes accessed | tf_op | source)
XLA Modules:
  0.0 750.9 jit_solution(1142877091106448625)
XLA Ops:
  26.9 9.4 %collective-permute-done.1 = bf16[2,64,2048]{2,1,0:T(8,128)(2,1)S(1)} collective-permute-done((bf16[2,64,2048]{2,1,0:T(8,128)(2,1)S(1)}, bf16[2,64,2048]{2,1,0:T(8,128)(2,1)S(1)}, u32[]{:S(2)}, u32[]{:S(2)}) %collective-permute-start.1) | collective-permute-done | bytes 524320 | tf_op jit(solution)/shard_map/ppermute | solution.py:619
  49.7 11.0 %all-to-all-done = bf16[8,64,1024]{2,1,0:T(8,128)(2,1)S(1)} async-done(((bf16[8,64,1024]{2,1,0:T(8,128)(2,1)}), bf16[8,64,1024]{2,1,0:T(8,128)(2,1)S(1)}, u32[]{:S(2)}, u32[]{:S(2)}) %all-to-all-start) | async-done | bytes 1048608 | tf_op jit(solution)/shard_map/all_to_all | solution.py:718
  92.5 10.7 %collective-permute-done.7 = bf16[4,64,32]{1,2,0:T(8,128)(2,1)S(1)} collective-permute-done((bf16[4,64,32]{1,2,0:T(8,128)(2,1)S(1)}, bf16[4,64,32]{1,2,0:T(8,128)(2,1)S(1)}, u32[]{:S(2)}, u32[]{:S(2)}) %collective-permute-start.7) | collective-permute-done | bytes 16416 | tf_op jit(solution)/shard_map/ppermute | solution.py:619
  106.4 7.6 %collective-permute-done.11 = bf16[2,64,2048]{2,1,0:T(8,128)(2,1)} collective-permute-done((bf16[2,64,2048]{2,1,0:T(8,128)(2,1)}, bf16[2,64,2048]{2,1,0:T(8,128)(2,1)}, u32[]{:S(2)}, u32[]{:S(2)}) %collective-permute-start.11) | collective-permute-done | bytes 524320 | tf_op jit(solution)/shard_map/ppermute | solution.py:619
  124.6 17.2 %collective-permute-done.9 = bf16[2,8,64,32]{2,3,1,0:T(8,128)(2,1)S(1)} collective-permute-done((bf16[2,8,64,32]{2,3,1,0:T(8,128)(2,1)S(1)}, bf16[2,8,64,32]{2,3,1,0:T(8,128)(2,1)S(1)}, u32[]{:S(2)}, u32[]{:S(2)}) %collective-permute-start.9) | collective-permute-done | bytes 65568 | tf_op jit(solution)/shard_map/ppermute | solution.py:619
  143.0 7.5 all-gather.15.cloned.1.call-done
  163.5 10.0 %fusion.63 = f32[1024,1024]{1,0:T(8,128)} fusion(bf16[1024,2048]{1,0:T(8,128)(2,1)} %pad_maximum_fusion.1, bf16[2048,1024]{1,0:T(8,128)(2,1)} %bitcast.381), kind=kOutput, calls=%fused_computation.207 | convolution fusion | flops 4294967296 | bytes 12582912 | tf_op jit(solution)/shard_map/dot_general | solution.py:698
  175.7 75.6 %delta_forward.1 = (f32[2,2,4,64,512]{4,3,2,1,0:T(8,128)}, f32[8,4,128,256]{3,2,1,0:T(8,128)}, f32[8,4,64,64]{3,2,1,0:T(8,128)}, f32[8,4,64,256]{3,2,1,0:T(8,128)}) custom-call(s32[8]{0:T(128)} %iota_xor_fusion.pos_ref, s32[2]{0:T(128)} %reset_ref.3, f32[2,2,4,64,1024]{4,3,2,1,0:T(8,128)} %bitcast.396, f32[2,2,4,64,128]{4,3,2,1,0:T(8,128)} %bitcast.342, ...), custom_call_target="tpu_custom_call" | custom-call | flops 60000002048 | bytes 40000000 | tf_op jit(solution)/shard_map/delta_forward/pallas_call | solution.py:336
  251.3 6.6 fusion.65.gate_ref
  267.4 11.4 %all-gather.19.cloned.1.call-done = bf16[32,64,1024]{2,1,0:T(8,128)(2,1)} async-done(((bf16[8,64,1024]{2,1,0:T(8,128)(2,1)}), bf16[32,64,1024]{2,1,0:T(8,128)(2,1)}) %all-gather.19.cloned.1.call-update) | async-done | bytes 4194320 | tf_op jit(solution)/shard_map/all_gather | solution.py:722
  289.0 10.8 %collective-permute-done.16.refs_2_ = bf16[2,64,2048]{2,1,0:T(8,128)(2,1)S(1)} collective-permute-done((bf16[2,64,2048]{2,1,0:T(8,128)(2,1)S(1)}, bf16[2,64,2048]{2,1,0:T(8,128)(2,1)S(1)}, u32[]{:S(2)}, u32[]{:S(2)}) %collective-permute-start.16) | collective-permute-done | bytes 524320 | tf_op jit(solution)/shard_map/ppermute | solution.py:619
  305.6 10.2 %all-gather.21.cloned.1.call-done = bf16[32,64,384]{2,1,0:T(8,128)(2,1)} async-done(((bf16[8,64,384]{2,1,0:T(8,128)(2,1)}), bf16[32,64,384]{2,1,0:T(8,128)(2,1)}) %all-gather.21.cloned.1.call-update) | async-done | bytes 1572880 | tf_op jit(solution)/shard_map/all_gather | solution.py:722
  324.0 5.0 collective-permute-done.20
  336.8 6.2 collective-permute-done.21
  351.1 8.8 %fusion.5 = f32[1024,1408]{1,0:T(8,128)S(1)} fusion(bf16[2048,384]{1,0:T(8,128)(2,1)} %bitcast.392, bf16[2048,1024]{1,0:T(8,128)(2,1)S(1)} %bitcast.384, bf16[512,2048]{1,0:T(8,128)(2,1)S(1)} %bitcast.325, bf16[512,2048]{1,0:T(8,128)(2,1)S(1)} %bitcast.312), kind=kOutput, calls=%fused_computation.38 | convolution fusion | flops 5925502976 | bytes 15728640 | tf_op jit(solution)/shard_map/dot_general | solution.py:698
  364.7 25.4 %all-gather.13.cloned.1.call-done = bf16[704,2048]{1,0:T(8,128)(2,1)} async-done(((bf16[176,2048]{1,0:T(8,128)(2,1)}), bf16[704,2048]{1,0:T(8,128)(2,1)}) %all-gather.13.cloned.1.call-update) | async-done | bytes 2883600 | tf_op jit(solution)/shard_map/all_gather | solution.py:836
  390.1 7.5 convolution_convert_fusion.2
  401.6 7.0 multiply_convert_fusion
  416.9 8.8 %convolution_convert_fusion = bf16[2048,1408]{1,0:T(8,128)(2,1)} fusion(bf16[1024,2048]{1,0:T(8,128)(2,1)S(1)} %pad_maximum_fusion.3, bf16[1024,704]{1,0:T(8,128)(2,1)S(1)} %get-tuple-element.127, bf16[1024,704]{1,0:T(8,128)(2,1)S(1)} %get-tuple-element.128), kind=kOutput, calls=%fused_computation.3 | convolution fusion | flops 5914230784 | bytes 12845056 | tf_op jit(solution)/shard_map/dot_general | solution.py:702
  437.0 7.8 %collective-permute-done.28.refs_4_ = bf16[2,64,2048]{2,1,0:T(8,128)(2,1)S(1)} collective-permute-done((bf16[2,64,2048]{2,1,0:T(8,128)(2,1)S(1)}, bf16[2,64,2048]{2,1,0:T(8,128)(2,1)S(1)}, u32[]{:S(2)}, u32[]{:S(2)}) %collective-permute-start.28) | collective-permute-done | bytes 524320 | tf_op jit(solution)/shard_map/ppermute | solution.py:619
  463.3 5.4 collective-permute-done.30
  472.5 7.9 %collective-permute-done.31 = bf16[2,64,2048]{2,1,0:T(8,128)(2,1)S(1)} collective-permute-done((bf16[2,64,2048]{2,1,0:T(8,128)(2,1)S(1)}, bf16[2,64,2048]{2,1,0:T(8,128)(2,1)S(1)}, u32[]{:S(2)}, u32[]{:S(2)}) %collective-permute-start.31) | collective-permute-done | bytes 524320 | tf_op jit(solution)/shard_map/ppermute | solution.py:619
  488.5 5.9 gated_norm_back.1
  502.1 62.2 %delta_backward.1 = (bf16[2,2,4,64,1024]{4,3,2,1,0:T(8,128)(2,1)}, bf16[2,2,4,64,128]{4,3,2,1,0:T(8,128)(2,1)}, f32[8,1024]{1,0:T(8,128)}, f32[8,128]{1,0:T(8,128)}) custom-call(s32[8]{0:T(128)} %iota_xor_fusion.pos_ref, s32[2]{0:T(128)} %reset_ref.3, f32[2,2,4,64,1024]{4,3,2,1,0:T(8,128)} %bitcast.397, f32[2,2,4,64,128]{4,3,2,1,0:T(8,128)} %bitcast.343, ...), custom_call_target="tpu_custom_call" | custom-call | flops 60000002048 | bytes 40000000 | tf_op jit(solution)/shard_map/delta_backward/pallas_call | solution.py:370
  572.9 9.6 %convolution_convert_fusion.1 = bf16[2048,1024]{1,0:T(8,128)(2,1)} fusion(bf16[1024,2048]{1,0:T(8,128)(2,1)} %pad_maximum_fusion.1, bf16[1024,1024]{1,0:T(8,128)(2,1)} %bitcast.399), kind=kOutput, calls=%fused_computation.13 | convolution fusion | flops 4297064448 | bytes 10485760 | tf_op jit(solution)/shard_map/dot_general | solution.py:702
  585.6 7.0 fusion.15
  605.9 5.7 add_convert_fusion
  614.5 19.4 %collective-permute-done.48 = f32[2,12292]{1,0:T(2,128)S(1)} collective-permute-done((f32[2,12292]{1,0:T(2,128)S(1)}, f32[2,12292]{1,0:T(2,128)S(1)}, u32[]{:S(2)}, u32[]{:S(2)}) %collective-permute-start.48) | collective-permute-done | bytes 98368 | tf_op jit(solution)/shard_map/ppermute | solution.py:619
  656.8 8.0 %collective-permute-done.36.refs_2_ = bf16[2,64,2048]{2,1,0:T(8,128)(2,1)S(1)} collective-permute-done((bf16[2,64,2048]{2,1,0:T(8,128)(2,1)S(1)}, bf16[2,64,2048]{2,1,0:T(8,128)(2,1)S(1)}, u32[]{:S(2)}, u32[]{:S(2)}) %collective-permute-start.36) | collective-permute-done | bytes 524320 | tf_op jit(solution)/shard_map/ppermute | solution.py:619
  668.9 11.8 %collective-permute-done.37 = bf16[64,2048]{1,0:T(8,128)(2,1)S(1)} collective-permute-done((bf16[64,2048]{1,0:T(8,128)(2,1)S(1)}, bf16[64,2048]{1,0:T(8,128)(2,1)S(1)}, u32[]{:S(2)}, u32[]{:S(2)}) %collective-permute-start.37) | collective-permute-done | bytes 262176 | tf_op jit(solution)/shard_map/ppermute | solution.py:619
  701.3 7.1 collective-permute-done.51
  710.0 8.5 %reduce-scatter.9.cloned.1.call-done = bf16[512,1024]{1,0:T(8,128)(2,1)} async-done(((bf16[2048,1024]{1,0:T(8,128)(2,1)}), bf16[512,1024]{1,0:T(8,128)(2,1)}) %reduce-scatter.9.cloned.1.call-update) | async-done | bytes 1048592 | tf_op jit(solution)/shard_map/reduce_scatter | solution.py:727
  (477 shorter events, 312.1 us)
Async XLA Ops:
  7.2 56.6 %all-gather.11.cloned.1.call-start = ((), (), s32[]{:S(2)}) async-start(), calls=%async_computation.10 | async-start | bytes 2621440 | tf_op jit(solution)/shard_map/all_gather | solution.py:769
  41.8 18.9 %all-to-all-start = ((bf16[8,64,1024]{2,1,0:T(8,128)(2,1)}), bf16[8,64,1024]{2,1,0:T(8,128)(2,1)S(1)}, u32[]{:S(2)}, u32[]{:S(2)}) async-start(bf16[8,64,1024]{2,1,0:T(8,128)(2,1)} %copy.114), calls=%async_computation | async-start | bytes 2097152 | tf_op jit(solution)/shard_map/all_to_all | solution.py:718
  45.4 105.1 %all-gather.15.cloned.1.call-start = ((), (), s32[]{:S(2)}) async-start(), calls=%async_computation.16 | async-start | bytes 5242880 | tf_op jit(solution)/shard_map/all_gather | solution.py:722
  83.7 32.9 %all-to-all-start.1 = ((bf16[8,64,512]{2,1,0:T(8,128)(2,1)}), bf16[8,64,512]{2,1,0:T(8,128)(2,1)S(1)}, u32[]{:S(2)}, u32[]{:S(2)}) async-start(bf16[8,64,512]{2,1,0:T(8,128)(2,1)} %copy.115), calls=%async_computation.1 | async-start | bytes 1048576 | tf_op jit(solution)/shard_map/all_to_all | solution.py:718
  87.5 16.3 %collective-permute-start.12 = (bf16[1,64,2048]{2,1,0:T(8,128)(2,1)S(1)}, bf16[1,64,2048]{2,1,0:T(8,128)(2,1)S(1)}, u32[]{:S(2)}, u32[]{:S(2)}) collective-permute-start(bf16[1,64,2048]{2,1,0:T(8,128)(2,1)S(1)} %get-tuple-element.149), channel_id=1, source_target_pairs={{0,16},{4,20},{8,24},{12,28},{16,0},{20,4},{24,8},{28,12},{1,17},{... | collective-permute-start | bytes 786440 | tf_op jit(solution)/shard_map/ppermute | solution.py:619
  91.1 22.9 %collective-permute-start.11 = (bf16[2,64,2048]{2,1,0:T(8,128)(2,1)}, bf16[2,64,2048]{2,1,0:T(8,128)(2,1)}, u32[]{:S(2)}, u32[]{:S(2)}) collective-permute-start(bf16[2,64,2048]{2,1,0:T(8,128)(2,1)} %pad_maximum_fusion.16), channel_id=1, source_target_pairs={{0,16},{4,20},{8,24},{12,28},{16,0},{20,4},{24,8},{28,12},{1,17},{... | collective-permute-start | bytes 1572872 | tf_op jit(solution)/shard_map/ppermute | solution.py:619
  103.7 20.3 %collective-permute-start.8 = (bf16[1,8,64,32]{2,3,1,0:T(8,128)(2,1)S(1)}, bf16[1,8,64,32]{2,3,1,0:T(8,128)(2,1)S(1)}, u32[]{:S(2)}, u32[]{:S(2)}) collective-permute-start(bf16[1,8,64,32]{2,3,1,0:T(8,128)(2,1)S(1)} %bitcast.337), channel_id=1, source_target_pairs={{0,1},{1,0},{2,3},{3,2},{4,5},{5,4},{6,7},{7,6},{8,9},{9,8},{10,11... | collective-permute-start | bytes 98312 | tf_op jit(solution)/shard_map/ppermute | solution.py:619
  104.7 17.1 %collective-permute-start.13 = (bf16[2,64,2048]{2,1,0:T(8,128)(2,1)}, bf16[2,64,2048]{2,1,0:T(8,128)(2,1)}, u32[]{:S(2)}, u32[]{:S(2)}) collective-permute-start(bf16[2,64,2048]{2,1,0:T(8,128)(2,1)} %pad_maximum_fusion.17), channel_id=1, source_target_pairs={{0,8},{4,12},{8,0},{12,4},{16,24},{20,28},{24,16},{28,20},{1,9},{5... | collective-permute-start | bytes 1572872 | tf_op jit(solution)/shard_map/ppermute | solution.py:619
  117.4 25.6 %all-to-all-start.2 = ((bf16[8,64,1408]{2,1,0:T(8,128)(2,1)}), bf16[8,64,1408]{2,1,0:T(8,128)(2,1)S(1)}, u32[]{:S(2)}, u32[]{:S(2)}) async-start(bf16[8,64,1408]{2,1,0:T(8,128)(2,1)} %reshape.474), calls=%async_computation.2 | async-start | bytes 2883584 | tf_op jit(solution)/shard_map/all_to_all | solution.py:718
  121.0 130.3 %all-gather.17.cloned.1.call-start = ((), (), s32[]{:S(2)}) async-start(), calls=%async_computation.17 | async-start | bytes 2621440 | tf_op jit(solution)/shard_map/all_gather | solution.py:722
  123.6 33.7 %collective-permute-start.14 = (bf16[2,4,64,2048]{3,2,1,0:T(8,128)(2,1)}, bf16[2,4,64,2048]{3,2,1,0:T(8,128)(2,1)}, u32[]{:S(2)}, u32[]{:S(2)}) collective-permute-start(bf16[2,4,64,2048]{3,2,1,0:T(8,128)(2,1)} %bitcast.309), channel_id=1, source_target_pairs={{0,4},{4,0},{8,12},{12,8},{16,20},{20,16},{24,28},{28,24},{1,5},{5... | collective-permute-start | bytes 6291464 | tf_op jit(solution)/shard_map/ppermute | solution.py:619
  124.0 17.8 %collective-permute-start.9 = (bf16[2,8,64,32]{2,3,1,0:T(8,128)(2,1)S(1)}, bf16[2,8,64,32]{2,3,1,0:T(8,128)(2,1)S(1)}, u32[]{:S(2)}, u32[]{:S(2)}) collective-permute-start(bf16[2,8,64,32]{2,3,1,0:T(8,128)(2,1)S(1)} %pad_maximum_fusion.25), channel_id=1, source_target_pairs={{0,2},{1,3},{2,0},{3,1},{4,6},{5,7},{6,4},{7,5},{8,10},{9,11},{10,... | collective-permute-start | bytes 196616 | tf_op jit(solution)/shard_map/ppermute | solution.py:619
  150.5 128.3 %all-gather.19.cloned.1.call-start = ((), (), s32[]{:S(2)}) async-start(), calls=%async_computation.18 | async-start | bytes 5242880 | tf_op jit(solution)/shard_map/all_gather | solution.py:722
  175.7 140.2 %all-gather.21.cloned.1.call-start = ((), (), s32[]{:S(2)}) async-start(), calls=%async_computation.19 | async-start | bytes 1966080 | tf_op jit(solution)/shard_map/all_gather | solution.py:722
  278.8 111.3 %all-gather.13.cloned.1.call-start = ((), (), s32[]{:S(2)}) async-start(), calls=%async_computation.11 | async-start | bytes 3604480 | tf_op jit(solution)/shard_map/all_gather | solution.py:836
  287.5 15.1 %collective-permute-start.18 = (bf16[2,64,2048]{2,1,0:T(8,128)(2,1)S(1)}, bf16[2,64,2048]{2,1,0:T(8,128)(2,1)S(1)}, u32[]{:S(2)}, u32[]{:S(2)}) collective-permute-start(bf16[2,64,2048]{2,1,0:T(8,128)(2,1)S(1)} %fusion.22), channel_id=1, source_target_pairs={{0,8},{4,12},{8,0},{12,4},{16,24},{20,28},{24,16},{28,20},{1,9},{5... | collective-permute-start | bytes 1572872 | tf_op jit(solution)/shard_map/ppermute | solution.py:619
  301.0 14.9 %collective-permute-start.17 = (bf16[64,2048]{1,0:T(8,128)(2,1)S(1)}, bf16[64,2048]{1,0:T(8,128)(2,1)S(1)}, u32[]{:S(2)}, u32[]{:S(2)}) collective-permute-start(bf16[64,2048]{1,0:T(8,128)(2,1)S(1)} %fusion.36), channel_id=1, source_target_pairs={{0,8},{4,12},{8,0},{12,4},{16,24},{20,28},{24,16},{28,20},{1,9},{5... | collective-permute-start | bytes 786440 | tf_op jit(solution)/shard_map/ppermute | solution.py:619
  332.6 127.0 %reduce-scatter.5.cloned.1.call-start = ((), (), s32[]{:S(2)}) async-start(), calls=%async_computation.12 | async-start | bytes 3604480 | tf_op jit(solution)/shard_map/reduce_scatter | solution.py:727
  397.6 175.3 %reduce-scatter.7.cloned.1.call-start = ((), (), s32[]{:S(2)}) async-start(), calls=%async_computation.13 | async-start | bytes 7208960 | tf_op jit(solution)/shard_map/reduce_scatter | solution.py:727
  425.6 218.9 %reduce-scatter.11.cloned.1.call-start = ((), (), s32[]{:S(2)}) async-start(), calls=%async_computation.15 | async-start | bytes 5242880 | tf_op jit(solution)/shard_map/reduce_scatter | solution.py:727
  502.0 216.5 %reduce-scatter.9.cloned.1.call-start = ((), (), s32[]{:S(2)}) async-start(), calls=%async_computation.14 | async-start | bytes 5242880 | tf_op jit(solution)/shard_map/reduce_scatter | solution.py:727
  600.1 46.8 %all-to-all-start.3 = ((bf16[8,64,2112]{2,1,0:T(8,128)(2,1)}), bf16[8,64,2112]{2,1,0:T(8,128)(2,1)}, u32[]{:S(2)}, u32[]{:S(2)}) async-start(bf16[8,64,2112]{2,1,0:T(8,128)(2,1)} %pad_maximum_fusion.10), calls=%async_computation.6 | async-start | bytes 4456448 | tf_op jit(solution)/shard_map/all_to_all | solution.py:718
  611.7 35.2 %collective-permute-start.35 = (bf16[2,4,64,2048]{3,2,1,0:T(8,128)(2,1)}, bf16[2,4,64,2048]{3,2,1,0:T(8,128)(2,1)}, u32[]{:S(2)}, u32[]{:S(2)}) collective-permute-start(bf16[2,4,64,2048]{3,2,1,0:T(8,128)(2,1)} %bitcast.75), channel_id=1, source_target_pairs={{0,4},{4,0},{8,12},{12,8},{16,20},{20,16},{24,28},{28,24},{1,5},{5... | collective-permute-start | bytes 6291464 | tf_op jit(solution)/shard_map/ppermute | solution.py:619
  612.2 21.8 %collective-permute-start.48 = (f32[2,12292]{1,0:T(2,128)S(1)}, f32[2,12292]{1,0:T(2,128)S(1)}, u32[]{:S(2)}, u32[]{:S(2)}) collective-permute-start(f32[2,12292]{1,0:T(2,128)S(1)} %pad_maximum_fusion.27), channel_id=1, source_target_pairs={{0,8},{4,12},{8,0},{12,4},{16,24},{20,28},{24,16},{28,20},{1,9},{5... | collective-permute-start | bytes 295016 | tf_op jit(solution)/shard_map/ppermute | solution.py:619
  614.5 30.0 %collective-permute-start.40 = (bf16[2,4,64,2048]{3,2,1,0:T(8,128)(2,1)}, bf16[2,4,64,2048]{3,2,1,0:T(8,128)(2,1)}, u32[]{:S(2)}, u32[]{:S(2)}) collective-permute-start(bf16[2,4,64,2048]{3,2,1,0:T(8,128)(2,1)} %bitcast.65), channel_id=1, source_target_pairs={{0,4},{4,0},{8,12},{12,8},{16,20},{20,16},{24,28},{28,24},{1,5},{5... | collective-permute-start | bytes 6291464 | tf_op jit(solution)/shard_map/ppermute | solution.py:619
  649.9 14.9 %collective-permute-start.36 = (bf16[2,64,2048]{2,1,0:T(8,128)(2,1)S(1)}, bf16[2,64,2048]{2,1,0:T(8,128)(2,1)S(1)}, u32[]{:S(2)}, u32[]{:S(2)}) collective-permute-start(bf16[2,64,2048]{2,1,0:T(8,128)(2,1)S(1)} %fusion.12), channel_id=1, source_target_pairs={{0,16},{4,20},{8,24},{12,28},{16,0},{20,4},{24,8},{28,12},{1,17},{... | collective-permute-start | bytes 1572872 | tf_op jit(solution)/shard_map/ppermute | solution.py:619
  651.5 15.1 %collective-permute-start.38 = (bf16[2,64,2048]{2,1,0:T(8,128)(2,1)S(1)}, bf16[2,64,2048]{2,1,0:T(8,128)(2,1)S(1)}, u32[]{:S(2)}, u32[]{:S(2)}) collective-permute-start(bf16[2,64,2048]{2,1,0:T(8,128)(2,1)S(1)} %fusion.23), channel_id=1, source_target_pairs={{0,8},{4,12},{8,0},{12,4},{16,24},{20,28},{24,16},{28,20},{1,9},{5... | collective-permute-start | bytes 1572872 | tf_op jit(solution)/shard_map/ppermute | solution.py:619
  654.6 31.4 %collective-permute-start.43 = (bf16[2,64,2048]{2,1,0:T(8,128)(2,1)}, bf16[2,64,2048]{2,1,0:T(8,128)(2,1)S(1)}, u32[]{:S(2)}, u32[]{:S(2)}) collective-permute-start(bf16[2,64,2048]{2,1,0:T(8,128)(2,1)} %get-tuple-element.131), channel_id=1, source_target_pairs={{0,8},{4,12},{8,0},{12,4},{16,24},{20,28},{24,16},{28,20},{1,9},{5... | collective-permute-start | bytes 1572872 | tf_op jit(solution)/shard_map/ppermute | solution.py:619
  656.1 29.9 %collective-permute-start.41 = (bf16[2,64,2048]{2,1,0:T(8,128)(2,1)}, bf16[2,64,2048]{2,1,0:T(8,128)(2,1)S(1)}, u32[]{:S(2)}, u32[]{:S(2)}) collective-permute-start(bf16[2,64,2048]{2,1,0:T(8,128)(2,1)} %get-tuple-element.132), channel_id=1, source_target_pairs={{0,16},{4,20},{8,24},{12,28},{16,0},{20,4},{24,8},{28,12},{1,17},{... | collective-permute-start | bytes 1572872 | tf_op jit(solution)/shard_map/ppermute | solution.py:619
  689.0 21.0 %all-to-all-start.4 = ((bf16[8,64,1024]{2,1,0:T(8,128)(2,1)}), bf16[8,64,1024]{2,1,0:T(8,128)(2,1)S(1)}, u32[]{:S(2)}, u32[]{:S(2)}) async-start(bf16[8,64,1024]{2,1,0:T(8,128)(2,1)} %bitcast.76), calls=%async_computation.8 | async-start | bytes 2097152 | tf_op jit(solution)/shard_map/all_to_all | solution.py:718
  692.6 15.8 %collective-permute-start.51 = (f32[4352]{0:T(1024)S(1)}, f32[4352]{0:T(1024)S(1)}, u32[]{:S(2)}, u32[]{:S(2)}) collective-permute-start(f32[4352]{0:T(1024)S(1)} %fusion.54), channel_id=1, source_target_pairs={{0,8},{4,12},{8,0},{12,4},{16,24},{20,28},{24,16},{28,20},{1,9},{5... | collective-permute-start | bytes 52232 | tf_op jit(solution)/shard_map/ppermute | solution.py:619
  718.5 22.0 %all-to-all-start.5 = ((bf16[8,64,1024]{2,1,0:T(8,128)(2,1)}), bf16[8,64,1024]{2,1,0:T(8,128)(2,1)}, u32[]{:S(2)}, u32[]{:S(2)}) async-start(bf16[8,64,1024]{2,1,0:T(8,128)(2,1)} %bitcast.333), calls=%async_computation.9 | async-start | bytes 2097152 | tf_op jit(solution)/shard_map/all_to_all | solution.py:718
  (118 other events, 1178.8 us)
Sparse Core Ops, SparseCore 0:
  17.2 46.5 all-gather.10
  65.9 84.4 all-gather.14
  152.6 44.4 all-gather.16
  199.1 79.6 all-gather.18
  280.2 35.6 all-gather.20
  332.7 57.3 all-gather.12
  397.7 54.8 reduce-scatter.4
  454.9 102.1 reduce-scatter.6
  559.4 79.5 reduce-scatter.10
  641.2 77.1 reduce-scatter.8

commit v3 on v2

--- a/solution.py
+++ b/solution.py
@@ -25,7 +25,7 @@
 f32 = jnp.float32
 bf16 = jnp.bfloat16
 VMEM_BYTES = 56 * 1024 * 1024
-KERNEL_COST = pl.CostEstimate(flops=60_000_000_000, bytes_accessed=40_000_000, transcendentals=0)
+KERNEL_COST = pl.CostEstimate(flops=30_000_000_000, bytes_accessed=40_000_000, transcendentals=0)
 
 
 def dot_in(left, right, contract, precision):
@@ -39,11 +39,11 @@
 
 
 def fine(left, right, contract=(1, 0)):
-    return dot_in(left, right, contract, lax.Precision.HIGHEST)
+    return dot_in(left, right, contract, lax.Precision.HIGH)
 
 
 def coarse(left, right, contract=(1, 0)):
-    return dot_in(left, right, contract, lax.Precision.HIGHEST)
+    return dot_in(left, right, contract, lax.Precision.HIGH)
 
 
 def position_masks(reset, chunk):
@@ -83,19 +83,24 @@
     return fine(jnp.where(pick_row == pick_col, 1.0, 0.0), total, (1, 1))
 
 
-def inverse_unit_lower(strict_part):
-    rows = lax.broadcasted_iota(jnp.int32, (CH, CH), 0)
-    cols = lax.broadcasted_iota(jnp.int32, (CH, CH), 1)
+def inverses_unit_lower(parts):
+    size = parts[0].shape[0]
+    rows = lax.broadcasted_iota(jnp.int32, (size, size), 0)
+    cols = lax.broadcasted_iota(jnp.int32, (size, size), 1)
     eye = jnp.where(rows == cols, 1.0, 0.0)
-    diag = jnp.where(rows // 16 == cols // 16, strict_part, 0.0)
-    inv = eye - diag
-    power = diag
+    block = lambda n: jnp.where((rows & -n) == (cols & -n), 1.0, 0.0)
+    inside = {n: block(n) for n in (16, 32, 64)}
+    power = [part * inside[16] for part in parts]
+    inv = [eye - diag for diag in power]
     for _ in range(3):
-        power = fine(power, power)
-        inv = inv + fine(inv, power)
-    for size in (16, 32):
-        off = jnp.where((rows // size != cols // size) & (rows // (2 * size) == cols // (2 * size)), strict_part, 0.0)
-        inv = inv - fine(fine(inv, off), inv)
+        power = [fine(p, p) for p in power]
+        more = [fine(i, p) for i, p in zip(inv, power)]
+        inv = [i + m for i, m in zip(inv, more)]
+    for n in (16, 32):
+        ring = inside[2 * n] - inside[n]
+        left = [fine(i, part * ring) for i, part in zip(inv, parts)]
+        more = [fine(l, i) for l, i in zip(left, inv)]
+        inv = [i - m for i, m in zip(inv, more)]
     return inv
 
 
@@ -129,49 +134,6 @@
     start_last = jnp.exp(last) * last_first
     end_fade = jnp.exp(jnp.where(in_last > 0, last - col, 0.0)) * in_last
     return ratios, start_fade, start_last, end_fade
-
-
-def forward_kernel(
-    heads, pos_ref, reset_ref, proj, small_ref, conv_w_ref, aux_ref, outs, state_out, inv_out, delta_out, ext, state
-):
-    chunk = pl.program_id(0)
-    width = heads * (2 * DK + DV)
-
-    @pl.when(chunk == 0)
-    def _():
-        ext[...] = jnp.zeros_like(ext)
-        state[...] = jnp.zeros_like(state)
-
-    state_out[0] = state[...]
-    conv_w = conv_w_ref[...]
-    aux = aux_ref[...]
-    for row in range(proj.shape[1]):
-        masks = position_masks(reset_ref[row], chunk)
-        ext[row, 0:8, :] = ext[row, CH : CH + 8, :]
-        ext[row, 8:, :] = proj[0, row, 0].astype(bf16).astype(f32)
-        conv = conv_taps(ext, row, conv_w, masks[5])
-        active = conv * jax.nn.sigmoid(conv)
-        beta_all, decay, _ = gates(small_ref[0, row, 0], aux)
-        total = running(decay)
-        total_rows = as_rows(total)
-        for head in range(heads):
-            at = row * heads + head
-            q, k, v = head_parts(active, head, heads)
-            q = q * (unit(q) * DK**-0.5)
-            k = k * unit(k)
-            beta = beta_all[:, head : head + 1]
-            ratios, start_fade, start_last, end_fade = decay_terms(total, total_rows, head, heads, masks)
-            both = jnp.concatenate([q, k], axis=0)
-            pair = fine(both, k, (1, 1))
-            inv = inverse_unit_lower(beta * (ratios * masks[1] * pair[CH:]))
-            old = state[at]
-            read = coarse(both, old)
-            delta = coarse(inv, beta * (v - start_fade * read[CH:]))
-            out = start_fade * read[:CH] + coarse(ratios * pair[:CH], delta)
-            state[at] = start_last * old + coarse(end_fade * k, delta, (0, 0))
-            outs[0, row, 0, :, head * DV : (head + 1) * DV] = out
-            inv_out[0, at] = inv
-            delta_out[0, at] = delta
 
 
 def backward_kernel(
@@ -210,106 +172,126 @@
     conv_w = conv_w_ref[...]
     aux = aux_ref[...]
     lane_ids = lax.broadcasted_iota(jnp.int32, (CH, LANES), 1)
+    last_row = lax.broadcasted_iota(jnp.int32, (CH, 1), 0) == CH - 1
     ones = jnp.ones((CH, LANES), f32)
-    for row in range(proj.shape[1]):
-        masks = position_masks(reset_ref[row], chunk)
-        taps = masks[5]
-        ext[row, 0:8, :] = tail[0, row, 0].astype(bf16).astype(f32)
-        ext[row, 8:, :] = proj[0, row, 0].astype(bf16).astype(f32)
-        conv = conv_taps(ext, row, conv_w, taps)
-        sig = jax.nn.sigmoid(conv)
-        active = conv * sig
-        small = small_ref[0, row, 0]
-        beta_all, decay, shifted = gates(small, aux)
-        total = running(decay)
-        total_rows = as_rows(total)
-        d_beta_all = jnp.zeros((CH, LANES), f32)
-        d_total = jnp.zeros((CH, LANES), f32)
-        d_active = []
-        for head in range(heads):
-            at = row * heads + head
-            a_q, a_k, v = head_parts(active, head, heads)
-            q_scale = unit(a_q)
-            k_scale = unit(a_k)
-            q = a_q * (q_scale * DK**-0.5)
-            k = a_k * k_scale
-            beta = beta_all[:, head : head + 1]
-            ratios, start_fade, start_last, end_fade = decay_terms(total, total_rows, head, heads, masks)
-            both = jnp.concatenate([q, k], axis=0)
-            pair = fine(both, k, (1, 1))
-            key_key, query_key = pair[CH:], pair[:CH]
-            old = state_ref[0, at]
-            inv = inv_ref[0, at]
-            delta = delta_ref[0, at]
-            do = d_out[0, row, 0, :, head * DV : (head + 1) * DV]
-            ds = d_state[at]
-            read = coarse(both, old)
-            readings = ratios * query_key
-            faded = end_fade * k
-            d_delta = coarse(readings, do, (0, 0)) + coarse(faded, ds)
-            d_right = coarse(inv, d_delta, (0, 0))
-            d_pair = coarse(jnp.concatenate([do, d_right], axis=0), delta, (1, 1))
-            d_faded = coarse(delta, ds, (1, 1))
-            d_read = jnp.concatenate([start_fade * do, -(beta * start_fade) * d_right], axis=0)
-            d_both = coarse(d_read, old, (1, 1))
-            d_state[at] = start_last * ds + coarse(both, d_read, (0, 0))
-            d_v = beta * d_right
-            d_read_pair = d_pair[:CH] * ratios
-            d_sys = -d_pair[CH:] * (ratios * masks[1])
-            d_key_key = beta * d_sys
-            moved = d_key_key * key_key + d_read_pair * query_key
-            recall = read[CH:]
-            d_beta = jnp.sum(d_right * (v - start_fade * recall), axis=-1, keepdims=True) + jnp.sum(
-                d_sys * key_key, axis=-1, keepdims=True
-            )
-            d_start = jnp.sum(do * read[:CH], axis=-1, keepdims=True) - beta * jnp.sum(
-                d_right * recall, axis=-1, keepdims=True
-            )
-            d_end = jnp.sum(d_faded * k, axis=-1, keepdims=True) * end_fade
-            d_last = jnp.sum(d_end, axis=0, keepdims=True) + start_last * jnp.sum(
-                jnp.sum(ds * old, axis=-1, keepdims=True), axis=0, keepdims=True
-            )
-            last_row = lax.broadcasted_iota(jnp.int32, (CH, 1), 0) == CH - 1
-            d_col = (
-                jnp.sum(moved, axis=-1, keepdims=True)
-                - fine(moved, ones, (0, 0))[:, 0:1]
-                + d_start * start_fade
-                - d_end
-                + jnp.where(last_row, d_last, 0.0)
-            )
-            d_q = d_both[:CH] + coarse(d_read_pair, k)
-            d_k = (
-                d_both[CH:]
-                + coarse(d_read_pair, q, (0, 0))
-                + coarse(d_key_key, k)
-                + coarse(d_key_key, k, (0, 0))
-                + end_fade * d_faded
-            )
-            d_aq = (q_scale * DK**-0.5) * (d_q - a_q * (q_scale * q_scale * jnp.sum(a_q * d_q, axis=-1, keepdims=True)))
-            d_ak = k_scale * (d_k - a_k * (k_scale * k_scale * jnp.sum(a_k * d_k, axis=-1, keepdims=True)))
-            d_active.append((d_aq, d_ak, d_v))
-            d_beta_all = jnp.where(lane_ids == head, d_beta, d_beta_all)
-            d_total = jnp.where(lane_ids == heads + head, d_col, d_total)
-        d_decay = running(d_total, reverse=True)
-        d_shift = d_decay * (-aux[0:1]) * jax.nn.sigmoid(shifted)
-        d_small = d_beta_all * beta_all * (1.0 - beta_all) + d_shift
-        g_decay[0:1, :] += jnp.sum(d_decay * decay, axis=0, keepdims=True)
+    rows = range(proj.shape[1])
+    units = range(len(rows) * heads)
+    row_of = [u // heads for u in units]
+    head_of = [u % heads for u in units]
+    masks = [position_masks(reset_ref[r], chunk) for r in rows]
+    conv = []
+    for r in rows:
+        ext[r, 0:8, :] = tail[0, r, 0].astype(bf16).astype(f32)
+        ext[r, 8:, :] = proj[0, r, 0].astype(bf16).astype(f32)
+        conv.append(conv_taps(ext, r, conv_w, masks[r][5]))
+    sig = [jax.nn.sigmoid(c) for c in conv]
+    active = [c * g for c, g in zip(conv, sig)]
+    gated = [gates(small_ref[0, r, 0], aux) for r in rows]
+    beta_all = [g[0] for g in gated]
+    decay = [g[1] for g in gated]
+    shifted = [g[2] for g in gated]
+    total = [running(d) for d in decay]
+    total_rows = [as_rows(t) for t in total]
+    parts = [head_parts(active[row_of[u]], head_of[u], heads) for u in units]
+    a_q, a_k, v = ([p[i] for p in parts] for i in range(3))
+    q_scale = [unit(a) for a in a_q]
+    k_scale = [unit(a) for a in a_k]
+    q = [a_q[u] * (q_scale[u] * DK**-0.5) for u in units]
+    k = [a_k[u] * k_scale[u] for u in units]
+    beta = [beta_all[row_of[u]][:, head_of[u] : head_of[u] + 1] for u in units]
+    terms = [
+        decay_terms(total[row_of[u]], total_rows[row_of[u]], head_of[u], heads, masks[row_of[u]]) for u in units
+    ]
+    ratios, start_fade, start_last, end_fade = ([t[i] for t in terms] for i in range(4))
+    both = [jnp.concatenate([q[u], k[u]], axis=0) for u in units]
+    pair = [fine(both[u], k[u], (1, 1)) for u in units]
+    key_key = [p[CH:] for p in pair]
+    query_key = [p[:CH] for p in pair]
+    old = [state_ref[0, u] for u in units]
+    inv = [inv_ref[0, u] for u in units]
+    delta = [delta_ref[0, u] for u in units]
+    do = [d_out[0, row_of[u], 0, :, head_of[u] * DV : (head_of[u] + 1) * DV] for u in units]
+    ds = [d_state[u] for u in units]
+    read = [coarse(both[u], old[u]) for u in units]
+    readings = [ratios[u] * query_key[u] for u in units]
+    faded = [end_fade[u] * k[u] for u in units]
+    back_read = [coarse(readings[u], do[u], (0, 0)) for u in units]
+    back_state = [coarse(faded[u], ds[u]) for u in units]
+    d_right = [coarse(inv[u], back_read[u] + back_state[u], (0, 0)) for u in units]
+    d_pair = [coarse(jnp.concatenate([do[u], d_right[u]], axis=0), delta[u], (1, 1)) for u in units]
+    d_faded = [coarse(delta[u], ds[u], (1, 1)) for u in units]
+    d_read = [
+        jnp.concatenate([start_fade[u] * do[u], -(beta[u] * start_fade[u]) * d_right[u]], axis=0) for u in units
+    ]
+    grown = [coarse(both[u], d_read[u], (0, 0)) for u in units]
+    d_both = [coarse(d_read[u], old[u], (1, 1)) for u in units]
+    for u in units:
+        d_state[u] = start_last[u] * ds[u] + grown[u]
+    d_v = [beta[u] * d_right[u] for u in units]
+    d_read_pair = [d_pair[u][:CH] * ratios[u] for u in units]
+    d_sys = [-d_pair[u][CH:] * (ratios[u] * masks[row_of[u]][1]) for u in units]
+    d_key_key = [beta[u] * d_sys[u] for u in units]
+    moved = [d_key_key[u] * key_key[u] + d_read_pair[u] * query_key[u] for u in units]
+    moved_cols = [fine(m, ones, (0, 0))[:, 0:1] for m in moved]
+    q_more = [coarse(d_read_pair[u], k[u]) for u in units]
+    k_more = [coarse(jnp.concatenate([d_read_pair[u], d_key_key[u]], axis=0), both[u], (0, 0)) for u in units]
+    k_most = [coarse(d_key_key[u], k[u]) for u in units]
+    d_beta_all = [jnp.zeros((CH, LANES), f32) for _ in rows]
+    d_total = [jnp.zeros((CH, LANES), f32) for _ in rows]
+    d_active = []
+    for u in units:
+        r, head = row_of[u], head_of[u]
+        recall = read[u][CH:]
+        d_beta = jnp.sum(d_right[u] * (v[u] - start_fade[u] * recall), axis=-1, keepdims=True) + jnp.sum(
+            d_sys[u] * key_key[u], axis=-1, keepdims=True
+        )
+        d_start = jnp.sum(do[u] * read[u][:CH], axis=-1, keepdims=True) - beta[u] * jnp.sum(
+            d_right[u] * recall, axis=-1, keepdims=True
+        )
+        d_end = jnp.sum(d_faded[u] * k[u], axis=-1, keepdims=True) * end_fade[u]
+        d_last = jnp.sum(d_end, axis=0, keepdims=True) + start_last[u] * jnp.sum(
+            jnp.sum(ds[u] * old[u], axis=-1, keepdims=True), axis=0, keepdims=True
+        )
+        d_col = (
+            jnp.sum(moved[u], axis=-1, keepdims=True)
+            - moved_cols[u]
+            + d_start * start_fade[u]
+            - d_end
+            + jnp.where(last_row, d_last, 0.0)
+        )
+        d_q = d_both[u][:CH] + q_more[u]
+        d_k = d_both[u][CH:] + k_more[u] + k_most[u] + end_fade[u] * d_faded[u]
+        d_aq = (q_scale[u] * DK**-0.5) * (
+            d_q - a_q[u] * (q_scale[u] * q_scale[u] * jnp.sum(a_q[u] * d_q, axis=-1, keepdims=True))
+        )
+        d_ak = k_scale[u] * (
+            d_k - a_k[u] * (k_scale[u] * k_scale[u] * jnp.sum(a_k[u] * d_k, axis=-1, keepdims=True))
+        )
+        d_active.append((d_aq, d_ak, d_v[u]))
+        d_beta_all[r] = jnp.where(lane_ids == head, d_beta, d_beta_all[r])
+        d_total[r] = jnp.where(lane_ids == heads + head, d_col, d_total[r])
+    d_decay = [running(d, reverse=True) for d in d_total]
+    for r in rows:
+        taps = masks[r][5]
+        d_shift = d_decay[r] * (-aux[0:1]) * jax.nn.sigmoid(shifted[r])
+        d_small_ref[0, r, 0] = (d_beta_all[r] * beta_all[r] * (1.0 - beta_all[r]) + d_shift).astype(bf16)
+        g_decay[0:1, :] += jnp.sum(d_decay[r] * decay[r], axis=0, keepdims=True)
         g_decay[1:2, :] += jnp.sum(d_shift, axis=0, keepdims=True)
-        d_act = jnp.concatenate([d_active[h][i] for i in range(3) for h in range(heads)], axis=1)
-        d_conv = d_act * (sig * (1.0 + conv * (1.0 - sig)))
+        own = d_active[r * heads : (r + 1) * heads]
+        d_act = jnp.concatenate([own[h][i] for i in range(3) for h in range(heads)], axis=1)
+        d_conv = d_act * (sig[r] * (1.0 + conv[r] * (1.0 - sig[r])))
         d_in = None
         for j in range(TAPS):
             masked = d_conv * taps[j]
             g_conv[j : j + 1, :] += jnp.sum(
-                masked * ext[row, 8 - (TAPS - 1) + j : 8 - (TAPS - 1) + j + CH, :], axis=0, keepdims=True
+                masked * ext[r, 8 - (TAPS - 1) + j : 8 - (TAPS - 1) + j + CH, :], axis=0, keepdims=True
             )
-            dext[row, j, 0:CH, :] = masked
+            dext[r, j, 0:CH, :] = masked
             shift = TAPS - 1 - j
-            part = conv_w[j : j + 1] * dext[row, j, shift : shift + CH, :]
+            part = conv_w[j : j + 1] * dext[r, j, shift : shift + CH, :]
             d_in = part if d_in is None else d_in + part
-            dext[row, j, CH : CH + 8, :] = masked[0:8]
-        d_proj[0, row, 0] = d_in.astype(bf16)
-        d_small_ref[0, row, 0] = d_small.astype(bf16)
+            dext[r, j, CH : CH + 8, :] = masked[0:8]
+        d_proj[0, r, 0] = d_in.astype(bf16)
 
 
 def params():
@@ -318,6 +300,9 @@
 
 def whole(array):
     return pl.BlockSpec(array.shape, lambda c, pos, rst: (0,) * array.ndim)
+
+
+SMALL_COST = pl.CostEstimate(flops=1_000_000, bytes_accessed=1_000, transcendentals=0)
 
 
 def slot_spec(rows_n, width, chunk_of):
@@ -326,36 +311,145 @@
     )
 
 
-def mixer_forward(proj, small, pos, resets, conv_w, aux):
-    _, rows_n, half, _, width = proj.shape
+def prepare_kernel(
+    heads, pos_ref, reset_ref, first, second, tail, small_a, small_b, conv_w_ref, aux_ref, *outs_and_scratch
+):
+    both_out, value_out, inv_out, read_out, cols_out, ext = outs_and_scratch
+    step = pl.program_id(0)
+    conv_w = conv_w_ref[...]
+    aux = aux_ref[...]
+    lane_ids = lax.broadcasted_iota(jnp.int32, (CH, LANES), 1)
+    systems = []
+    for row in range(first.shape[1]):
+        ext[row, 0:8, :] = jnp.where(step > 0, tail[0, row, 0].astype(bf16).astype(f32), 0.0)
+        ext[row, 8 : 8 + CH, :] = first[0, row, 0].astype(bf16).astype(f32)
+        ext[row, 8 + CH :, :] = second[0, row, 0].astype(bf16).astype(f32)
+        for which, small_ref in enumerate((small_a, small_b)):
+            masks = position_masks(reset_ref[row], 2 * step + which)
+            conv = None
+            for j in range(TAPS):
+                at = which * CH + 8 - (TAPS - 1) + j
+                part = conv_w[j : j + 1] * (ext[row, at : at + CH, :] * masks[5][j])
+                conv = part if conv is None else conv + part
+            active = conv * jax.nn.sigmoid(conv)
+            beta_all, decay, _ = gates(small_ref[0, row, 0], aux)
+            total = running(decay)
+            total_rows = as_rows(total)
+            for head in range(heads):
+                at = row * heads + head
+                q, k, v = head_parts(active, head, heads)
+                q = q * (unit(q) * DK**-0.5)
+                k = k * unit(k)
+                beta = beta_all[:, head : head + 1]
+                ratios, start_fade, start_last, end_fade = decay_terms(total, total_rows, head, heads, masks)
+                both = jnp.concatenate([q, k], axis=0)
+                pair = fine(both, k, (1, 1))
+                both_out[which, at] = both
+                value_out[which, at] = v
+                systems.append((which, at, beta * (ratios * masks[1] * pair[CH:])))
+                read_out[which, at] = ratios * pair[:CH]
+                cols_out[which, at] = jnp.where(
+                    lane_ids == 0,
+                    beta,
+                    jnp.where(lane_ids == 1, start_fade, jnp.where(lane_ids == 2, end_fade, start_last)),
+                )
+    for (which, at, _), inv in zip(systems, inverses_unit_lower([part for _, _, part in systems])):
+        inv_out[which, at] = inv
+
+
+def scan_kernel(heads, pos_ref, both_ref, value_ref, inv_ref, read_ref, cols_ref, outs, state_out, delta_out, state):
+    @pl.when(pl.program_id(0) == 0)
+    def _():
+        state[...] = jnp.zeros_like(state)
+
+    state_out[0] = state[...]
+    units = range(state.shape[0])
+    old = [state[u] for u in units]
+    beta = [cols_ref[0, u, :, 0:1] for u in units]
+    start_fade = [cols_ref[0, u, :, 1:2] for u in units]
+    end_fade = [cols_ref[0, u, :, 2:3] for u in units]
+    start_last = [cols_ref[0, u, 0:1, 3:4] for u in units]
+    read = [coarse(both_ref[0, u], old[u]) for u in units]
+    right = [beta[u] * (value_ref[0, u] - start_fade[u] * read[u][CH:]) for u in units]
+    delta = [coarse(inv_ref[0, u], right[u]) for u in units]
+    grown = [coarse(end_fade[u] * both_ref[0, u, CH:, :], delta[u], (0, 0)) for u in units]
+    local = [coarse(read_ref[0, u], delta[u]) for u in units]
+    for u in units:
+        row, head = divmod(u, heads)
+        state[u] = start_last[u] * old[u] + grown[u]
+        outs[0, row, 0, :, head * DV : (head + 1) * DV] = start_fade[u] * read[u][:CH] + local[u]
+        delta_out[0, u] = delta[u]
+
+
+def mixer_prepare(proj, small, pos, resets, conv_w, aux):
+    _, rows_n, half, _, _ = proj.shape
+    width = conv_w.shape[1]
     chunks = 2 * half
     heads = width // (2 * DK + DV)
     units = rows_n * heads
-    spec = lambda w: slot_spec(rows_n, w, lambda c: c)
-    kept = lambda *s: pl.BlockSpec((1, units) + s, lambda c, pos, rst: (c, 0, 0, 0))
+    tail = pl.BlockSpec(
+        (1, rows_n, 1, 8, width),
+        lambda i, pos, rst: (
+            pos[jnp.maximum(2 * i - 1, 0)] & 1,
+            0,
+            pos[jnp.maximum(2 * i - 1, 0)] >> 1,
+            CH // 8 - 1,
+            0,
+        ),
+    )
+    even = lambda w: slot_spec(rows_n, w, lambda i: 2 * i)
+    odd = lambda w: slot_spec(rows_n, w, lambda i: 2 * i + 1)
+    shapes = ((2 * CH, DK), (CH, DV), (CH, CH), (CH, CH), (CH, LANES))
     return pl.pallas_call(
-        partial(forward_kernel, heads),
+        partial(prepare_kernel, heads),
         grid_spec=pltpu.PrefetchScalarGridSpec(
             num_scalar_prefetch=2,
+            grid=(half,),
+            in_specs=[even(width), odd(width), tail, even(LANES), odd(LANES), whole(conv_w), whole(aux)],
+            out_specs=[pl.BlockSpec((2, units) + s, lambda i, pos, rst: (i, 0, 0, 0)) for s in shapes],
+            scratch_shapes=[pltpu.VMEM((rows_n, 2 * CH + 8, width), f32)],
+        ),
+        out_shape=[jax.ShapeDtypeStruct((chunks, units) + s, f32) for s in shapes],
+        cost_estimate=KERNEL_COST,
+        compiler_params=params(),
+        name="delta_prepare",
+    )(pos, resets, proj, proj, proj, small, small, conv_w, aux)
+
+
+def mixer_scan(prepared, pos, rows_n):
+    chunks, units = prepared[0].shape[:2]
+    heads = units // rows_n
+    kept = lambda *s: pl.BlockSpec((1, units) + s, lambda c, pos: (c, 0, 0, 0))
+    mixed, states, deltas = pl.pallas_call(
+        partial(scan_kernel, heads),
+        grid_spec=pltpu.PrefetchScalarGridSpec(
+            num_scalar_prefetch=1,
             grid=(chunks,),
-            in_specs=[spec(width), spec(LANES), whole(conv_w), whole(aux)],
-            out_specs=[spec(heads * DV), kept(DK, DV), kept(CH, CH), kept(CH, DV)],
-            scratch_shapes=[pltpu.VMEM((rows_n, CH + 8, width), f32), pltpu.VMEM((units, DK, DV), f32)],
+            in_specs=[kept(*p.shape[2:]) for p in prepared],
+            out_specs=[
+                pl.BlockSpec(
+                    (1, rows_n, 1, CH, heads * DV), lambda c, pos: (pos[c] & 1, 0, pos[c] >> 1, 0, 0)
+                ),
+                kept(DK, DV),
+                kept(CH, DV),
+            ],
+            scratch_shapes=[pltpu.VMEM((units, DK, DV), f32)],
         ),
         out_shape=[
-            jax.ShapeDtypeStruct((2, rows_n, half, CH, heads * DV), f32),
+            jax.ShapeDtypeStruct((2, rows_n, chunks // 2, CH, heads * DV), f32),
             jax.ShapeDtypeStruct((chunks, units, DK, DV), f32),
-            jax.ShapeDtypeStruct((chunks, units, CH, CH), f32),
             jax.ShapeDtypeStruct((chunks, units, CH, DV), f32),
         ],
-        cost_estimate=KERNEL_COST,
+        cost_estimate=SMALL_COST,
         compiler_params=params(),
-        name="delta_forward",
-    )(pos, resets, proj, small, conv_w, aux)
+        name="delta_scan",
+    )(pos, *prepared)
+    return mixed, states, prepared[2], deltas
 
 
 def mixer_backward(proj, small, d_out, pos, resets, conv_w, aux, states, invs, deltas):
-    _, rows_n, half, _, width = proj.shape
+    _, rows_n, half, _, _ = proj.shape
+    width = conv_w.shape[1]
     chunks = 2 * half
     heads = width // (2 * DK + DV)
     units = rows_n * heads
@@ -398,14 +492,14 @@
     )(pos, resets, proj, small, proj, d_out, conv_w, aux, states, invs, deltas)
 
 
-def local_call(body, name, inputs, specs, outs, bytes_accessed):
+def local_call(body, name, inputs, specs, outs, bytes_accessed=0):
     return pl.pallas_call(
         body,
         grid=(1,),
         in_specs=specs,
         out_specs=whole_specs(outs),
         out_shape=outs,
-        cost_estimate=pl.CostEstimate(flops=1_000_000, bytes_accessed=bytes_accessed, transcendentals=0),
+        cost_estimate=SMALL_COST,
         compiler_params=pltpu.CompilerParams(vmem_limit_bytes=VMEM_BYTES),
         name=name,
     )(*inputs)
@@ -533,8 +627,9 @@
 ROW_BLOCK = 256
 
 
-def gated_norm(mixed, gate, gain):
+def gated_norm(mixed, proj, gain):
     rows_n, width = mixed.shape
+    gate_block = pl.BlockSpec((ROW_BLOCK, width), lambda i: (i, proj.shape[1] // width - 1))
 
     def body(mixed_ref, gate_ref, gain_ref, out_ref):
         for at in range(0, width, DV):
@@ -547,17 +642,18 @@
     return pl.pallas_call(
         body,
         grid=(rows_n // ROW_BLOCK,),
-        in_specs=[block, block, pl.BlockSpec((1, DV), lambda i: (0, 0))],
+        in_specs=[block, gate_block, pl.BlockSpec((1, DV), lambda i: (0, 0))],
         out_specs=block,
         out_shape=jax.ShapeDtypeStruct((rows_n, width), bf16),
-        cost_estimate=pl.CostEstimate(flops=1_000_000, bytes_accessed=5_000_000, transcendentals=0),
+        cost_estimate=SMALL_COST,
         compiler_params=params(),
         name="gated_norm",
-    )(mixed, gate, gain.reshape(1, DV))
-
-
-def gated_norm_back(mixed, gate, gain, d_out):
+    )(mixed, proj, gain.reshape(1, DV))
+
+
+def gated_norm_back(mixed, proj, gain, d_out):
     rows_n, width = mixed.shape
+    gate_block = pl.BlockSpec((ROW_BLOCK, width), lambda i: (i, proj.shape[1] // width - 1))
 
     def body(mixed_ref, gate_ref, gain_ref, d_ref, d_mixed_ref, d_gate_ref, g_gain_ref):
         @pl.when(pl.program_id(0) == 0)
@@ -586,17 +682,17 @@
     return pl.pallas_call(
         body,
         grid=(rows_n // ROW_BLOCK,),
-        in_specs=[block, block, pl.BlockSpec((1, DV), lambda i: (0, 0)), block],
+        in_specs=[block, gate_block, pl.BlockSpec((1, DV), lambda i: (0, 0)), block],
         out_specs=[block, block, pl.BlockSpec((8, DV), lambda i: (0, 0))],
         out_shape=[
             jax.ShapeDtypeStruct((rows_n, width), f32),
             jax.ShapeDtypeStruct((rows_n, width), bf16),
             jax.ShapeDtypeStruct((8, DV), f32),
         ],
-        cost_estimate=pl.CostEstimate(flops=1_000_000, bytes_accessed=9_000_000, transcendentals=0),
+        cost_estimate=SMALL_COST,
         compiler_params=params(),
         name="gated_norm_back",
-    )(mixed, gate, gain.reshape(1, DV), d_out)
+    )(mixed, proj, gain.reshape(1, DV), d_out)
 
 
 def laid_out(blocks, pieces, total):
@@ -624,7 +720,7 @@
     return [bits[1:] + bits[:1], bits[:0:-1] + bits[:1]]
 
 
-def gather_rows(rows, axis, ordered=True):
+def gather_rows(rows, axis, ordered=True, earlier=None):
     laid = []
     for row, order in zip(rows, routes(axis) * rows.shape[0]):
         held = row[None]
@@ -646,6 +742,9 @@
         else:
             laid.extend(parts)
     even = jnp.concatenate(laid, axis=0).reshape((rows.shape[0], -1) + rows.shape[1:])
+    if earlier is not None:
+        even, earlier = lax.optimization_barrier((even, earlier))
+        return even, swap(even, axis, 1), earlier
     return even, swap(even, axis, 1)
 
 
@@ -754,7 +853,6 @@
     key_w, val_w = heads * DK, heads * DV
     conv_cols = 2 * key_w + val_w
     half = batch_rows * size // 2 * span_len
-    cut = 16 * ff // 11 // LANES * LANES
     halves = (batch_rows, size // 2, span_len)
     blocks = (2,) + halves
 
@@ -772,6 +870,7 @@
             w_proj[:, :KW].reshape(own_rows, size, key_w),
             w_proj[:, KW : 2 * KW].reshape(own_rows, size, key_w),
             w_proj[:, 2 * KW : CW].reshape(own_rows, size, val_w),
+            w_proj[:, CW:].reshape(own_rows, size, val_w),
         ],
         axis=-1,
     ).transpose(1, 0, 2)
@@ -780,9 +879,8 @@
     gain_in, gain_ff = shuffled(norm_in), shuffled(norm_ff)
     h_in = joined(gather_rows(rms_scale(own_in.astype(f32), gain_in).astype(bf16).reshape(tokens.shape), "seq"))
     mix_w = stacked(after(moved_mix, out_w, h_in))
-    packed_gate, packed_gu, w_small, d_own, own_down = after(
+    packed_gu, w_small, d_own, own_down = after(
         (
-            w_proj[:, CW:].reshape(own_rows, size, val_w).transpose(1, 0, 2),
             w_gu.reshape(own_rows, 2, size, ff).transpose(2, 0, 1, 3).reshape(size, own_rows, 2 * ff),
             w_small,
             shuffled(grad_out),
@@ -790,7 +888,7 @@
         ),
         moved_mix,
     )
-    d_out = joined(gather_rows(d_own, "seq", False))
+    d_halves = gather_rows(d_own, "seq", False)
     small_all = gather_small(gather_small(w_small, "seq"), "batch").reshape(D, 2 * H)
     small_w = jnp.pad(
         jnp.concatenate(
@@ -803,11 +901,7 @@
         ((0, 0), (0, LANES - 2 * heads)),
     )
     out_w = shuffled(out_w)
-    moved_gate, moved_gu = exchanged(packed_gate), exchanged(packed_gu)
-    moved_gate, moved_gu, small_w, mix_w = lax.optimization_barrier((moved_gate, moved_gu, small_w, mix_w))
-    gate_w = stacked(moved_gate)
-    moved_first, moved_rest = moved_gu[:, :, :cut], moved_gu[:, :, cut:]
-    gu_first = stacked(moved_first)
+    moved_gu = exchanged(packed_gu)
 
     slots = jnp.arange(size, dtype=jnp.int32) ^ me.astype(jnp.int32)
     conv_l = jnp.concatenate(
@@ -829,35 +923,34 @@
         ((0, 6), at_heads),
     )
 
-    proj = mm(h_in, mix_w).reshape(blocks + (conv_cols,))
     small = mm(h_in, small_w).reshape(blocks + (LANES,))
-    proj, out_w, moved_rest, own_down = lax.optimization_barrier((proj, out_w, moved_rest, own_down))
-    gu_rest = stacked(moved_rest)
-    down_w = lax.all_gather(own_down, "batch", axis=0, tiled=True)
-    mixed, states, invs, deltas = mixer_forward(proj, small, slots, resets, conv_l, aux)
+    proj = mm(h_in, mix_w)
+    down_first = lax.all_gather(own_down[:, : D // 2], "batch", axis=0, tiled=True)
+    prepared = mixer_prepare(proj.reshape(blocks + (-1,)), small, slots, resets, conv_l, aux)
+    prepared, moved_gu, down_first = lax.optimization_barrier((prepared, moved_gu, down_first))
+    down_rest = lax.all_gather(own_down[:, D // 2 :], "batch", axis=0, tiled=True)
+    gu_w = stacked(moved_gu)
+    mixed, states, invs, deltas = mixer_scan(prepared, slots, batch_rows)
     mixed = mixed.reshape(-1, val_w)
-    gate = mm(h_in, gate_w)
-    z_rows = gated_norm(mixed, gate, norm_head)
+    z_rows = gated_norm(mixed, proj, norm_head)
 
     def parts(product, left):
         send = product(left[half:]).astype(bf16).reshape(halves + (D,))
         return product(left[:half]).astype(bf16).reshape(halves + (D,)), send
 
     keep, send = parts(lambda rows: mm(rows, out_w), z_rows)
-    keep, send, d_out = after((keep, send, d_out), gu_first)
-    residual, normed_ff = add_and_norm(
-        scatter_rows(keep, send, "seq"), after(own_in, gu_rest), gain_ff
-    )
-
-    h_halves = gather_rows(normed_ff, "seq", False)
-    gu_w = jnp.concatenate([gu_first, gu_rest], axis=1)
-    h_ff = joined(h_halves)
+    d_out = joined(after(d_halves, keep, send))
+    residual, normed_ff = add_and_norm(scatter_rows(keep, send, "seq"), own_in, gain_ff)
+
+    even, odd, gu_w = gather_rows(normed_ff, "seq", False, gu_w)
+    h_ff = joined((even, odd))
     gate_up = mm(h_ff, gu_w)
     hidden_full, pull_glu = jax.vjp(glu_hidden, gate_up[:, :ff], gate_up[:, ff:])
-    hidden = after(hidden_full.astype(bf16), down_w)
+    hidden, down_rest = lax.optimization_barrier((hidden_full.astype(bf16), down_rest))
     down_grad = contract_rows(d_out, hidden).astype(bf16)
     down_own = summed(down_grad)
-    d_hidden = contract_cols(after(d_out, down_grad), down_w)
+    d_hidden = contract_cols(d_out[:, : D // 2], down_first) + contract_cols(d_out[:, D // 2 :], down_rest)
+    down_w = jnp.concatenate([down_first, down_rest], axis=1)
     d_gate_up = jnp.concatenate(pull_glu(d_hidden), axis=1).astype(bf16)
     keep, send = parts(lambda rows: contract_cols(rows, gu_w), d_gate_up)
     terms = scatter_rows(keep, send, "seq", False)
@@ -868,31 +961,33 @@
 
     d_branch = joined(gather_rows(after(d_branch, gu_grad, down_own, out_parts), "seq"))
     d_heads = contract_cols(d_branch, out_w)
-    d_mixed, d_gate, g_norm_head = gated_norm_back(mixed, gate, norm_head, d_heads)
+    d_mixed, d_gate, g_norm_head = gated_norm_back(mixed, proj, norm_head, d_heads)
     out_grad = jnp.concatenate(
         [contract_rows(h_in, d_gate).astype(bf16), contract_rows(d_branch, z_rows).astype(bf16)], axis=1
     )
-    d_mixed = after(d_mixed, out_grad)
+    d_mixed, out_grad = lax.optimization_barrier((d_mixed, out_grad))
     d_proj, d_small, g_conv_l, g_decay = mixer_backward(
-        proj, small, d_mixed.reshape(blocks + (val_w,)), slots, resets, conv_l, aux, states, invs, deltas
+        proj.reshape(blocks + (-1,)), small, d_mixed.reshape(blocks + (val_w,)), slots, resets, conv_l, aux, states, invs, deltas
     )
     d_proj, gu_own = lax.optimization_barrier((d_proj.reshape(-1, conv_cols), gu_own))
     d_small = d_small.reshape(-1, LANES)
     out_own = summed(out_grad)
     mix_grad = contract_rows(h_in, d_proj).astype(bf16)
-    mix_own = summed(mix_grad)
-    d_proj, d_small, g_conv_l, gu_own, out_parts = after((d_proj, d_small, g_conv_l, gu_own, out_parts), mix_grad)
-    ff_grads = exchanged(jnp.concatenate([gu_own, down_own], axis=-1))
+    mix_moved = lax.all_to_all(
+        mix_grad.reshape(groups, size, own_rows, conv_cols), "seq", split_axis=1, concat_axis=1, tiled=True
+    )
+    mix_grads = lax.psum_scatter(mix_moved, "batch", scatter_dimension=0, tiled=True)[0]
+    d_proj, d_small, g_conv_l, gu_own = after((d_proj, d_small, g_conv_l, gu_own), mix_grad)
+    gu_grads, down_grads = exchanged(gu_own), exchanged(down_own)
+    block_out = add_in_order(scatter_rows(*out_parts, "seq", False), residual, (size, groups))
     keep, send = parts(
-        lambda rows: contract_cols(rows[:, :conv_cols], mix_w)
-        + contract_cols(rows[:, conv_cols : conv_cols + val_w], gate_w)
+        lambda rows: contract_cols(rows[:, : conv_cols + val_w], mix_w)
         + contract_cols(rows[:, conv_cols + val_w :], small_w),
         jnp.concatenate([d_proj, d_gate, d_small], axis=1),
     )
     d_tokens, g_norm_in = norm_back(
-        scatter_rows(keep, send, "seq", earlier=(ff_grads, out_own)), own_in, d_residual, gain_in, bf16, (size, groups)
-    )
-    block_out = add_in_order(scatter_rows(*after(out_parts, keep, send), "seq", False), residual, (size, groups))
+        scatter_rows(keep, send, "seq"), own_in, after(d_residual, out_own), gain_in, bf16, (size, groups)
+    )
 
     small_grad = contract_rows(d_small, h_in)[: 2 * heads]
     local = jnp.concatenate(
@@ -918,13 +1013,15 @@
     )
     g_small = g_small.transpose(3, 1, 0, 2).reshape(own_rows, 2 * H)
     gains = sum_all(jnp.concatenate([g_norm_in[0], g_norm_ff[0], g_norm_head[0]]), ("seq", "batch"))
+    gains = jnp.concatenate([restored(gains[: 2 * D].reshape(2, D)).reshape(-1), gains[2 * D :]])
 
     out_grads = exchanged(out_own)
-    mix_own, d_tokens, block_out, out_grads = lax.optimization_barrier((mix_own, d_tokens, block_out, out_grads))
-    g_gu = laid_out([ff_grads], [(0, 0, ff, 0), (0, ff, ff, FF)], 2 * FF)
-    g_down = ff_grads[:, :, 2 * ff :].astype(f32).transpose(0, 2, 1).reshape(FF, own_rows)
+    g_gu = laid_out([gu_grads], [(0, 0, ff, 0), (0, ff, ff, FF)], 2 * FF)
+    g_down = down_grads.astype(f32).transpose(0, 2, 1).reshape(FF, own_rows)
     g_out = out_grads[:, :, val_w:].astype(f32).transpose(0, 2, 1).reshape(VW, own_rows)
-    mix_grads = exchanged(mix_own)
+    ready = (d_tokens, block_out, out_grads, g_gu, g_down, g_out, gains, g_conv, g_small)
+    mix_grads, ready = lax.optimization_barrier((mix_grads, ready))
+    d_tokens, block_out, out_grads, g_gu, g_down, g_out, gains, g_conv, g_small = ready
     g_proj = laid_out(
         [mix_grads, out_grads],
         [(0, 0, key_w, 0), (0, key_w, key_w, KW), (0, 2 * key_w, val_w, 2 * KW), (1, 0, val_w, CW)],
@@ -938,8 +1035,8 @@
         g_out,
         g_gu,
         g_down,
-        restored(gains[:D]),
-        restored(gains[D : 2 * D]),
+        gains[:D],
+        gains[D : 2 * D],
         gains[2 * D :],
         g_conv,
         g_alog,

time: 757 us -> 713 us (0.942)
  Pallas kernels: 169 us -> 99.1 us
  waiting for transfers between devices: 250 us -> 293 us
  blocking collectives: 0 us -> 26.2 us
  other arithmetic: 39.3 us -> 22.7 us
  matrix products: 117 us -> 104 us
  starting transfers between devices: 82 us -> 69 us
    pallas_call x3 -> x4, Pallas kernels: 85.8 us -> 39 us  [the longest x1 16.1 us: mixer_prepare(): pl.pallas_call(partial(prepare_kernel, heads), grid_spec=pltpu.PrefetchSc...]
    all_to_all x0 -> x1, blocking collectives: none -> 26.2 us  [exchanged(): lax.all_to_all(packed, 'seq', split_axis=0, concat_axis=0, tiled=True)]
    pallas_call x1, Pallas kernels: 62.2 us -> 39.3 us  [mixer_backward(): pl.pallas_call(partial(backward_kernel, heads, chunks), grid_spec=pltpu.P...]
    all_gather x4 -> x2, waiting for transfers between devices: 29.1 us -> 48.8 us  [stacked(): full = lax.all_gather(blocks, 'batch', axis=0, tiled=False)]
    all_gather x1, waiting for transfers between devices: 3.1 us -> 22.3 us  [shards(): out_w = lax.all_gather(w_out, 'batch', axis=0, tiled=True)]
    all_to_all x0 -> x1, waiting for transfers between devices: none -> 14.5 us  [shards(): lax.all_to_all(mix_grad.reshape(groups, size, own_rows, conv_cols), 'seq'...]
    dot_general x10 -> x9, matrix products: 44.7 us -> 31.7 us  [contract_cols(): lax.dot_general(left, right, (((1,), (1,)), ((), ())), preferred_element_...]
    ppermute x55, starting transfers between devices: 56.9 us -> 46.8 us  [swap(): lax.ppermute(value, axis, [(i, i ^ bit) for i in range(lax.axis_size(axis...]
  transfers between devices with their start and end apart: 71 -> 69, of which waited for: 38 -> 46; matrix products, arithmetic and copies ran while one was open for 28% -> 26% of each run, Pallas kernels for 22% -> 14%
where the time goes in v3:
time: 713 us; the launch traced here: 703 us
  waiting for transfers between devices  293 us (41%)
  matrix products  104 us (15%)
  Pallas kernels  99.1 us (14%)
  local copies, waits for them, and re-layouts  73.1 us (10%)
  starting transfers between devices  69 us (10%)
  blocking collectives  26.2 us (4%)
  other arithmetic  22.7 us (3%)
  between operations  15.6 us (2%)
    ppermute x55, waiting for transfers between devices, swap(): lax.ppermute(value, axis, [(i, i ^ bit) for i in range(lax.axis_size(axis...  172 us
    all_gather x2, waiting for transfers between devices, stacked(): full = lax.all_gather(blocks, 'batch', axis=0, tiled=False)  48.8 us
    ppermute x55, starting transfers between devices, swap(): lax.ppermute(value, axis, [(i, i ^ bit) for i in range(lax.axis_size(axis...  46.8 us
    pallas_call x1, Pallas kernels, mixer_backward(): pl.pallas_call(partial(backward_kernel, heads, chunks), grid_spec=pltpu.P...  39.3 us
    dot_general x7, matrix products, mm(): return jnp.dot(left, right, preferred_element_type=f32)  38 us
    dot_general x6, matrix products, contract_rows(): lax.dot_general(left, right, (((0,), (0,)), ((), ())), preferred_element_...  34 us
    dot_general x9, matrix products, contract_cols(): lax.dot_general(left, right, (((1,), (1,)), ((), ())), preferred_element_...  31.7 us
    all_to_all x1, blocking collectives, exchanged(): lax.all_to_all(packed, 'seq', split_axis=0, concat_axis=0, tiled=True)  26.2 us
  transfers between devices with their start and end apart: 69, of which 46 were waited for; matrix products, arithmetic and copies ran while one was open for 26% of the time, Pallas kernels for 14%

profile of v3, /device:TPU:0, one launch (start us, length us, event | category | flops | bytes accessed | tf_op | source)
XLA Modules:
  0.0 702.7 jit_solution(5448625459321984356)
XLA Ops:
  10.7 26.2 %all_to_all.30 = bf16[8,64,1536]{2,1,0:T(8,128)(2,1)} all-to-all(bf16[8,64,1536]{2,1,0:T(8,128)(2,1)S(1)} %copy.108), channel_id=1, replica_groups=mesh['seq'=8,'batch'=4] {'seq'}, dimensions={0} | all-to-all | bytes 3145728 | tf_op jit(solution)/shard_map/all_to_all | solution.py:817
  36.9 22.3 %all-gather.8.cloned.1.call-done = bf16[512,2048]{0,1:T(8,128)(2,1)} async-done(((bf16[128,2048]{0,1:T(8,128)(2,1)}), bf16[512,2048]{0,1:T(8,128)(2,1)}) %all-gather.8.cloned.1.call-update) | async-done | bytes 2097168 | tf_op jit(solution)/shard_map/all_gather | solution.py:867
  76.0 8.3 %collective-permute-done.1 = bf16[2,64,2048]{2,1,0:T(8,128)(2,1)S(1)} collective-permute-done((bf16[2,64,2048]{2,1,0:T(8,128)(2,1)S(1)}, bf16[2,64,2048]{2,1,0:T(8,128)(2,1)S(1)}, u32[]{:S(2)}, u32[]{:S(2)}) %collective-permute-start.1) | collective-permute-done | bytes 524320 | tf_op jit(solution)/shard_map/ppermute | solution.py:715
  110.5 8.6 %collective-permute-done.8 = bf16[1,8,64,32]{2,3,1,0:T(8,128)(2,1)S(1)} collective-permute-done((bf16[1,8,64,32]{2,3,1,0:T(8,128)(2,1)S(1)}, bf16[1,8,64,32]{2,3,1,0:T(8,128)(2,1)S(1)}, u32[]{:S(2)}, u32[]{:S(2)}) %collective-permute-start.8) | collective-permute-done | bytes 32800 | tf_op jit(solution)/shard_map/ppermute | solution.py:715
  124.8 10.6 %collective-permute-done.9 = bf16[2,8,64,32]{2,3,1,0:T(8,128)(2,1)S(1)} collective-permute-done((bf16[2,8,64,32]{2,3,1,0:T(8,128)(2,1)S(1)}, bf16[2,8,64,32]{2,3,1,0:T(8,128)(2,1)S(1)}, u32[]{:S(2)}, u32[]{:S(2)}) %collective-permute-start.9) | collective-permute-done | bytes 65568 | tf_op jit(solution)/shard_map/ppermute | solution.py:715
  140.8 39.2 %all-gather.14.cloned.1.call-done = bf16[32,64,1536]{2,1,0:T(8,128)(2,1)} async-done(((bf16[8,64,1536]{2,1,0:T(8,128)(2,1)}), bf16[32,64,1536]{2,1,0:T(8,128)(2,1)}) %all-gather.14.cloned.1.call-update) | async-done | bytes 6291472 | tf_op jit(solution)/shard_map/all_gather | solution.py:821
  180.0 11.8 %fusion.77.gate_ref = f32[1024,1536]{1,0:T(8,128)} fusion(bf16[2048,1536]{1,0:T(8,128)(2,1)} %bitcast.399, bf16[512,2048]{1,0:T(8,128)(2,1)} %bitcast.6, bf16[512,2048]{1,0:T(8,128)(2,1)} %bitcast.390), kind=kOutput, calls=%fused_computation.231 | convolution fusion | flops 6450839552 | bytes 16777216 | tf_op jit(solution)/shard_map/dot_general | solution.py:797
  191.7 16.1 %delta_prepare.1 = (f32[8,4,128,128]{3,2,1,0:T(8,128)}, f32[8,4,64,256]{3,2,1,0:T(8,128)}, f32[8,4,64,64]{3,2,1,0:T(8,128)}, f32[8,4,64,64]{3,2,1,0:T(8,128)}, f32[8,4,64,128]{3,2,1,0:T(8,128)}) custom-call(s32[8]{0:T(128)} %iota_xor_fusion.pos_ref, s32[2]{0:T(128)} %reset_ref.3, f32[2,2,4,64,1536]{4,3,2,1,0:T(8,128)} %bitcast.294, ...), custom_call_target="tpu_custom_call" | custom-call | flops 30000001024 | bytes 40000000 | tf_op jit(solution)/shard_map/delta_prepare/pallas_call | solution.py:403
  207.9 7.3 %all-gather.10.cloned.1.call-done = bf16[704,1024]{1,0:T(8,128)(2,1)} async-done(((bf16[176,1024]{1,0:T(8,128)(2,1)}), bf16[704,1024]{1,0:T(8,128)(2,1)}) %all-gather.10.cloned.1.call-update) | async-done | bytes 1441808 | tf_op jit(solution)/shard_map/all_gather | solution.py:928
  217.3 12.6 %delta_scan.1 = (f32[2,2,4,64,512]{4,3,2,1,0:T(8,128)}, f32[8,4,128,256]{3,2,1,0:T(8,128)}, f32[8,4,64,256]{3,2,1,0:T(8,128)}) custom-call(s32[8]{0:T(128)} %iota_xor_fusion.pos_ref, f32[8,4,128,128]{3,2,1,0:T(8,128)} %get-tuple-element.84.both_ref, f32[8,4,64,256]{3,2,1,0:T(8,128)} %get-tuple-element.85.value_ref, ...), custom_call_target="tpu_custom_call" | custom-call | flops 1000000 | bytes 1000 | tf_op jit(solution)/shard_map/delta_scan/pallas_call | solution.py:423
  242.6 5.3 collective-permute-done.10
  257.7 11.2 %collective-permute-done.18.refs_4_ = bf16[2,64,2048]{2,1,0:T(8,128)(2,1)S(1)} collective-permute-done((bf16[2,64,2048]{2,1,0:T(8,128)(2,1)S(1)}, bf16[2,64,2048]{2,1,0:T(8,128)(2,1)S(1)}, u32[]{:S(2)}, u32[]{:S(2)}) %collective-permute-start.18) | collective-permute-done | bytes 524320 | tf_op jit(solution)/shard_map/ppermute | solution.py:715
  269.7 5.5 collective-permute-done.16.refs_2_
  301.1 9.0 %collective-permute-done.21 = bf16[2,64,2048]{2,1,0:T(8,128)(2,1)S(1)} collective-permute-done((bf16[2,64,2048]{2,1,0:T(8,128)(2,1)S(1)}, bf16[2,64,2048]{2,1,0:T(8,128)(2,1)S(1)}, u32[]{:S(2)}, u32[]{:S(2)}) %collective-permute-start.21) | collective-permute-done | bytes 524320 | tf_op jit(solution)/shard_map/ppermute | solution.py:715
  313.3 9.6 %all-gather.16.cloned.1.call-done = bf16[32,64,1408]{2,1,0:T(8,128)(2,1)} async-done(((bf16[8,64,1408]{2,1,0:T(8,128)(2,1)}), bf16[32,64,1408]{2,1,0:T(8,128)(2,1)}) %all-gather.16.cloned.1.call-update) | async-done | bytes 5767184 | tf_op jit(solution)/shard_map/all_gather | solution.py:821
  327.1 10.1 %fusion.76 = f32[1024,1408]{0,1:T(8,128)S(1)} fusion(bf16[2048,1408]{1,0:T(8,128)(2,1)} %bitcast.404, bf16[512,2048]{1,0:T(8,128)(2,1)} %bitcast.47, bf16[512,2048]{1,0:T(8,128)(2,1)S(1)} %bitcast.324), kind=kOutput, calls=%fused_computation.230 | convolution fusion | flops 5913968640 | bytes 15728640 | tf_op jit(solution)/shard_map/dot_general | solution.py:797
  340.6 17.5 %all-gather.12.cloned.1.call-done = bf16[704,1024]{1,0:T(8,128)(2,1)} async-done(((bf16[176,1024]{1,0:T(8,128)(2,1)}), bf16[704,1024]{1,0:T(8,128)(2,1)}) %all-gather.12.cloned.1.call-update) | async-done | bytes 1441808 | tf_op jit(solution)/shard_map/all_gather | solution.py:931
  358.1 6.7 fusion.1
  383.8 8.5 %convolution_convert_fusion = bf16[2048,1408]{1,0:T(8,128)(2,1)} fusion(bf16[1024,2048]{1,0:T(8,128)(2,1)S(1)} %pad_maximum_fusion.3, bf16[1024,704]{0,1:T(8,128)(2,1)S(1)} %get-tuple-element.137, bf16[1024,704]{0,1:T(8,128)(2,1)S(1)} %get-tuple-element.138), kind=kOutput, calls=%fused_computation.3 | convolution fusion | flops 5914230784 | bytes 12845056 | tf_op jit(solution)/shard_map/dot_general | solution.py:801
  403.8 7.6 %collective-permute-done.26.refs_2_ = bf16[2,64,2048]{2,1,0:T(8,128)(2,1)S(1)} collective-permute-done((bf16[2,64,2048]{2,1,0:T(8,128)(2,1)S(1)}, bf16[2,64,2048]{2,1,0:T(8,128)(2,1)S(1)}, u32[]{:S(2)}, u32[]{:S(2)}) %collective-permute-start.26) | collective-permute-done | bytes 524320 | tf_op jit(solution)/shard_map/ppermute | solution.py:715
  430.9 5.3 collective-permute-done.30
  439.9 8.2 %collective-permute-done.31 = bf16[2,64,2048]{2,1,0:T(8,128)(2,1)S(1)} collective-permute-done((bf16[2,64,2048]{2,1,0:T(8,128)(2,1)S(1)}, bf16[2,64,2048]{2,1,0:T(8,128)(2,1)S(1)}, u32[]{:S(2)}, u32[]{:S(2)}) %collective-permute-start.31) | collective-permute-done | bytes 524320 | tf_op jit(solution)/shard_map/ppermute | solution.py:715
  460.8 5.9 gated_norm_back.1
  481.1 12.1 %collective-permute-done.41.refs_2_ = bf16[2,64,2048]{2,1,0:T(8,128)(2,1)S(1)} collective-permute-done((bf16[2,64,2048]{2,1,0:T(8,128)(2,1)S(1)}, bf16[2,64,2048]{2,1,0:T(8,128)(2,1)S(1)}, u32[]{:S(2)}, u32[]{:S(2)}) %collective-permute-start.41) | collective-permute-done | bytes 524320 | tf_op jit(solution)/shard_map/ppermute | solution.py:715
  501.7 39.3 %delta_backward.1 = (bf16[2,2,4,64,1024]{4,3,2,1,0:T(8,128)(2,1)}, bf16[2,2,4,64,128]{4,3,2,1,0:T(8,128)(2,1)}, f32[8,1024]{1,0:T(8,128)}, f32[8,128]{1,0:T(8,128)}) custom-call(s32[8]{0:T(128)} %iota_xor_fusion.pos_ref, s32[2]{0:T(128)} %reset_ref.3, f32[2,2,4,64,1536]{4,3,2,1,0:T(8,128)} %bitcast.297, f32[2,2,4,64,128]{4,3,2,1,0:T(8,128)} %bitcast.417, ...), custom_call_target="tpu_custom_call" | custom-call | flops 30000001024 | bytes 40000000 | tf_op jit(solution)/shard_map/delta_backward/pallas_call | solution.py:464
  541.1 7.5 %convolution_convert_fusion.1 = bf16[2048,1024]{1,0:T(8,128)(2,1)S(1)} fusion(bf16[1024,1024]{1,0:T(8,128)(2,1)} %bitcast.331, bf16[512,2048]{1,0:T(8,128)(2,1)} %bitcast.6, bf16[512,2048]{1,0:T(8,128)(2,1)} %bitcast.391), kind=kOutput, calls=%fused_computation.17 | convolution fusion | flops 4305453056 | bytes 10485760 | tf_op jit(solution)/shard_map/dot_general | solution.py:801
  569.4 6.3 fusion.16
  582.9 5.7 collective-permute-done.51
  590.6 14.5 %all-to-all-done.2 = bf16[4,8,64,1024]{3,2,0,1:T(8,128)(2,1)} async-done(((bf16[4,8,64,1024]{3,2,0,1:T(8,128)(2,1)}), bf16[4,8,64,1024]{3,2,0,1:T(8,128)(2,1)}, u32[]{:S(2)}, u32[]{:S(2)}) %all-to-all-start.2) | async-done | bytes 4194336 | tf_op jit(solution)/shard_map/all_to_all | solution.py:976
  621.2 9.3 %collective-permute-done.53 = f32[2,12292]{1,0:T(2,128)S(1)} collective-permute-done((f32[2,12292]{1,0:T(2,128)S(1)}, f32[2,12292]{1,0:T(2,128)S(1)}, u32[]{:S(2)}, u32[]{:S(2)}) %collective-permute-start.53) | collective-permute-done | bytes 98368 | tf_op jit(solution)/shard_map/ppermute | solution.py:715
  632.3 9.0 %collective-permute-done.38.refs_4_ = bf16[2,64,2048]{2,1,0:T(8,128)(2,1)S(1)} collective-permute-done((bf16[2,64,2048]{2,1,0:T(8,128)(2,1)S(1)}, bf16[2,64,2048]{2,1,0:T(8,128)(2,1)S(1)}, u32[]{:S(2)}, u32[]{:S(2)}) %collective-permute-start.38) | collective-permute-done | bytes 524320 | tf_op jit(solution)/shard_map/ppermute | solution.py:715
  685.1 6.2 reduce-scatter.9.cloned.1.call-done
  (469 shorter events, 303.9 us)
Async XLA Ops:
  7.2 51.9 %all-gather.8.cloned.1.call-start = ((), (), s32[]{:S(2)}) async-start(), calls=%async_computation.10 | async-start | bytes 2621440 | tf_op jit(solution)/shard_map/all_gather | solution.py:867
  9.4 170.6 %all-gather.14.cloned.1.call-start = ((), (), s32[]{:S(2)}) async-start(), calls=%async_computation.17 | async-start | bytes 7864320 | tf_op jit(solution)/shard_map/all_gather | solution.py:821
  88.7 47.8 %collective-permute-start.4 = (bf16[2,4,64,2048]{3,2,1,0:T(8,128)(2,1)}, bf16[2,4,64,2048]{3,2,1,0:T(8,128)(2,1)}, u32[]{:S(2)}, u32[]{:S(2)}) collective-permute-start(bf16[2,4,64,2048]{3,2,1,0:T(8,128)(2,1)} %bitcast.388), channel_id=1, source_target_pairs={{0,4},{4,0},{8,12},{12,8},{16,20},{20,16},{24,28},{28,24},{1,5},{5... | collective-permute-start | bytes 6291464 | tf_op jit(solution)/shard_map/ppermute | solution.py:715
  119.1 16.3 %collective-permute-start.9 = (bf16[2,8,64,32]{2,3,1,0:T(8,128)(2,1)S(1)}, bf16[2,8,64,32]{2,3,1,0:T(8,128)(2,1)S(1)}, u32[]{:S(2)}, u32[]{:S(2)}) collective-permute-start(bf16[2,8,64,32]{2,3,1,0:T(8,128)(2,1)S(1)} %pad_maximum_fusion.23), channel_id=1, source_target_pairs={{0,2},{1,3},{2,0},{3,1},{4,6},{5,7},{6,4},{7,5},{8,10},{9,11},{10,... | collective-permute-start | bytes 196616 | tf_op jit(solution)/shard_map/ppermute | solution.py:715
  120.2 87.7 %all-to-all-start.1 = ((bf16[8,64,1408]{2,1,0:T(8,128)(2,1)}), bf16[8,64,1408]{2,1,0:T(8,128)(2,1)S(1)}, u32[]{:S(2)}, u32[]{:S(2)}) async-start(bf16[8,64,1408]{2,1,0:T(8,128)(2,1)} %reshape.473), calls=%async_computation.1 | async-start | bytes 2883584 | tf_op jit(solution)/shard_map/all_to_all | solution.py:817
  123.8 91.4 %all-gather.10.cloned.1.call-start = ((), (), s32[]{:S(2)}) async-start(), calls=%async_computation.11 | async-start | bytes 1802240 | tf_op jit(solution)/shard_map/all_gather | solution.py:928
  124.6 198.3 %all-gather.16.cloned.1.call-start = ((), (), s32[]{:S(2)}) async-start(), calls=%async_computation.18 | async-start | bytes 7208960 | tf_op jit(solution)/shard_map/all_gather | solution.py:821
  215.2 142.9 %all-gather.12.cloned.1.call-start = ((), (), s32[]{:S(2)}) async-start(), calls=%async_computation.12 | async-start | bytes 1802240 | tf_op jit(solution)/shard_map/all_gather | solution.py:931
  238.0 15.8 %collective-permute-start.15 = (bf16[2,4,64,2048]{3,2,1,0:T(8,128)(2,1)}, bf16[2,4,64,2048]{3,2,1,0:T(8,128)(2,1)S(1)}, u32[]{:S(2)}, u32[]{:S(2)}) collective-permute-start(bf16[2,4,64,2048]{3,2,1,0:T(8,128)(2,1)} %bitcast.29), channel_id=1, source_target_pairs={{0,4},{4,0},{8,12},{12,8},{16,20},{20,16},{24,28},{28,24},{1,5},{5... | collective-permute-start | bytes 6291464 | tf_op jit(solution)/shard_map/ppermute | solution.py:715
  241.1 15.2 %collective-permute-start.12 = (bf16[1,64,2048]{2,1,0:T(8,128)(2,1)S(1)}, bf16[1,64,2048]{2,1,0:T(8,128)(2,1)S(1)}, u32[]{:S(2)}, u32[]{:S(2)}) collective-permute-start(bf16[1,64,2048]{2,1,0:T(8,128)(2,1)S(1)} %get-tuple-element.160), channel_id=1, source_target_pairs={{0,16},{4,20},{8,24},{12,28},{16,0},{20,4},{24,8},{28,12},{1,17},{... | collective-permute-start | bytes 786440 | tf_op jit(solution)/shard_map/ppermute | solution.py:715
  249.0 29.5 %collective-permute-start.11 = (bf16[2,64,2048]{2,1,0:T(8,128)(2,1)S(1)}, bf16[2,64,2048]{2,1,0:T(8,128)(2,1)S(1)}, u32[]{:S(2)}, u32[]{:S(2)}) collective-permute-start(bf16[2,64,2048]{2,1,0:T(8,128)(2,1)S(1)} %pad_maximum_fusion.14), channel_id=1, source_target_pairs={{0,16},{4,20},{8,24},{12,28},{16,0},{20,4},{24,8},{28,12},{1,17},{... | collective-permute-start | bytes 1572872 | tf_op jit(solution)/shard_map/ppermute | solution.py:715
  254.0 14.9 %collective-permute-start.18 = (bf16[2,64,2048]{2,1,0:T(8,128)(2,1)S(1)}, bf16[2,64,2048]{2,1,0:T(8,128)(2,1)S(1)}, u32[]{:S(2)}, u32[]{:S(2)}) collective-permute-start(bf16[2,64,2048]{2,1,0:T(8,128)(2,1)S(1)} %fusion.34), channel_id=1, source_target_pairs={{0,8},{4,12},{8,0},{12,4},{16,24},{20,28},{24,16},{28,20},{1,9},{5... | collective-permute-start | bytes 1572872 | tf_op jit(solution)/shard_map/ppermute | solution.py:715
  255.7 19.5 %collective-permute-start.16 = (bf16[2,64,2048]{2,1,0:T(8,128)(2,1)S(1)}, bf16[2,64,2048]{2,1,0:T(8,128)(2,1)S(1)}, u32[]{:S(2)}, u32[]{:S(2)}) collective-permute-start(bf16[2,64,2048]{2,1,0:T(8,128)(2,1)S(1)} %fusion.31), channel_id=1, source_target_pairs={{0,16},{4,20},{8,24},{12,28},{16,0},{20,4},{24,8},{28,12},{1,17},{... | collective-permute-start | bytes 1572872 | tf_op jit(solution)/shard_map/ppermute | solution.py:715
  257.2 39.7 %collective-permute-start.13 = (bf16[2,64,2048]{2,1,0:T(8,128)(2,1)}, bf16[2,64,2048]{2,1,0:T(8,128)(2,1)}, u32[]{:S(2)}, u32[]{:S(2)}) collective-permute-start(bf16[2,64,2048]{2,1,0:T(8,128)(2,1)} %pad_maximum_fusion.15), channel_id=1, source_target_pairs={{0,8},{4,12},{8,0},{12,4},{16,24},{20,28},{24,16},{28,20},{1,9},{5... | collective-permute-start | bytes 1572872 | tf_op jit(solution)/shard_map/ppermute | solution.py:715
  298.8 25.6 %collective-permute-start.14 = (bf16[2,4,64,2048]{3,2,1,0:T(8,128)(2,1)}, bf16[2,4,64,2048]{3,2,1,0:T(8,128)(2,1)}, u32[]{:S(2)}, u32[]{:S(2)}) collective-permute-start(bf16[2,4,64,2048]{3,2,1,0:T(8,128)(2,1)} %bitcast.377), channel_id=1, source_target_pairs={{0,4},{4,0},{8,12},{12,8},{16,20},{20,16},{24,28},{28,24},{1,5},{5... | collective-permute-start | bytes 6291464 | tf_op jit(solution)/shard_map/ppermute | solution.py:715
  323.8 102.3 %reduce-scatter.5.cloned.1.call-start = ((), (), s32[]{:S(2)}) async-start(), calls=%async_computation.13 | async-start | bytes 3604480 | tf_op jit(solution)/shard_map/reduce_scatter | solution.py:826
  364.8 176.3 %reduce-scatter.7.cloned.1.call-start = ((), (), s32[]{:S(2)}) async-start(), calls=%async_computation.14 | async-start | bytes 7208960 | tf_op jit(solution)/shard_map/reduce_scatter | solution.py:826
  392.3 255.0 %reduce-scatter.11.cloned.1.call-start = ((), (), s32[]{:S(2)}) async-start(), calls=%async_computation.16 | async-start | bytes 5242880 | tf_op jit(solution)/shard_map/reduce_scatter | solution.py:826
  437.0 14.7 %collective-permute-start.40 = (bf16[2,4,64,2048]{3,2,1,0:T(8,128)(2,1)S(1)}, bf16[2,4,64,2048]{3,2,1,0:T(8,128)(2,1)}, u32[]{:S(2)}, u32[]{:S(2)}) collective-permute-start(bf16[2,4,64,2048]{3,2,1,0:T(8,128)(2,1)S(1)} %bitcast.409), channel_id=1, source_target_pairs={{0,4},{4,0},{8,12},{12,8},{16,20},{20,16},{24,28},{28,24},{1,5},{5... | collective-permute-start | bytes 6291464 | tf_op jit(solution)/shard_map/ppermute | solution.py:715
  496.5 60.1 %collective-permute-start.42 = (bf16[64,2048]{1,0:T(8,128)(2,1)}, bf16[64,2048]{1,0:T(8,128)(2,1)S(1)}, u32[]{:S(2)}, u32[]{:S(2)}) collective-permute-start(bf16[64,2048]{1,0:T(8,128)(2,1)} %get-tuple-element.140), channel_id=1, source_target_pairs={{0,8},{4,12},{8,0},{12,4},{16,24},{20,28},{24,16},{28,20},{1,9},{5... | collective-permute-start | bytes 786440 | tf_op jit(solution)/shard_map/ppermute | solution.py:715
  497.0 59.6 %collective-permute-start.44 = (bf16[64,2048]{1,0:T(8,128)(2,1)S(1)}, bf16[64,2048]{1,0:T(8,128)(2,1)S(1)}, u32[]{:S(2)}, u32[]{:S(2)}) collective-permute-start(bf16[64,2048]{1,0:T(8,128)(2,1)S(1)} %get-tuple-element.139), channel_id=1, source_target_pairs={{0,16},{4,20},{8,24},{12,28},{16,0},{20,4},{24,8},{28,12},{1,17},{... | collective-permute-start | bytes 786440 | tf_op jit(solution)/shard_map/ppermute | solution.py:715
  497.6 53.5 %all-to-all-start.5 = ((bf16[8,64,704]{2,1,0:T(8,128)(2,1)}), bf16[8,64,704]{2,1,0:T(8,128)(2,1)S(1)}, u32[]{:S(2)}, u32[]{:S(2)}) async-start(bf16[8,64,704]{2,1,0:T(8,128)(2,1)} %bitcast.61), calls=%async_computation.9 | async-start | bytes 1572864 | tf_op jit(solution)/shard_map/all_to_all | solution.py:817
  551.0 54.0 %all-to-all-start.2 = ((bf16[4,8,64,1024]{3,2,0,1:T(8,128)(2,1)}), bf16[4,8,64,1024]{3,2,0,1:T(8,128)(2,1)}, u32[]{:S(2)}, u32[]{:S(2)}) async-start(bf16[4,8,64,1024]{3,2,0,1:T(8,128)(2,1)} %copy.124), calls=%async_computation.4 | async-start | bytes 8388608 | tf_op jit(solution)/shard_map/all_to_all | solution.py:976
  577.7 38.7 %collective-permute-start.35 = (bf16[2,4,64,2048]{3,2,1,0:T(8,128)(2,1)}, bf16[2,4,64,2048]{3,2,1,0:T(8,128)(2,1)}, u32[]{:S(2)}, u32[]{:S(2)}) collective-permute-start(bf16[2,4,64,2048]{3,2,1,0:T(8,128)(2,1)} %bitcast.74), channel_id=1, source_target_pairs={{0,4},{4,0},{8,12},{12,8},{16,20},{20,16},{24,28},{28,24},{1,5},{5... | collective-permute-start | bytes 6291464 | tf_op jit(solution)/shard_map/ppermute | solution.py:715
  588.7 25.7 %collective-permute-start.52 = (f32[1,12292]{1,0:T(1,128)S(1)}, f32[1,12292]{1,0:T(1,128)S(1)}, u32[]{:S(2)}, u32[]{:S(2)}) collective-permute-start(f32[1,12292]{1,0:T(1,128)S(1)} %broadcast_in_dim.15), channel_id=1, source_target_pairs={{0,4},{4,0},{8,12},{12,8},{16,20},{20,16},{24,28},{28,24},{1,5},{5... | collective-permute-start | bytes 147512 | tf_op jit(solution)/shard_map/ppermute | solution.py:715
  605.1 59.9 %all-to-all-start.4 = ((bf16[8,64,1408]{2,1,0:T(8,128)(2,1)}), bf16[8,64,1408]{2,1,0:T(8,128)(2,1)}, u32[]{:S(2)}, u32[]{:S(2)}) async-start(bf16[8,64,1408]{2,1,0:T(8,128)(2,1)} %bitcast.341), calls=%async_computation.8 | async-start | bytes 2883584 | tf_op jit(solution)/shard_map/all_to_all | solution.py:817
  609.3 82.0 %reduce-scatter.9.cloned.1.call-start = ((), (), s32[]{:S(2)}) async-start(), calls=%async_computation.15 | async-start | bytes 5242880 | tf_op jit(solution)/shard_map/reduce_scatter | solution.py:979
  614.5 16.1 %collective-permute-start.53 = (f32[2,12292]{1,0:T(2,128)S(1)}, f32[2,12292]{1,0:T(2,128)S(1)}, u32[]{:S(2)}, u32[]{:S(2)}) collective-permute-start(f32[2,12292]{1,0:T(2,128)S(1)} %pad_maximum_fusion.25), channel_id=1, source_target_pairs={{0,8},{4,12},{8,0},{12,4},{16,24},{20,28},{24,16},{28,20},{1,9},{5... | collective-permute-start | bytes 295016 | tf_op jit(solution)/shard_map/ppermute | solution.py:715
  617.9 23.5 %collective-permute-start.38 = (bf16[2,64,2048]{2,1,0:T(8,128)(2,1)S(1)}, bf16[2,64,2048]{2,1,0:T(8,128)(2,1)S(1)}, u32[]{:S(2)}, u32[]{:S(2)}) collective-permute-start(bf16[2,64,2048]{2,1,0:T(8,128)(2,1)S(1)} %fusion.35), channel_id=1, source_target_pairs={{0,8},{4,12},{8,0},{12,4},{16,24},{20,28},{24,16},{28,20},{1,9},{5... | collective-permute-start | bytes 1572872 | tf_op jit(solution)/shard_map/ppermute | solution.py:715
  619.6 24.2 %collective-permute-start.36 = (bf16[2,64,2048]{2,1,0:T(8,128)(2,1)S(1)}, bf16[2,64,2048]{2,1,0:T(8,128)(2,1)S(1)}, u32[]{:S(2)}, u32[]{:S(2)}) collective-permute-start(bf16[2,64,2048]{2,1,0:T(8,128)(2,1)S(1)} %fusion.28), channel_id=1, source_target_pairs={{0,16},{4,20},{8,24},{12,28},{16,0},{20,4},{24,8},{28,12},{1,17},{... | collective-permute-start | bytes 1572872 | tf_op jit(solution)/shard_map/ppermute | solution.py:715
  630.8 15.4 %collective-permute-start.54 = (f32[4,12292]{1,0:T(4,128)S(1)}, f32[4,12292]{1,0:T(4,128)S(1)}, u32[]{:S(2)}, u32[]{:S(2)}) collective-permute-start(f32[4,12292]{1,0:T(4,128)S(1)} %pad_maximum_fusion.22), channel_id=1, source_target_pairs={{0,16},{4,20},{8,24},{12,28},{16,0},{20,4},{24,8},{28,12},{1,17},{... | collective-permute-start | bytes 590024 | tf_op jit(solution)/shard_map/ppermute | solution.py:715
  664.9 18.9 %all-to-all-start.3 = ((bf16[8,64,1024]{2,1,0:T(8,128)(2,1)}), bf16[8,64,1024]{2,1,0:T(8,128)(2,1)S(1)}, u32[]{:S(2)}, u32[]{:S(2)}) async-start(bf16[8,64,1024]{2,1,0:T(8,128)(2,1)} %bitcast.86), calls=%async_computation.7 | async-start | bytes 2097152 | tf_op jit(solution)/shard_map/all_to_all | solution.py:817
  (112 other events, 1268.2 us)
Sparse Core Ops, SparseCore 0:
  10.2 48.9 all-gather.7
  60.7 119.2 all-gather.13
  182.1 33.0 all-gather.9
  217.2 105.5 all-gather.15
  324.8 33.2 all-gather.11
  364.9 55.0 reduce-scatter.4
  422.3 102.1 reduce-scatter.6
  526.7 79.5 reduce-scatter.10
  614.5 76.8 reduce-scatter.8

commit v4 on v3

--- a/solution.py
+++ b/solution.py
@@ -946,8 +946,9 @@
     h_ff = joined((even, odd))
     gate_up = mm(h_ff, gu_w)
     hidden_full, pull_glu = jax.vjp(glu_hidden, gate_up[:, :ff], gate_up[:, ff:])
-    hidden, down_rest = lax.optimization_barrier((hidden_full.astype(bf16), down_rest))
+    hidden = hidden_full.astype(bf16)
     down_grad = contract_rows(d_out, hidden).astype(bf16)
+    hidden, down_rest = lax.optimization_barrier((hidden, down_rest))
     down_own = summed(down_grad)
     d_hidden = contract_cols(d_out[:, : D // 2], down_first) + contract_cols(d_out[:, D // 2 :], down_rest)
     down_w = jnp.concatenate([down_first, down_rest], axis=1)
@@ -976,8 +977,9 @@
     mix_moved = lax.all_to_all(
         mix_grad.reshape(groups, size, own_rows, conv_cols), "seq", split_axis=1, concat_axis=1, tiled=True
     )
+    d_proj, d_small, g_conv_l, gu_own = after((d_proj, d_small, g_conv_l, gu_own), mix_grad)
+    mix_moved, gu_own = lax.optimization_barrier((mix_moved, gu_own))
     mix_grads = lax.psum_scatter(mix_moved, "batch", scatter_dimension=0, tiled=True)[0]
-    d_proj, d_small, g_conv_l, gu_own = after((d_proj, d_small, g_conv_l, gu_own), mix_grad)
     gu_grads, down_grads = exchanged(gu_own), exchanged(down_own)
     block_out = add_in_order(scatter_rows(*out_parts, "seq", False), residual, (size, groups))
     keep, send = parts(

time: 713 us -> 704 us (0.987)
  waiting for transfers between devices: 293 us -> 283 us
    ppermute x55, waiting for transfers between devices: 172 us -> 161 us  [swap(): lax.ppermute(value, axis, [(i, i ^ bit) for i in range(lax.axis_size(axis...]
  transfers between devices with their start and end apart: 69 -> 69, of which waited for: 46 -> 44; matrix products, arithmetic and copies ran while one was open for 26% -> 27% of each run, Pallas kernels for 14% -> 14%
where the time goes in v4:
time: 704 us; the launch traced here: 694 us
  waiting for transfers between devices  283 us (40%)
  matrix products  103 us (15%)
  Pallas kernels  99.1 us (14%)
  starting transfers between devices  72.4 us (10%)
  local copies, waits for them, and re-layouts  70.9 us (10%)
  blocking collectives  26.2 us (4%)
  other arithmetic  24.3 us (3%)
  between operations  15.6 us (2%)
    ppermute x55, waiting for transfers between devices, swap(): lax.ppermute(value, axis, [(i, i ^ bit) for i in range(lax.axis_size(axis...  161 us
    ppermute x55, starting transfers between devices, swap(): lax.ppermute(value, axis, [(i, i ^ bit) for i in range(lax.axis_size(axis...  50.9 us
    all_gather x2, waiting for transfers between devices, stacked(): full = lax.all_gather(blocks, 'batch', axis=0, tiled=False)  48.8 us
    pallas_call x1, Pallas kernels, mixer_backward(): pl.pallas_call(partial(backward_kernel, heads, chunks), grid_spec=pltpu.P...  39.3 us
    dot_general x7, matrix products, mm(): return jnp.dot(left, right, preferred_element_type=f32)  38 us
    dot_general x6, matrix products, contract_rows(): lax.dot_general(left, right, (((0,), (0,)), ((), ())), preferred_element_...  33.3 us
    dot_general x9, matrix products, contract_cols(): lax.dot_general(left, right, (((1,), (1,)), ((), ())), preferred_element_...  31.6 us
    all_to_all x1, blocking collectives, exchanged(): lax.all_to_all(packed, 'seq', split_axis=0, concat_axis=0, tiled=True)  26.2 us
  transfers between devices with their start and end apart: 69, of which 44 were waited for; matrix products, arithmetic and copies ran while one was open for 27% of the time, Pallas kernels for 14%

profile of v4, /device:TPU:0, one launch (start us, length us, event | category | flops | bytes accessed | tf_op | source)
XLA Modules:
  0.0 694.1 jit_solution(6733657591081778957)
XLA Ops:
  10.7 26.2 %all_to_all.30 = bf16[8,64,1536]{2,1,0:T(8,128)(2,1)} all-to-all(bf16[8,64,1536]{2,1,0:T(8,128)(2,1)S(1)} %copy.108), channel_id=1, replica_groups=mesh['seq'=8,'batch'=4] {'seq'}, dimensions={0} | all-to-all | bytes 3145728 | tf_op jit(solution)/shard_map/all_to_all | solution.py:817
  36.9 22.3 %all-gather.8.cloned.1.call-done = bf16[512,2048]{0,1:T(8,128)(2,1)} async-done(((bf16[128,2048]{0,1:T(8,128)(2,1)}), bf16[512,2048]{0,1:T(8,128)(2,1)}) %all-gather.8.cloned.1.call-update) | async-done | bytes 2097168 | tf_op jit(solution)/shard_map/all_gather | solution.py:867
  66.0 5.1 collective-permute-done
  76.0 8.3 %collective-permute-done.1 = bf16[2,64,2048]{2,1,0:T(8,128)(2,1)S(1)} collective-permute-done((bf16[2,64,2048]{2,1,0:T(8,128)(2,1)S(1)}, bf16[2,64,2048]{2,1,0:T(8,128)(2,1)S(1)}, u32[]{:S(2)}, u32[]{:S(2)}) %collective-permute-start.1) | collective-permute-done | bytes 524320 | tf_op jit(solution)/shard_map/ppermute | solution.py:715
  110.5 8.6 %collective-permute-done.8 = bf16[1,8,64,32]{2,3,1,0:T(8,128)(2,1)S(1)} collective-permute-done((bf16[1,8,64,32]{2,3,1,0:T(8,128)(2,1)S(1)}, bf16[1,8,64,32]{2,3,1,0:T(8,128)(2,1)S(1)}, u32[]{:S(2)}, u32[]{:S(2)}) %collective-permute-start.8) | collective-permute-done | bytes 32800 | tf_op jit(solution)/shard_map/ppermute | solution.py:715
  124.8 10.6 %collective-permute-done.9 = bf16[2,8,64,32]{2,3,1,0:T(8,128)(2,1)S(1)} collective-permute-done((bf16[2,8,64,32]{2,3,1,0:T(8,128)(2,1)S(1)}, bf16[2,8,64,32]{2,3,1,0:T(8,128)(2,1)S(1)}, u32[]{:S(2)}, u32[]{:S(2)}) %collective-permute-start.9) | collective-permute-done | bytes 65568 | tf_op jit(solution)/shard_map/ppermute | solution.py:715
  140.8 39.2 %all-gather.14.cloned.1.call-done = bf16[32,64,1536]{2,1,0:T(8,128)(2,1)} async-done(((bf16[8,64,1536]{2,1,0:T(8,128)(2,1)}), bf16[32,64,1536]{2,1,0:T(8,128)(2,1)}) %all-gather.14.cloned.1.call-update) | async-done | bytes 6291472 | tf_op jit(solution)/shard_map/all_gather | solution.py:821
  180.0 11.8 %fusion.77.gate_ref = f32[1024,1536]{1,0:T(8,128)} fusion(bf16[2048,1536]{1,0:T(8,128)(2,1)} %bitcast.398, bf16[512,2048]{1,0:T(8,128)(2,1)} %bitcast.6, bf16[512,2048]{1,0:T(8,128)(2,1)} %bitcast.389), kind=kOutput, calls=%fused_computation.231 | convolution fusion | flops 6450839552 | bytes 16777216 | tf_op jit(solution)/shard_map/dot_general | solution.py:797
  191.7 16.1 %delta_prepare.1 = (f32[8,4,128,128]{3,2,1,0:T(8,128)}, f32[8,4,64,256]{3,2,1,0:T(8,128)}, f32[8,4,64,64]{3,2,1,0:T(8,128)}, f32[8,4,64,64]{3,2,1,0:T(8,128)}, f32[8,4,64,128]{3,2,1,0:T(8,128)}) custom-call(s32[8]{0:T(128)} %iota_xor_fusion.pos_ref, s32[2]{0:T(128)} %reset_ref.3, f32[2,2,4,64,1536]{4,3,2,1,0:T(8,128)} %bitcast.294, ...), custom_call_target="tpu_custom_call" | custom-call | flops 30000001024 | bytes 40000000 | tf_op jit(solution)/shard_map/delta_prepare/pallas_call | solution.py:403
  207.9 7.3 %all-gather.10.cloned.1.call-done = bf16[704,1024]{1,0:T(8,128)(2,1)} async-done(((bf16[176,1024]{1,0:T(8,128)(2,1)}), bf16[704,1024]{1,0:T(8,128)(2,1)}) %all-gather.10.cloned.1.call-update) | async-done | bytes 1441808 | tf_op jit(solution)/shard_map/all_gather | solution.py:928
  217.3 12.6 %delta_scan.1 = (f32[2,2,4,64,512]{4,3,2,1,0:T(8,128)}, f32[8,4,128,256]{3,2,1,0:T(8,128)}, f32[8,4,64,256]{3,2,1,0:T(8,128)}) custom-call(s32[8]{0:T(128)} %iota_xor_fusion.pos_ref, f32[8,4,128,128]{3,2,1,0:T(8,128)} %get-tuple-element.86.both_ref, f32[8,4,64,256]{3,2,1,0:T(8,128)} %get-tuple-element.87.value_ref, ...), custom_call_target="tpu_custom_call" | custom-call | flops 1000000 | bytes 1000 | tf_op jit(solution)/shard_map/delta_scan/pallas_call | solution.py:423
  242.6 5.3 collective-permute-done.10
  257.7 11.2 %collective-permute-done.18.refs_4_ = bf16[2,64,2048]{2,1,0:T(8,128)(2,1)S(1)} collective-permute-done((bf16[2,64,2048]{2,1,0:T(8,128)(2,1)S(1)}, bf16[2,64,2048]{2,1,0:T(8,128)(2,1)S(1)}, u32[]{:S(2)}, u32[]{:S(2)}) %collective-permute-start.18) | collective-permute-done | bytes 524320 | tf_op jit(solution)/shard_map/ppermute | solution.py:715
  269.7 5.5 collective-permute-done.16.refs_2_
  301.1 9.0 %collective-permute-done.21 = bf16[2,64,2048]{2,1,0:T(8,128)(2,1)S(1)} collective-permute-done((bf16[2,64,2048]{2,1,0:T(8,128)(2,1)S(1)}, bf16[2,64,2048]{2,1,0:T(8,128)(2,1)S(1)}, u32[]{:S(2)}, u32[]{:S(2)}) %collective-permute-start.21) | collective-permute-done | bytes 524320 | tf_op jit(solution)/shard_map/ppermute | solution.py:715
  313.3 9.6 %all-gather.16.cloned.1.call-done = bf16[32,64,1408]{2,1,0:T(8,128)(2,1)} async-done(((bf16[8,64,1408]{2,1,0:T(8,128)(2,1)}), bf16[32,64,1408]{2,1,0:T(8,128)(2,1)}) %all-gather.16.cloned.1.call-update) | async-done | bytes 5767184 | tf_op jit(solution)/shard_map/all_gather | solution.py:821
  327.1 10.1 %fusion.76 = f32[1024,1408]{0,1:T(8,128)S(1)} fusion(bf16[2048,1408]{1,0:T(8,128)(2,1)} %bitcast.403, bf16[512,2048]{1,0:T(8,128)(2,1)} %bitcast.47, bf16[512,2048]{1,0:T(8,128)(2,1)S(1)} %bitcast.324), kind=kOutput, calls=%fused_computation.230 | convolution fusion | flops 5913968640 | bytes 15728640 | tf_op jit(solution)/shard_map/dot_general | solution.py:797
  340.4 6.1 fusion.1
  346.7 11.4 %all-gather.12.cloned.1.call-done = bf16[704,1024]{1,0:T(8,128)(2,1)} async-done(((bf16[176,1024]{1,0:T(8,128)(2,1)}), bf16[704,1024]{1,0:T(8,128)(2,1)}) %all-gather.12.cloned.1.call-update) | async-done | bytes 1441808 | tf_op jit(solution)/shard_map/all_gather | solution.py:931
  376.4 8.5 %convolution_convert_fusion = bf16[2048,1408]{1,0:T(8,128)(2,1)} fusion(bf16[1024,2048]{1,0:T(8,128)(2,1)S(1)} %pad_maximum_fusion.3, bf16[1024,704]{0,1:T(8,128)(2,1)S(1)} %get-tuple-element.141, bf16[1024,704]{0,1:T(8,128)(2,1)S(1)} %get-tuple-element.142), kind=kOutput, calls=%fused_computation.3 | convolution fusion | flops 5914230784 | bytes 12845056 | tf_op jit(solution)/shard_map/dot_general | solution.py:801
  396.4 7.6 %collective-permute-done.26.refs_2_ = bf16[2,64,2048]{2,1,0:T(8,128)(2,1)S(1)} collective-permute-done((bf16[2,64,2048]{2,1,0:T(8,128)(2,1)S(1)}, bf16[2,64,2048]{2,1,0:T(8,128)(2,1)S(1)}, u32[]{:S(2)}, u32[]{:S(2)}) %collective-permute-start.26) | collective-permute-done | bytes 524320 | tf_op jit(solution)/shard_map/ppermute | solution.py:715
  423.6 5.2 collective-permute-done.30
  432.8 7.7 %collective-permute-done.31 = bf16[2,64,2048]{2,1,0:T(8,128)(2,1)S(1)} collective-permute-done((bf16[2,64,2048]{2,1,0:T(8,128)(2,1)S(1)}, bf16[2,64,2048]{2,1,0:T(8,128)(2,1)S(1)}, u32[]{:S(2)}, u32[]{:S(2)}) %collective-permute-start.31) | collective-permute-done | bytes 524320 | tf_op jit(solution)/shard_map/ppermute | solution.py:715
  453.3 5.9 gated_norm_back.1
  473.6 12.0 %collective-permute-done.41.refs_2_ = bf16[2,64,2048]{2,1,0:T(8,128)(2,1)S(1)} collective-permute-done((bf16[2,64,2048]{2,1,0:T(8,128)(2,1)S(1)}, bf16[2,64,2048]{2,1,0:T(8,128)(2,1)S(1)}, u32[]{:S(2)}, u32[]{:S(2)}) %collective-permute-start.41) | collective-permute-done | bytes 524320 | tf_op jit(solution)/shard_map/ppermute | solution.py:715
  494.6 39.3 %delta_backward.1 = (bf16[2,2,4,64,1024]{4,3,2,1,0:T(8,128)(2,1)}, bf16[2,2,4,64,128]{4,3,2,1,0:T(8,128)(2,1)}, f32[8,1024]{1,0:T(8,128)}, f32[8,128]{1,0:T(8,128)}) custom-call(s32[8]{0:T(128)} %iota_xor_fusion.pos_ref, s32[2]{0:T(128)} %reset_ref.3, f32[2,2,4,64,1536]{4,3,2,1,0:T(8,128)} %bitcast.297, f32[2,2,4,64,128]{4,3,2,1,0:T(8,128)} %bitcast.416, ...), custom_call_target="tpu_custom_call" | custom-call | flops 30000001024 | bytes 40000000 | tf_op jit(solution)/shard_map/delta_backward/pallas_call | solution.py:464
  534.0 7.4 %convolution_convert_fusion.1 = bf16[2048,1024]{1,0:T(8,128)(2,1)S(1)} fusion(bf16[1024,1024]{1,0:T(8,128)(2,1)} %bitcast.331, bf16[512,2048]{1,0:T(8,128)(2,1)} %bitcast.6, bf16[512,2048]{1,0:T(8,128)(2,1)} %bitcast.390), kind=kOutput, calls=%fused_computation.17 | convolution fusion | flops 4305453056 | bytes 10485760 | tf_op jit(solution)/shard_map/dot_general | solution.py:801
  562.4 6.3 fusion.16
  582.3 15.4 %all-to-all-done.2 = bf16[4,8,64,1024]{3,2,0,1:T(8,128)(2,1)} async-done(((bf16[4,8,64,1024]{3,2,0,1:T(8,128)(2,1)}), bf16[4,8,64,1024]{3,2,0,1:T(8,128)(2,1)}, u32[]{:S(2)}, u32[]{:S(2)}) %all-to-all-start.2) | async-done | bytes 4194336 | tf_op jit(solution)/shard_map/all_to_all | solution.py:977
  610.6 8.2 %collective-permute-done.38.refs_4_ = bf16[2,64,2048]{2,1,0:T(8,128)(2,1)S(1)} collective-permute-done((bf16[2,64,2048]{2,1,0:T(8,128)(2,1)S(1)}, bf16[2,64,2048]{2,1,0:T(8,128)(2,1)S(1)}, u32[]{:S(2)}, u32[]{:S(2)}) %collective-permute-start.38) | collective-permute-done | bytes 524320 | tf_op jit(solution)/shard_map/ppermute | solution.py:715
  641.4 6.4 collective-permute-done.46
  669.5 13.3 %reduce-scatter.9.cloned.1.call-done = bf16[1,8,64,1024]{3,2,1,0:T(8,128)(2,1)} async-done(((bf16[4,8,64,1024]{3,2,1,0:T(8,128)(2,1)}), bf16[1,8,64,1024]{3,2,1,0:T(8,128)(2,1)}) %reduce-scatter.9.cloned.1.call-update) | async-done | bytes 1048592 | tf_op jit(solution)/shard_map/reduce_scatter | solution.py:982
  (469 shorter events, 299.3 us)
Async XLA Ops:
  7.2 51.9 %all-gather.8.cloned.1.call-start = ((), (), s32[]{:S(2)}) async-start(), calls=%async_computation.10 | async-start | bytes 2621440 | tf_op jit(solution)/shard_map/all_gather | solution.py:867
  9.4 170.6 %all-gather.14.cloned.1.call-start = ((), (), s32[]{:S(2)}) async-start(), calls=%async_computation.17 | async-start | bytes 7864320 | tf_op jit(solution)/shard_map/all_gather | solution.py:821
  88.7 47.8 %collective-permute-start.4 = (bf16[2,4,64,2048]{3,2,1,0:T(8,128)(2,1)}, bf16[2,4,64,2048]{3,2,1,0:T(8,128)(2,1)}, u32[]{:S(2)}, u32[]{:S(2)}) collective-permute-start(bf16[2,4,64,2048]{3,2,1,0:T(8,128)(2,1)} %bitcast.387), channel_id=1, source_target_pairs={{0,4},{4,0},{8,12},{12,8},{16,20},{20,16},{24,28},{28,24},{1,5},{5... | collective-permute-start | bytes 6291464 | tf_op jit(solution)/shard_map/ppermute | solution.py:715
  119.1 16.3 %collective-permute-start.9 = (bf16[2,8,64,32]{2,3,1,0:T(8,128)(2,1)S(1)}, bf16[2,8,64,32]{2,3,1,0:T(8,128)(2,1)S(1)}, u32[]{:S(2)}, u32[]{:S(2)}) collective-permute-start(bf16[2,8,64,32]{2,3,1,0:T(8,128)(2,1)S(1)} %pad_maximum_fusion.23), channel_id=1, source_target_pairs={{0,2},{1,3},{2,0},{3,1},{4,6},{5,7},{6,4},{7,5},{8,10},{9,11},{10,... | collective-permute-start | bytes 196616 | tf_op jit(solution)/shard_map/ppermute | solution.py:715
  120.2 87.7 %all-to-all-start.1 = ((bf16[8,64,1408]{2,1,0:T(8,128)(2,1)}), bf16[8,64,1408]{2,1,0:T(8,128)(2,1)S(1)}, u32[]{:S(2)}, u32[]{:S(2)}) async-start(bf16[8,64,1408]{2,1,0:T(8,128)(2,1)} %reshape.473), calls=%async_computation.1 | async-start | bytes 2883584 | tf_op jit(solution)/shard_map/all_to_all | solution.py:817
  123.8 91.4 %all-gather.10.cloned.1.call-start = ((), (), s32[]{:S(2)}) async-start(), calls=%async_computation.11 | async-start | bytes 1802240 | tf_op jit(solution)/shard_map/all_gather | solution.py:928
  124.6 198.3 %all-gather.16.cloned.1.call-start = ((), (), s32[]{:S(2)}) async-start(), calls=%async_computation.18 | async-start | bytes 7208960 | tf_op jit(solution)/shard_map/all_gather | solution.py:821
  215.2 142.9 %all-gather.12.cloned.1.call-start = ((), (), s32[]{:S(2)}) async-start(), calls=%async_computation.12 | async-start | bytes 1802240 | tf_op jit(solution)/shard_map/all_gather | solution.py:931
  238.0 15.8 %collective-permute-start.15 = (bf16[2,4,64,2048]{3,2,1,0:T(8,128)(2,1)}, bf16[2,4,64,2048]{3,2,1,0:T(8,128)(2,1)S(1)}, u32[]{:S(2)}, u32[]{:S(2)}) collective-permute-start(bf16[2,4,64,2048]{3,2,1,0:T(8,128)(2,1)} %bitcast.29), channel_id=1, source_target_pairs={{0,4},{4,0},{8,12},{12,8},{16,20},{20,16},{24,28},{28,24},{1,5},{5... | collective-permute-start | bytes 6291464 | tf_op jit(solution)/shard_map/ppermute | solution.py:715
  241.1 15.2 %collective-permute-start.12 = (bf16[1,64,2048]{2,1,0:T(8,128)(2,1)S(1)}, bf16[1,64,2048]{2,1,0:T(8,128)(2,1)S(1)}, u32[]{:S(2)}, u32[]{:S(2)}) collective-permute-start(bf16[1,64,2048]{2,1,0:T(8,128)(2,1)S(1)} %get-tuple-element.164), channel_id=1, source_target_pairs={{0,16},{4,20},{8,24},{12,28},{16,0},{20,4},{24,8},{28,12},{1,17},{... | collective-permute-start | bytes 786440 | tf_op jit(solution)/shard_map/ppermute | solution.py:715
  249.0 29.5 %collective-permute-start.11 = (bf16[2,64,2048]{2,1,0:T(8,128)(2,1)S(1)}, bf16[2,64,2048]{2,1,0:T(8,128)(2,1)S(1)}, u32[]{:S(2)}, u32[]{:S(2)}) collective-permute-start(bf16[2,64,2048]{2,1,0:T(8,128)(2,1)S(1)} %pad_maximum_fusion.14), channel_id=1, source_target_pairs={{0,16},{4,20},{8,24},{12,28},{16,0},{20,4},{24,8},{28,12},{1,17},{... | collective-permute-start | bytes 1572872 | tf_op jit(solution)/shard_map/ppermute | solution.py:715
  254.0 14.9 %collective-permute-start.18 = (bf16[2,64,2048]{2,1,0:T(8,128)(2,1)S(1)}, bf16[2,64,2048]{2,1,0:T(8,128)(2,1)S(1)}, u32[]{:S(2)}, u32[]{:S(2)}) collective-permute-start(bf16[2,64,2048]{2,1,0:T(8,128)(2,1)S(1)} %fusion.34), channel_id=1, source_target_pairs={{0,8},{4,12},{8,0},{12,4},{16,24},{20,28},{24,16},{28,20},{1,9},{5... | collective-permute-start | bytes 1572872 | tf_op jit(solution)/shard_map/ppermute | solution.py:715
  255.7 19.5 %collective-permute-start.16 = (bf16[2,64,2048]{2,1,0:T(8,128)(2,1)S(1)}, bf16[2,64,2048]{2,1,0:T(8,128)(2,1)S(1)}, u32[]{:S(2)}, u32[]{:S(2)}) collective-permute-start(bf16[2,64,2048]{2,1,0:T(8,128)(2,1)S(1)} %fusion.31), channel_id=1, source_target_pairs={{0,16},{4,20},{8,24},{12,28},{16,0},{20,4},{24,8},{28,12},{1,17},{... | collective-permute-start | bytes 1572872 | tf_op jit(solution)/shard_map/ppermute | solution.py:715
  257.2 39.7 %collective-permute-start.13 = (bf16[2,64,2048]{2,1,0:T(8,128)(2,1)}, bf16[2,64,2048]{2,1,0:T(8,128)(2,1)}, u32[]{:S(2)}, u32[]{:S(2)}) collective-permute-start(bf16[2,64,2048]{2,1,0:T(8,128)(2,1)} %pad_maximum_fusion.15), channel_id=1, source_target_pairs={{0,8},{4,12},{8,0},{12,4},{16,24},{20,28},{24,16},{28,20},{1,9},{5... | collective-permute-start | bytes 1572872 | tf_op jit(solution)/shard_map/ppermute | solution.py:715
  298.8 25.6 %collective-permute-start.14 = (bf16[2,4,64,2048]{3,2,1,0:T(8,128)(2,1)}, bf16[2,4,64,2048]{3,2,1,0:T(8,128)(2,1)}, u32[]{:S(2)}, u32[]{:S(2)}) collective-permute-start(bf16[2,4,64,2048]{3,2,1,0:T(8,128)(2,1)} %bitcast.376), channel_id=1, source_target_pairs={{0,4},{4,0},{8,12},{12,8},{16,20},{20,16},{24,28},{28,24},{1,5},{5... | collective-permute-start | bytes 6291464 | tf_op jit(solution)/shard_map/ppermute | solution.py:715
  323.8 95.0 %reduce-scatter.5.cloned.1.call-start = ((), (), s32[]{:S(2)}) async-start(), calls=%async_computation.13 | async-start | bytes 3604480 | tf_op jit(solution)/shard_map/reduce_scatter | solution.py:826
  346.5 187.4 %reduce-scatter.7.cloned.1.call-start = ((), (), s32[]{:S(2)}) async-start(), calls=%async_computation.14 | async-start | bytes 7208960 | tf_op jit(solution)/shard_map/reduce_scatter | solution.py:826
  384.9 245.8 %reduce-scatter.11.cloned.1.call-start = ((), (), s32[]{:S(2)}) async-start(), calls=%async_computation.16 | async-start | bytes 5242880 | tf_op jit(solution)/shard_map/reduce_scatter | solution.py:826
  390.0 14.0 %collective-permute-start.26 = (bf16[2,64,2048]{2,1,0:T(8,128)(2,1)S(1)}, bf16[2,64,2048]{2,1,0:T(8,128)(2,1)S(1)}, u32[]{:S(2)}, u32[]{:S(2)}) collective-permute-start(bf16[2,64,2048]{2,1,0:T(8,128)(2,1)S(1)} %get-tuple-element.152), channel_id=1, source_target_pairs={{0,16},{4,20},{8,24},{12,28},{16,0},{20,4},{24,8},{28,12},{1,17},{... | collective-permute-start | bytes 1572872 | tf_op jit(solution)/shard_map/ppermute | solution.py:715
  429.5 14.7 %collective-permute-start.40 = (bf16[2,4,64,2048]{3,2,1,0:T(8,128)(2,1)S(1)}, bf16[2,4,64,2048]{3,2,1,0:T(8,128)(2,1)}, u32[]{:S(2)}, u32[]{:S(2)}) collective-permute-start(bf16[2,4,64,2048]{3,2,1,0:T(8,128)(2,1)S(1)} %bitcast.408), channel_id=1, source_target_pairs={{0,4},{4,0},{8,12},{12,8},{16,20},{20,16},{24,28},{28,24},{1,5},{5... | collective-permute-start | bytes 6291464 | tf_op jit(solution)/shard_map/ppermute | solution.py:715
  471.7 14.0 %collective-permute-start.41 = (bf16[2,64,2048]{2,1,0:T(8,128)(2,1)S(1)}, bf16[2,64,2048]{2,1,0:T(8,128)(2,1)S(1)}, u32[]{:S(2)}, u32[]{:S(2)}) collective-permute-start(bf16[2,64,2048]{2,1,0:T(8,128)(2,1)S(1)} %get-tuple-element.148), channel_id=1, source_target_pairs={{0,16},{4,20},{8,24},{12,28},{16,0},{20,4},{24,8},{28,12},{1,17},{... | collective-permute-start | bytes 1572872 | tf_op jit(solution)/shard_map/ppermute | solution.py:715
  489.1 60.4 %collective-permute-start.42 = (bf16[64,2048]{1,0:T(8,128)(2,1)}, bf16[64,2048]{1,0:T(8,128)(2,1)S(1)}, u32[]{:S(2)}, u32[]{:S(2)}) collective-permute-start(bf16[64,2048]{1,0:T(8,128)(2,1)} %get-tuple-element.144), channel_id=1, source_target_pairs={{0,8},{4,12},{8,0},{12,4},{16,24},{20,28},{24,16},{28,20},{1,9},{5... | collective-permute-start | bytes 786440 | tf_op jit(solution)/shard_map/ppermute | solution.py:715
  489.5 59.9 %collective-permute-start.44 = (bf16[64,2048]{1,0:T(8,128)(2,1)S(1)}, bf16[64,2048]{1,0:T(8,128)(2,1)S(1)}, u32[]{:S(2)}, u32[]{:S(2)}) collective-permute-start(bf16[64,2048]{1,0:T(8,128)(2,1)S(1)} %get-tuple-element.143), channel_id=1, source_target_pairs={{0,16},{4,20},{8,24},{12,28},{16,0},{20,4},{24,8},{28,12},{1,17},{... | collective-permute-start | bytes 786440 | tf_op jit(solution)/shard_map/ppermute | solution.py:715
  490.6 53.2 %all-to-all-start.5 = ((bf16[8,64,704]{2,1,0:T(8,128)(2,1)}), bf16[8,64,704]{2,1,0:T(8,128)(2,1)S(1)}, u32[]{:S(2)}, u32[]{:S(2)}) async-start(bf16[8,64,704]{2,1,0:T(8,128)(2,1)} %bitcast.61), calls=%async_computation.9 | async-start | bytes 1572864 | tf_op jit(solution)/shard_map/all_to_all | solution.py:817
  543.8 53.9 %all-to-all-start.2 = ((bf16[4,8,64,1024]{3,2,0,1:T(8,128)(2,1)}), bf16[4,8,64,1024]{3,2,0,1:T(8,128)(2,1)}, u32[]{:S(2)}, u32[]{:S(2)}) async-start(bf16[4,8,64,1024]{3,2,0,1:T(8,128)(2,1)} %copy.124), calls=%async_computation.4 | async-start | bytes 8388608 | tf_op jit(solution)/shard_map/all_to_all | solution.py:977
  548.5 134.3 %reduce-scatter.9.cloned.1.call-start = ((), (), s32[]{:S(2)}) async-start(), calls=%async_computation.15 | async-start | bytes 5242880 | tf_op jit(solution)/shard_map/reduce_scatter | solution.py:982
  570.7 32.7 %collective-permute-start.35 = (bf16[2,4,64,2048]{3,2,1,0:T(8,128)(2,1)}, bf16[2,4,64,2048]{3,2,1,0:T(8,128)(2,1)}, u32[]{:S(2)}, u32[]{:S(2)}) collective-permute-start(bf16[2,4,64,2048]{3,2,1,0:T(8,128)(2,1)} %bitcast.74), channel_id=1, source_target_pairs={{0,4},{4,0},{8,12},{12,8},{16,20},{20,16},{24,28},{28,24},{1,5},{5... | collective-permute-start | bytes 6291464 | tf_op jit(solution)/shard_map/ppermute | solution.py:715
  580.3 22.4 %collective-permute-start.52 = (f32[1,12292]{1,0:T(1,128)S(1)}, f32[1,12292]{1,0:T(1,128)S(1)}, u32[]{:S(2)}, u32[]{:S(2)}) collective-permute-start(f32[1,12292]{1,0:T(1,128)S(1)} %broadcast_in_dim.15), channel_id=1, source_target_pairs={{0,4},{4,0},{8,12},{12,8},{16,20},{20,16},{24,28},{28,24},{1,5},{5... | collective-permute-start | bytes 147512 | tf_op jit(solution)/shard_map/ppermute | solution.py:715
  607.6 14.9 %collective-permute-start.36 = (bf16[2,64,2048]{2,1,0:T(8,128)(2,1)S(1)}, bf16[2,64,2048]{2,1,0:T(8,128)(2,1)S(1)}, u32[]{:S(2)}, u32[]{:S(2)}) collective-permute-start(bf16[2,64,2048]{2,1,0:T(8,128)(2,1)S(1)} %fusion.28), channel_id=1, source_target_pairs={{0,16},{4,20},{8,24},{12,28},{16,0},{20,4},{24,8},{28,12},{1,17},{... | collective-permute-start | bytes 1572872 | tf_op jit(solution)/shard_map/ppermute | solution.py:715
  609.1 19.7 %collective-permute-start.54 = (f32[4,12292]{1,0:T(4,128)}, f32[4,12292]{1,0:T(4,128)}, u32[]{:S(2)}, u32[]{:S(2)}) collective-permute-start(f32[4,12292]{1,0:T(4,128)} %pad_maximum_fusion.22), channel_id=1, source_target_pairs={{0,16},{4,20},{8,24},{12,28},{16,0},{20,4},{24,8},{28,12},{1,17},{... | collective-permute-start | bytes 590024 | tf_op jit(solution)/shard_map/ppermute | solution.py:715
  624.9 24.4 %all-to-all-start.4 = ((bf16[8,64,1408]{2,1,0:T(8,128)(2,1)}), bf16[8,64,1408]{2,1,0:T(8,128)(2,1)S(1)}, u32[]{:S(2)}, u32[]{:S(2)}) async-start(bf16[8,64,1408]{2,1,0:T(8,128)(2,1)} %bitcast.341), calls=%async_computation.8 | async-start | bytes 2883584 | tf_op jit(solution)/shard_map/all_to_all | solution.py:817
  649.3 18.9 %all-to-all-start.3 = ((bf16[8,64,1024]{2,1,0:T(8,128)(2,1)}), bf16[8,64,1024]{2,1,0:T(8,128)(2,1)S(1)}, u32[]{:S(2)}, u32[]{:S(2)}) async-start(bf16[8,64,1024]{2,1,0:T(8,128)(2,1)} %bitcast.86), calls=%async_computation.7 | async-start | bytes 2097152 | tf_op jit(solution)/shard_map/all_to_all | solution.py:817
  (112 other events, 1256.8 us)
Sparse Core Ops, SparseCore 0:
  10.2 48.9 all-gather.7
  60.7 119.2 all-gather.13
  182.1 33.0 all-gather.9
  217.2 105.5 all-gather.15
  324.8 33.2 all-gather.11
  360.8 55.0 reduce-scatter.4
  418.2 102.1 reduce-scatter.6
  522.7 79.5 reduce-scatter.10
  604.6 78.0 reduce-scatter.8

commit v5 on v4

--- a/solution.py
+++ b/solution.py
@@ -889,7 +889,7 @@
         moved_mix,
     )
     d_halves = gather_rows(d_own, "seq", False)
-    small_all = gather_small(gather_small(w_small, "seq"), "batch").reshape(D, 2 * H)
+    small_all = gather_small(gather_small(w_small, "batch"), "seq").swapaxes(0, 1).reshape(D, 2 * H)
     small_w = jnp.pad(
         jnp.concatenate(
             [

time: 704 us -> 700 us (level)
    ppermute x55, waiting for transfers between devices: 161 us -> 151 us  [swap(): lax.ppermute(value, axis, [(i, i ^ bit) for i in range(lax.axis_size(axis...]
  transfers between devices with their start and end apart: 69 -> 69, of which waited for: 44 -> 43; matrix products, arithmetic and copies ran while one was open for 27% -> 27% of each run, Pallas kernels for 14% -> 14%
where the time goes in v5:
time: 700 us; the launch traced here: 689 us
  waiting for transfers between devices  278 us (40%)
  matrix products  103 us (15%)
  Pallas kernels  99.1 us (14%)
  starting transfers between devices  72.4 us (10%)
  local copies, waits for them, and re-layouts  71 us (10%)
  blocking collectives  26.2 us (4%)
  other arithmetic  24.3 us (3%)
  between operations  15.6 us (2%)
    ppermute x55, waiting for transfers between devices, swap(): lax.ppermute(value, axis, [(i, i ^ bit) for i in range(lax.axis_size(axis...  151 us
    all_gather x2, waiting for transfers between devices, stacked(): full = lax.all_gather(blocks, 'batch', axis=0, tiled=False)  53.7 us
    ppermute x55, starting transfers between devices, swap(): lax.ppermute(value, axis, [(i, i ^ bit) for i in range(lax.axis_size(axis...  51 us
    pallas_call x1, Pallas kernels, mixer_backward(): pl.pallas_call(partial(backward_kernel, heads, chunks), grid_spec=pltpu.P...  39.3 us
    dot_general x7, matrix products, mm(): return jnp.dot(left, right, preferred_element_type=f32)  38 us
    dot_general x6, matrix products, contract_rows(): lax.dot_general(left, right, (((0,), (0,)), ((), ())), preferred_element_...  33.3 us
    dot_general x9, matrix products, contract_cols(): lax.dot_general(left, right, (((1,), (1,)), ((), ())), preferred_element_...  31.6 us
    all_to_all x1, blocking collectives, exchanged(): lax.all_to_all(packed, 'seq', split_axis=0, concat_axis=0, tiled=True)  26.2 us
  transfers between devices with their start and end apart: 69, of which 43 were waited for; matrix products, arithmetic and copies ran while one was open for 27% of the time, Pallas kernels for 14%

profile of v5, /device:TPU:0, one launch (start us, length us, event | category | flops | bytes accessed | tf_op | source)
XLA Modules:
  0.0 689.2 jit_solution(1953766835783808322)
XLA Ops:
  10.7 26.2 %all_to_all.30 = bf16[8,64,1536]{2,1,0:T(8,128)(2,1)} all-to-all(bf16[8,64,1536]{2,1,0:T(8,128)(2,1)S(1)} %copy.108), channel_id=1, replica_groups=mesh['seq'=8,'batch'=4] {'seq'}, dimensions={0} | all-to-all | bytes 3145728 | tf_op jit(solution)/shard_map/all_to_all | solution.py:817
  36.9 22.3 %all-gather.8.cloned.1.call-done = bf16[512,2048]{0,1:T(8,128)(2,1)} async-done(((bf16[128,2048]{0,1:T(8,128)(2,1)}), bf16[512,2048]{0,1:T(8,128)(2,1)}) %all-gather.8.cloned.1.call-update) | async-done | bytes 2097168 | tf_op jit(solution)/shard_map/all_gather | solution.py:867
  66.0 5.1 collective-permute-done
  76.0 8.3 %collective-permute-done.1 = bf16[2,64,2048]{2,1,0:T(8,128)(2,1)S(1)} collective-permute-done((bf16[2,64,2048]{2,1,0:T(8,128)(2,1)S(1)}, bf16[2,64,2048]{2,1,0:T(8,128)(2,1)S(1)}, u32[]{:S(2)}, u32[]{:S(2)}) %collective-permute-start.1) | collective-permute-done | bytes 524320 | tf_op jit(solution)/shard_map/ppermute | solution.py:715
  100.2 6.7 collective-permute-done.5
  107.1 5.0 collective-permute-done.6
  130.9 44.1 %all-gather.14.cloned.1.call-done = bf16[32,64,1536]{2,1,0:T(8,128)(2,1)} async-done(((bf16[8,64,1536]{2,1,0:T(8,128)(2,1)}), bf16[32,64,1536]{2,1,0:T(8,128)(2,1)}) %all-gather.14.cloned.1.call-update) | async-done | bytes 6291472 | tf_op jit(solution)/shard_map/all_gather | solution.py:821
  175.0 11.8 %fusion.77.gate_ref = f32[1024,1536]{1,0:T(8,128)} fusion(bf16[2048,1536]{1,0:T(8,128)(2,1)} %bitcast.400, bf16[512,2048]{1,0:T(8,128)(2,1)} %bitcast.6, bf16[512,2048]{1,0:T(8,128)(2,1)} %bitcast.388), kind=kOutput, calls=%fused_computation.231 | convolution fusion | flops 6450839552 | bytes 16777216 | tf_op jit(solution)/shard_map/dot_general | solution.py:797
  186.8 16.2 %delta_prepare.1 = (f32[8,4,128,128]{3,2,1,0:T(8,128)}, f32[8,4,64,256]{3,2,1,0:T(8,128)}, f32[8,4,64,64]{3,2,1,0:T(8,128)}, f32[8,4,64,64]{3,2,1,0:T(8,128)}, f32[8,4,64,128]{3,2,1,0:T(8,128)}) custom-call(s32[8]{0:T(128)} %iota_xor_fusion.pos_ref, s32[2]{0:T(128)} %reset_ref.3, f32[2,2,4,64,1536]{4,3,2,1,0:T(8,128)} %bitcast.295, ...), custom_call_target="tpu_custom_call" | custom-call | flops 30000001024 | bytes 40000000 | tf_op jit(solution)/shard_map/delta_prepare/pallas_call | solution.py:403
  203.0 7.3 %all-gather.10.cloned.1.call-done = bf16[704,1024]{1,0:T(8,128)(2,1)} async-done(((bf16[176,1024]{1,0:T(8,128)(2,1)}), bf16[704,1024]{1,0:T(8,128)(2,1)}) %all-gather.10.cloned.1.call-update) | async-done | bytes 1441808 | tf_op jit(solution)/shard_map/all_gather | solution.py:928
  212.5 12.6 %delta_scan.1 = (f32[2,2,4,64,512]{4,3,2,1,0:T(8,128)}, f32[8,4,128,256]{3,2,1,0:T(8,128)}, f32[8,4,64,256]{3,2,1,0:T(8,128)}) custom-call(s32[8]{0:T(128)} %iota_xor_fusion.pos_ref, f32[8,4,128,128]{3,2,1,0:T(8,128)} %get-tuple-element.86.both_ref, f32[8,4,64,256]{3,2,1,0:T(8,128)} %get-tuple-element.87.value_ref, ...), custom_call_target="tpu_custom_call" | custom-call | flops 1000000 | bytes 1000 | tf_op jit(solution)/shard_map/delta_scan/pallas_call | solution.py:423
  237.7 5.3 collective-permute-done.10
  252.9 11.2 %collective-permute-done.18.refs_4_ = bf16[2,64,2048]{2,1,0:T(8,128)(2,1)S(1)} collective-permute-done((bf16[2,64,2048]{2,1,0:T(8,128)(2,1)S(1)}, bf16[2,64,2048]{2,1,0:T(8,128)(2,1)S(1)}, u32[]{:S(2)}, u32[]{:S(2)}) %collective-permute-start.18) | collective-permute-done | bytes 524320 | tf_op jit(solution)/shard_map/ppermute | solution.py:715
  264.8 5.5 collective-permute-done.16.refs_2_
  296.2 9.0 %collective-permute-done.21 = bf16[2,64,2048]{2,1,0:T(8,128)(2,1)S(1)} collective-permute-done((bf16[2,64,2048]{2,1,0:T(8,128)(2,1)S(1)}, bf16[2,64,2048]{2,1,0:T(8,128)(2,1)S(1)}, u32[]{:S(2)}, u32[]{:S(2)}) %collective-permute-start.21) | collective-permute-done | bytes 524320 | tf_op jit(solution)/shard_map/ppermute | solution.py:715
  308.4 9.6 %all-gather.16.cloned.1.call-done = bf16[32,64,1408]{2,1,0:T(8,128)(2,1)} async-done(((bf16[8,64,1408]{2,1,0:T(8,128)(2,1)}), bf16[32,64,1408]{2,1,0:T(8,128)(2,1)}) %all-gather.16.cloned.1.call-update) | async-done | bytes 5767184 | tf_op jit(solution)/shard_map/all_gather | solution.py:821
  322.2 10.1 %fusion.76 = f32[1024,1408]{0,1:T(8,128)S(1)} fusion(bf16[2048,1408]{1,0:T(8,128)(2,1)} %bitcast.405, bf16[512,2048]{1,0:T(8,128)(2,1)} %bitcast.48, bf16[512,2048]{1,0:T(8,128)(2,1)S(1)} %bitcast.325), kind=kOutput, calls=%fused_computation.230 | convolution fusion | flops 5913968640 | bytes 15728640 | tf_op jit(solution)/shard_map/dot_general | solution.py:797
  335.5 6.1 fusion.1
  341.8 11.4 %all-gather.12.cloned.1.call-done = bf16[704,1024]{1,0:T(8,128)(2,1)} async-done(((bf16[176,1024]{1,0:T(8,128)(2,1)}), bf16[704,1024]{1,0:T(8,128)(2,1)}) %all-gather.12.cloned.1.call-update) | async-done | bytes 1441808 | tf_op jit(solution)/shard_map/all_gather | solution.py:931
  371.5 8.5 %convolution_convert_fusion = bf16[2048,1408]{1,0:T(8,128)(2,1)} fusion(bf16[1024,2048]{1,0:T(8,128)(2,1)S(1)} %pad_maximum_fusion.3, bf16[1024,704]{0,1:T(8,128)(2,1)S(1)} %get-tuple-element.141, bf16[1024,704]{0,1:T(8,128)(2,1)S(1)} %get-tuple-element.142), kind=kOutput, calls=%fused_computation.3 | convolution fusion | flops 5914230784 | bytes 12845056 | tf_op jit(solution)/shard_map/dot_general | solution.py:801
  391.5 7.6 %collective-permute-done.26.refs_2_ = bf16[2,64,2048]{2,1,0:T(8,128)(2,1)S(1)} collective-permute-done((bf16[2,64,2048]{2,1,0:T(8,128)(2,1)S(1)}, bf16[2,64,2048]{2,1,0:T(8,128)(2,1)S(1)}, u32[]{:S(2)}, u32[]{:S(2)}) %collective-permute-start.26) | collective-permute-done | bytes 524320 | tf_op jit(solution)/shard_map/ppermute | solution.py:715
  418.7 5.3 collective-permute-done.30
  428.0 7.7 %collective-permute-done.31 = bf16[2,64,2048]{2,1,0:T(8,128)(2,1)S(1)} collective-permute-done((bf16[2,64,2048]{2,1,0:T(8,128)(2,1)S(1)}, bf16[2,64,2048]{2,1,0:T(8,128)(2,1)S(1)}, u32[]{:S(2)}, u32[]{:S(2)}) %collective-permute-start.31) | collective-permute-done | bytes 524320 | tf_op jit(solution)/shard_map/ppermute | solution.py:715
  448.4 5.9 gated_norm_back.1
  468.8 12.1 %collective-permute-done.41.refs_2_ = bf16[2,64,2048]{2,1,0:T(8,128)(2,1)S(1)} collective-permute-done((bf16[2,64,2048]{2,1,0:T(8,128)(2,1)S(1)}, bf16[2,64,2048]{2,1,0:T(8,128)(2,1)S(1)}, u32[]{:S(2)}, u32[]{:S(2)}) %collective-permute-start.41) | collective-permute-done | bytes 524320 | tf_op jit(solution)/shard_map/ppermute | solution.py:715
  489.7 39.3 %delta_backward.1 = (bf16[2,2,4,64,1024]{4,3,2,1,0:T(8,128)(2,1)}, bf16[2,2,4,64,128]{4,3,2,1,0:T(8,128)(2,1)}, f32[8,1024]{1,0:T(8,128)}, f32[8,128]{1,0:T(8,128)}) custom-call(s32[8]{0:T(128)} %iota_xor_fusion.pos_ref, s32[2]{0:T(128)} %reset_ref.3, f32[2,2,4,64,1536]{4,3,2,1,0:T(8,128)} %bitcast.298, f32[2,2,4,64,128]{4,3,2,1,0:T(8,128)} %bitcast.418, ...), custom_call_target="tpu_custom_call" | custom-call | flops 30000001024 | bytes 40000000 | tf_op jit(solution)/shard_map/delta_backward/pallas_call | solution.py:464
  529.1 7.4 %convolution_convert_fusion.1 = bf16[2048,1024]{1,0:T(8,128)(2,1)S(1)} fusion(bf16[1024,1024]{1,0:T(8,128)(2,1)} %bitcast.333, bf16[512,2048]{1,0:T(8,128)(2,1)} %bitcast.6, bf16[512,2048]{1,0:T(8,128)(2,1)} %bitcast.389), kind=kOutput, calls=%fused_computation.17 | convolution fusion | flops 4305453056 | bytes 10485760 | tf_op jit(solution)/shard_map/dot_general | solution.py:801
  557.5 6.3 fusion.16
  577.4 15.4 %all-to-all-done.2 = bf16[4,8,64,1024]{3,2,0,1:T(8,128)(2,1)} async-done(((bf16[4,8,64,1024]{3,2,0,1:T(8,128)(2,1)}), bf16[4,8,64,1024]{3,2,0,1:T(8,128)(2,1)}, u32[]{:S(2)}, u32[]{:S(2)}) %all-to-all-start.2) | async-done | bytes 4194336 | tf_op jit(solution)/shard_map/all_to_all | solution.py:977
  605.7 8.2 %collective-permute-done.38.refs_4_ = bf16[2,64,2048]{2,1,0:T(8,128)(2,1)S(1)} collective-permute-done((bf16[2,64,2048]{2,1,0:T(8,128)(2,1)S(1)}, bf16[2,64,2048]{2,1,0:T(8,128)(2,1)S(1)}, u32[]{:S(2)}, u32[]{:S(2)}) %collective-permute-start.38) | collective-permute-done | bytes 524320 | tf_op jit(solution)/shard_map/ppermute | solution.py:715
  636.5 6.4 collective-permute-done.46
  664.6 13.3 %reduce-scatter.9.cloned.1.call-done = bf16[1,8,64,1024]{3,2,1,0:T(8,128)(2,1)} async-done(((bf16[4,8,64,1024]{3,2,1,0:T(8,128)(2,1)}), bf16[1,8,64,1024]{3,2,1,0:T(8,128)(2,1)}) %reduce-scatter.9.cloned.1.call-update) | async-done | bytes 1048592 | tf_op jit(solution)/shard_map/reduce_scatter | solution.py:982
  (469 shorter events, 296.9 us)
Async XLA Ops:
  7.2 51.9 %all-gather.8.cloned.1.call-start = ((), (), s32[]{:S(2)}) async-start(), calls=%async_computation.10 | async-start | bytes 2621440 | tf_op jit(solution)/shard_map/all_gather | solution.py:867
  9.4 165.6 %all-gather.14.cloned.1.call-start = ((), (), s32[]{:S(2)}) async-start(), calls=%async_computation.17 | async-start | bytes 7864320 | tf_op jit(solution)/shard_map/all_gather | solution.py:821
  88.7 37.9 %collective-permute-start.4 = (bf16[2,4,64,2048]{3,2,1,0:T(8,128)(2,1)}, bf16[2,4,64,2048]{3,2,1,0:T(8,128)(2,1)}, u32[]{:S(2)}, u32[]{:S(2)}) collective-permute-start(bf16[2,4,64,2048]{3,2,1,0:T(8,128)(2,1)} %bitcast.386), channel_id=1, source_target_pairs={{0,4},{4,0},{8,12},{12,8},{16,20},{20,16},{24,28},{28,24},{1,5},{5... | collective-permute-start | bytes 6291464 | tf_op jit(solution)/shard_map/ppermute | solution.py:715
  120.9 82.1 %all-to-all-start.1 = ((bf16[8,64,1408]{2,1,0:T(8,128)(2,1)}), bf16[8,64,1408]{2,1,0:T(8,128)(2,1)S(1)}, u32[]{:S(2)}, u32[]{:S(2)}) async-start(bf16[8,64,1408]{2,1,0:T(8,128)(2,1)} %reshape.473), calls=%async_computation.1 | async-start | bytes 2883584 | tf_op jit(solution)/shard_map/all_to_all | solution.py:817
  124.5 85.9 %all-gather.10.cloned.1.call-start = ((), (), s32[]{:S(2)}) async-start(), calls=%async_computation.11 | async-start | bytes 1802240 | tf_op jit(solution)/shard_map/all_gather | solution.py:928
  125.2 192.8 %all-gather.16.cloned.1.call-start = ((), (), s32[]{:S(2)}) async-start(), calls=%async_computation.18 | async-start | bytes 7208960 | tf_op jit(solution)/shard_map/all_gather | solution.py:821
  210.3 142.9 %all-gather.12.cloned.1.call-start = ((), (), s32[]{:S(2)}) async-start(), calls=%async_computation.12 | async-start | bytes 1802240 | tf_op jit(solution)/shard_map/all_gather | solution.py:931
  233.1 15.8 %collective-permute-start.15 = (bf16[2,4,64,2048]{3,2,1,0:T(8,128)(2,1)}, bf16[2,4,64,2048]{3,2,1,0:T(8,128)(2,1)S(1)}, u32[]{:S(2)}, u32[]{:S(2)}) collective-permute-start(bf16[2,4,64,2048]{3,2,1,0:T(8,128)(2,1)} %bitcast.30), channel_id=1, source_target_pairs={{0,4},{4,0},{8,12},{12,8},{16,20},{20,16},{24,28},{28,24},{1,5},{5... | collective-permute-start | bytes 6291464 | tf_op jit(solution)/shard_map/ppermute | solution.py:715
  236.3 15.2 %collective-permute-start.12 = (bf16[1,64,2048]{2,1,0:T(8,128)(2,1)S(1)}, bf16[1,64,2048]{2,1,0:T(8,128)(2,1)S(1)}, u32[]{:S(2)}, u32[]{:S(2)}) collective-permute-start(bf16[1,64,2048]{2,1,0:T(8,128)(2,1)S(1)} %get-tuple-element.164), channel_id=1, source_target_pairs={{0,16},{4,20},{8,24},{12,28},{16,0},{20,4},{24,8},{28,12},{1,17},{... | collective-permute-start | bytes 786440 | tf_op jit(solution)/shard_map/ppermute | solution.py:715
  244.1 29.5 %collective-permute-start.11 = (bf16[2,64,2048]{2,1,0:T(8,128)(2,1)S(1)}, bf16[2,64,2048]{2,1,0:T(8,128)(2,1)S(1)}, u32[]{:S(2)}, u32[]{:S(2)}) collective-permute-start(bf16[2,64,2048]{2,1,0:T(8,128)(2,1)S(1)} %pad_maximum_fusion.14), channel_id=1, source_target_pairs={{0,16},{4,20},{8,24},{12,28},{16,0},{20,4},{24,8},{28,12},{1,17},{... | collective-permute-start | bytes 1572872 | tf_op jit(solution)/shard_map/ppermute | solution.py:715
  249.1 14.9 %collective-permute-start.18 = (bf16[2,64,2048]{2,1,0:T(8,128)(2,1)S(1)}, bf16[2,64,2048]{2,1,0:T(8,128)(2,1)S(1)}, u32[]{:S(2)}, u32[]{:S(2)}) collective-permute-start(bf16[2,64,2048]{2,1,0:T(8,128)(2,1)S(1)} %fusion.34), channel_id=1, source_target_pairs={{0,8},{4,12},{8,0},{12,4},{16,24},{20,28},{24,16},{28,20},{1,9},{5... | collective-permute-start | bytes 1572872 | tf_op jit(solution)/shard_map/ppermute | solution.py:715
  250.8 19.4 %collective-permute-start.16 = (bf16[2,64,2048]{2,1,0:T(8,128)(2,1)S(1)}, bf16[2,64,2048]{2,1,0:T(8,128)(2,1)S(1)}, u32[]{:S(2)}, u32[]{:S(2)}) collective-permute-start(bf16[2,64,2048]{2,1,0:T(8,128)(2,1)S(1)} %fusion.31), channel_id=1, source_target_pairs={{0,16},{4,20},{8,24},{12,28},{16,0},{20,4},{24,8},{28,12},{1,17},{... | collective-permute-start | bytes 1572872 | tf_op jit(solution)/shard_map/ppermute | solution.py:715
  252.3 39.6 %collective-permute-start.13 = (bf16[2,64,2048]{2,1,0:T(8,128)(2,1)}, bf16[2,64,2048]{2,1,0:T(8,128)(2,1)}, u32[]{:S(2)}, u32[]{:S(2)}) collective-permute-start(bf16[2,64,2048]{2,1,0:T(8,128)(2,1)} %pad_maximum_fusion.15), channel_id=1, source_target_pairs={{0,8},{4,12},{8,0},{12,4},{16,24},{20,28},{24,16},{28,20},{1,9},{5... | collective-permute-start | bytes 1572872 | tf_op jit(solution)/shard_map/ppermute | solution.py:715
  293.9 25.6 %collective-permute-start.14 = (bf16[2,4,64,2048]{3,2,1,0:T(8,128)(2,1)}, bf16[2,4,64,2048]{3,2,1,0:T(8,128)(2,1)}, u32[]{:S(2)}, u32[]{:S(2)}) collective-permute-start(bf16[2,4,64,2048]{3,2,1,0:T(8,128)(2,1)} %bitcast.375), channel_id=1, source_target_pairs={{0,4},{4,0},{8,12},{12,8},{16,20},{20,16},{24,28},{28,24},{1,5},{5... | collective-permute-start | bytes 6291464 | tf_op jit(solution)/shard_map/ppermute | solution.py:715
  319.0 95.0 %reduce-scatter.5.cloned.1.call-start = ((), (), s32[]{:S(2)}) async-start(), calls=%async_computation.13 | async-start | bytes 3604480 | tf_op jit(solution)/shard_map/reduce_scatter | solution.py:826
  341.6 187.5 %reduce-scatter.7.cloned.1.call-start = ((), (), s32[]{:S(2)}) async-start(), calls=%async_computation.14 | async-start | bytes 7208960 | tf_op jit(solution)/shard_map/reduce_scatter | solution.py:826
  380.0 245.8 %reduce-scatter.11.cloned.1.call-start = ((), (), s32[]{:S(2)}) async-start(), calls=%async_computation.16 | async-start | bytes 5242880 | tf_op jit(solution)/shard_map/reduce_scatter | solution.py:826
  385.1 14.0 %collective-permute-start.26 = (bf16[2,64,2048]{2,1,0:T(8,128)(2,1)S(1)}, bf16[2,64,2048]{2,1,0:T(8,128)(2,1)S(1)}, u32[]{:S(2)}, u32[]{:S(2)}) collective-permute-start(bf16[2,64,2048]{2,1,0:T(8,128)(2,1)S(1)} %get-tuple-element.152), channel_id=1, source_target_pairs={{0,16},{4,20},{8,24},{12,28},{16,0},{20,4},{24,8},{28,12},{1,17},{... | collective-permute-start | bytes 1572872 | tf_op jit(solution)/shard_map/ppermute | solution.py:715
  424.6 14.7 %collective-permute-start.40 = (bf16[2,4,64,2048]{3,2,1,0:T(8,128)(2,1)S(1)}, bf16[2,4,64,2048]{3,2,1,0:T(8,128)(2,1)}, u32[]{:S(2)}, u32[]{:S(2)}) collective-permute-start(bf16[2,4,64,2048]{3,2,1,0:T(8,128)(2,1)S(1)} %bitcast.410), channel_id=1, source_target_pairs={{0,4},{4,0},{8,12},{12,8},{16,20},{20,16},{24,28},{28,24},{1,5},{5... | collective-permute-start | bytes 6291464 | tf_op jit(solution)/shard_map/ppermute | solution.py:715
  466.8 14.0 %collective-permute-start.41 = (bf16[2,64,2048]{2,1,0:T(8,128)(2,1)S(1)}, bf16[2,64,2048]{2,1,0:T(8,128)(2,1)S(1)}, u32[]{:S(2)}, u32[]{:S(2)}) collective-permute-start(bf16[2,64,2048]{2,1,0:T(8,128)(2,1)S(1)} %get-tuple-element.148), channel_id=1, source_target_pairs={{0,16},{4,20},{8,24},{12,28},{16,0},{20,4},{24,8},{28,12},{1,17},{... | collective-permute-start | bytes 1572872 | tf_op jit(solution)/shard_map/ppermute | solution.py:715
  484.2 60.4 %collective-permute-start.42 = (bf16[64,2048]{1,0:T(8,128)(2,1)}, bf16[64,2048]{1,0:T(8,128)(2,1)S(1)}, u32[]{:S(2)}, u32[]{:S(2)}) collective-permute-start(bf16[64,2048]{1,0:T(8,128)(2,1)} %get-tuple-element.144), channel_id=1, source_target_pairs={{0,8},{4,12},{8,0},{12,4},{16,24},{20,28},{24,16},{28,20},{1,9},{5... | collective-permute-start | bytes 786440 | tf_op jit(solution)/shard_map/ppermute | solution.py:715
  484.6 59.9 %collective-permute-start.44 = (bf16[64,2048]{1,0:T(8,128)(2,1)S(1)}, bf16[64,2048]{1,0:T(8,128)(2,1)S(1)}, u32[]{:S(2)}, u32[]{:S(2)}) collective-permute-start(bf16[64,2048]{1,0:T(8,128)(2,1)S(1)} %get-tuple-element.143), channel_id=1, source_target_pairs={{0,16},{4,20},{8,24},{12,28},{16,0},{20,4},{24,8},{28,12},{1,17},{... | collective-permute-start | bytes 786440 | tf_op jit(solution)/shard_map/ppermute | solution.py:715
  485.7 53.2 %all-to-all-start.5 = ((bf16[8,64,704]{2,1,0:T(8,128)(2,1)}), bf16[8,64,704]{2,1,0:T(8,128)(2,1)S(1)}, u32[]{:S(2)}, u32[]{:S(2)}) async-start(bf16[8,64,704]{2,1,0:T(8,128)(2,1)} %bitcast.62), calls=%async_computation.9 | async-start | bytes 1572864 | tf_op jit(solution)/shard_map/all_to_all | solution.py:817
  538.9 53.9 %all-to-all-start.2 = ((bf16[4,8,64,1024]{3,2,0,1:T(8,128)(2,1)}), bf16[4,8,64,1024]{3,2,0,1:T(8,128)(2,1)}, u32[]{:S(2)}, u32[]{:S(2)}) async-start(bf16[4,8,64,1024]{3,2,0,1:T(8,128)(2,1)} %copy.124), calls=%async_computation.4 | async-start | bytes 8388608 | tf_op jit(solution)/shard_map/all_to_all | solution.py:977
  543.6 134.3 %reduce-scatter.9.cloned.1.call-start = ((), (), s32[]{:S(2)}) async-start(), calls=%async_computation.15 | async-start | bytes 5242880 | tf_op jit(solution)/shard_map/reduce_scatter | solution.py:982
  565.8 32.7 %collective-permute-start.35 = (bf16[2,4,64,2048]{3,2,1,0:T(8,128)(2,1)}, bf16[2,4,64,2048]{3,2,1,0:T(8,128)(2,1)}, u32[]{:S(2)}, u32[]{:S(2)}) collective-permute-start(bf16[2,4,64,2048]{3,2,1,0:T(8,128)(2,1)} %bitcast.75), channel_id=1, source_target_pairs={{0,4},{4,0},{8,12},{12,8},{16,20},{20,16},{24,28},{28,24},{1,5},{5... | collective-permute-start | bytes 6291464 | tf_op jit(solution)/shard_map/ppermute | solution.py:715
  575.4 22.4 %collective-permute-start.52 = (f32[1,12292]{1,0:T(1,128)S(1)}, f32[1,12292]{1,0:T(1,128)S(1)}, u32[]{:S(2)}, u32[]{:S(2)}) collective-permute-start(f32[1,12292]{1,0:T(1,128)S(1)} %broadcast_in_dim.15), channel_id=1, source_target_pairs={{0,4},{4,0},{8,12},{12,8},{16,20},{20,16},{24,28},{28,24},{1,5},{5... | collective-permute-start | bytes 147512 | tf_op jit(solution)/shard_map/ppermute | solution.py:715
  599.9 14.0 %collective-permute-start.38 = (bf16[2,64,2048]{2,1,0:T(8,128)(2,1)S(1)}, bf16[2,64,2048]{2,1,0:T(8,128)(2,1)S(1)}, u32[]{:S(2)}, u32[]{:S(2)}) collective-permute-start(bf16[2,64,2048]{2,1,0:T(8,128)(2,1)S(1)} %fusion.35), channel_id=1, source_target_pairs={{0,8},{4,12},{8,0},{12,4},{16,24},{20,28},{24,16},{28,20},{1,9},{5... | collective-permute-start | bytes 1572872 | tf_op jit(solution)/shard_map/ppermute | solution.py:715
  602.8 14.9 %collective-permute-start.36 = (bf16[2,64,2048]{2,1,0:T(8,128)(2,1)S(1)}, bf16[2,64,2048]{2,1,0:T(8,128)(2,1)S(1)}, u32[]{:S(2)}, u32[]{:S(2)}) collective-permute-start(bf16[2,64,2048]{2,1,0:T(8,128)(2,1)S(1)} %fusion.28), channel_id=1, source_target_pairs={{0,16},{4,20},{8,24},{12,28},{16,0},{20,4},{24,8},{28,12},{1,17},{... | collective-permute-start | bytes 1572872 | tf_op jit(solution)/shard_map/ppermute | solution.py:715
  604.2 19.7 %collective-permute-start.54 = (f32[4,12292]{1,0:T(4,128)}, f32[4,12292]{1,0:T(4,128)}, u32[]{:S(2)}, u32[]{:S(2)}) collective-permute-start(f32[4,12292]{1,0:T(4,128)} %pad_maximum_fusion.22), channel_id=1, source_target_pairs={{0,16},{4,20},{8,24},{12,28},{16,0},{20,4},{24,8},{28,12},{1,17},{... | collective-permute-start | bytes 590024 | tf_op jit(solution)/shard_map/ppermute | solution.py:715
  620.0 24.4 %all-to-all-start.4 = ((bf16[8,64,1408]{2,1,0:T(8,128)(2,1)}), bf16[8,64,1408]{2,1,0:T(8,128)(2,1)S(1)}, u32[]{:S(2)}, u32[]{:S(2)}) async-start(bf16[8,64,1408]{2,1,0:T(8,128)(2,1)} %bitcast.343), calls=%async_computation.8 | async-start | bytes 2883584 | tf_op jit(solution)/shard_map/all_to_all | solution.py:817
  644.4 18.9 %all-to-all-start.3 = ((bf16[8,64,1024]{2,1,0:T(8,128)(2,1)}), bf16[8,64,1024]{2,1,0:T(8,128)(2,1)S(1)}, u32[]{:S(2)}, u32[]{:S(2)}) async-start(bf16[8,64,1024]{2,1,0:T(8,128)(2,1)} %bitcast.87), calls=%async_computation.7 | async-start | bytes 2097152 | tf_op jit(solution)/shard_map/all_to_all | solution.py:817
  (112 other events, 1261.6 us)
Sparse Core Ops, SparseCore 0:
  10.2 48.9 all-gather.7
  60.7 114.3 all-gather.13
  177.2 33.0 all-gather.9
  212.3 105.5 all-gather.15
  319.9 33.2 all-gather.11
  355.9 55.0 reduce-scatter.4
  413.3 102.1 reduce-scatter.6
  517.8 79.5 reduce-scatter.10
  599.8 78.0 reduce-scatter.8

commit v6 on v5

--- a/solution.py
+++ b/solution.py
@@ -927,7 +927,7 @@
     proj = mm(h_in, mix_w)
     down_first = lax.all_gather(own_down[:, : D // 2], "batch", axis=0, tiled=True)
     prepared = mixer_prepare(proj.reshape(blocks + (-1,)), small, slots, resets, conv_l, aux)
-    prepared, moved_gu, down_first = lax.optimization_barrier((prepared, moved_gu, down_first))
+    prepared, moved_gu = lax.optimization_barrier((prepared, moved_gu))
     down_rest = lax.all_gather(own_down[:, D // 2 :], "batch", axis=0, tiled=True)
     gu_w = stacked(moved_gu)
     mixed, states, invs, deltas = mixer_scan(prepared, slots, batch_rows)

time: 700 us -> 726 us (1.037)
  waiting for transfers between devices: 278 us -> 291 us
  matrix products: 103 us -> 115 us
    all_gather x1, waiting for transfers between devices: 7.32 us -> 26.8 us  [shards(): lax.all_gather(own_down[:, :D // 2], 'batch', axis=0, tiled=True)]
    dot_general x9, matrix products: 31.6 us -> 42.3 us  [contract_cols(): lax.dot_general(left, right, (((1,), (1,)), ((), ())), preferred_element_...]
    unnamed x183 -> x167, local copies, waits for them, and re-layouts: 20.6 us -> 21.3 us
  transfers between devices with their start and end apart: 69 -> 69, of which waited for: 43 -> 44; matrix products, arithmetic and copies ran while one was open for 27% -> 29% of each run, Pallas kernels for 14% -> 13%
where the time goes in v6:
time: 726 us; the launch traced here: 716 us
  waiting for transfers between devices  291 us (40%)
  matrix products  115 us (16%)
  Pallas kernels  99 us (14%)
  local copies, waits for them, and re-layouts  74.4 us (10%)
  starting transfers between devices  67.4 us (9%)
  other arithmetic  27.1 us (4%)
  blocking collectives  26.2 us (4%)
  between operations  15.5 us (2%)
    ppermute x55, waiting for transfers between devices, swap(): lax.ppermute(value, axis, [(i, i ^ bit) for i in range(lax.axis_size(axis...  154 us
    all_gather x2, waiting for transfers between devices, stacked(): full = lax.all_gather(blocks, 'batch', axis=0, tiled=False)  52.5 us
    ppermute x55, starting transfers between devices, swap(): lax.ppermute(value, axis, [(i, i ^ bit) for i in range(lax.axis_size(axis...  46.1 us
    dot_general x9, matrix products, contract_cols(): lax.dot_general(left, right, (((1,), (1,)), ((), ())), preferred_element_...  42.3 us
    pallas_call x1, Pallas kernels, mixer_backward(): pl.pallas_call(partial(backward_kernel, heads, chunks), grid_spec=pltpu.P...  39.3 us
    dot_general x7, matrix products, mm(): return jnp.dot(left, right, preferred_element_type=f32)  38 us
    dot_general x6, matrix products, contract_rows(): lax.dot_general(left, right, (((0,), (0,)), ((), ())), preferred_element_...  34.6 us
    all_gather x1, waiting for transfers between devices, shards(): lax.all_gather(own_down[:, :D // 2], 'batch', axis=0, tiled=True)  26.8 us
  transfers between devices with their start and end apart: 69, of which 44 were waited for; matrix products, arithmetic and copies ran while one was open for 29% of the time, Pallas kernels for 13%

profile of v6, /device:TPU:0, one launch (start us, length us, event | category | flops | bytes accessed | tf_op | source)
XLA Modules:
  0.0 715.7 jit_solution(10671097058494916900)
XLA Ops:
  10.7 26.2 %all_to_all.30 = bf16[8,64,1536]{2,1,0:T(8,128)(2,1)} all-to-all(bf16[8,64,1536]{2,1,0:T(8,128)(2,1)S(1)} %copy.108), channel_id=1, replica_groups=mesh['seq'=8,'batch'=4] {'seq'}, dimensions={0} | all-to-all | bytes 3145728 | tf_op jit(solution)/shard_map/all_to_all | solution.py:817
  36.9 22.3 %all-gather.8.cloned.1.call-done = bf16[512,2048]{0,1:T(8,128)(2,1)} async-done(((bf16[128,2048]{0,1:T(8,128)(2,1)}), bf16[512,2048]{0,1:T(8,128)(2,1)}) %all-gather.8.cloned.1.call-update) | async-done | bytes 2097168 | tf_op jit(solution)/shard_map/all_gather | solution.py:867
  75.4 8.3 %collective-permute-done.1 = bf16[2,64,2048]{2,1,0:T(8,128)(2,1)S(1)} collective-permute-done((bf16[2,64,2048]{2,1,0:T(8,128)(2,1)S(1)}, bf16[2,64,2048]{2,1,0:T(8,128)(2,1)S(1)}, u32[]{:S(2)}, u32[]{:S(2)}) %collective-permute-start.1) | collective-permute-done | bytes 524320 | tf_op jit(solution)/shard_map/ppermute | solution.py:715
  99.1 7.7 %collective-permute-done.5 = bf16[1,64,32]{1,2,0:T(8,128)(2,1)S(1)} collective-permute-done((bf16[1,64,32]{1,2,0:T(8,128)(2,1)S(1)}, bf16[1,64,32]{1,2,0:T(8,128)(2,1)S(1)}, u32[]{:S(2)}, u32[]{:S(2)}) %collective-permute-start.5) | collective-permute-done | bytes 4128 | tf_op jit(solution)/shard_map/ppermute | solution.py:715
  129.2 45.8 %all-gather.14.cloned.1.call-done = bf16[32,64,1536]{2,1,0:T(8,128)(2,1)} async-done(((bf16[8,64,1536]{2,1,0:T(8,128)(2,1)}), bf16[32,64,1536]{2,1,0:T(8,128)(2,1)}) %all-gather.14.cloned.1.call-update) | async-done | bytes 6291472 | tf_op jit(solution)/shard_map/all_gather | solution.py:821
  175.0 11.8 %fusion.77.gate_ref = f32[1024,1536]{1,0:T(8,128)} fusion(bf16[2048,1536]{1,0:T(8,128)(2,1)} %bitcast.388, bf16[512,2048]{1,0:T(8,128)(2,1)} %bitcast.6, bf16[512,2048]{1,0:T(8,128)(2,1)} %bitcast.4), kind=kOutput, calls=%fused_computation.231 | convolution fusion | flops 6450839552 | bytes 16777216 | tf_op jit(solution)/shard_map/dot_general | solution.py:797
  186.8 16.1 %delta_prepare.1 = (f32[8,4,128,128]{3,2,1,0:T(8,128)}, f32[8,4,64,256]{3,2,1,0:T(8,128)}, f32[8,4,64,64]{3,2,1,0:T(8,128)}, f32[8,4,64,64]{3,2,1,0:T(8,128)}, f32[8,4,64,128]{3,2,1,0:T(8,128)}) custom-call(s32[8]{0:T(128)} %iota_xor_fusion.pos_ref, s32[2]{0:T(128)} %reset_ref.3, f32[2,2,4,64,1536]{4,3,2,1,0:T(8,128)} %bitcast.295, ...), custom_call_target="tpu_custom_call" | custom-call | flops 30000001024 | bytes 40000000 | tf_op jit(solution)/shard_map/delta_prepare/pallas_call | solution.py:403
  205.9 12.6 %delta_scan.1 = (f32[2,2,4,64,512]{4,3,2,1,0:T(8,128)}, f32[8,4,128,256]{3,2,1,0:T(8,128)}, f32[8,4,64,256]{3,2,1,0:T(8,128)}) custom-call(s32[8]{0:T(128)} %iota_xor_fusion.pos_ref, f32[8,4,128,128]{3,2,1,0:T(8,128)} %get-tuple-element.84.both_ref, f32[8,4,64,256]{3,2,1,0:T(8,128)} %get-tuple-element.85.value_ref, ...), custom_call_target="tpu_custom_call" | custom-call | flops 1000000 | bytes 1000 | tf_op jit(solution)/shard_map/delta_scan/pallas_call | solution.py:423
  247.9 10.3 %collective-permute-done.18.refs_4_ = bf16[2,64,2048]{2,1,0:T(8,128)(2,1)S(1)} collective-permute-done((bf16[2,64,2048]{2,1,0:T(8,128)(2,1)S(1)}, bf16[2,64,2048]{2,1,0:T(8,128)(2,1)S(1)}, u32[]{:S(2)}, u32[]{:S(2)}) %collective-permute-start.18) | collective-permute-done | bytes 524320 | tf_op jit(solution)/shard_map/ppermute | solution.py:715
  291.8 8.3 %collective-permute-done.21 = bf16[2,64,2048]{2,1,0:T(8,128)(2,1)S(1)} collective-permute-done((bf16[2,64,2048]{2,1,0:T(8,128)(2,1)S(1)}, bf16[2,64,2048]{2,1,0:T(8,128)(2,1)S(1)}, u32[]{:S(2)}, u32[]{:S(2)}) %collective-permute-start.21) | collective-permute-done | bytes 524320 | tf_op jit(solution)/shard_map/ppermute | solution.py:715
  302.4 6.7 all-gather.16.cloned.1.call-done
  313.4 10.2 %fusion.76 = f32[1024,1408]{0,1:T(8,128)S(1)} fusion(bf16[2048,1408]{1,0:T(8,128)(2,1)} %bitcast.393, bf16[512,2048]{1,0:T(8,128)(2,1)} %bitcast.48, bf16[512,2048]{1,0:T(8,128)(2,1)S(1)} %bitcast.323), kind=kOutput, calls=%fused_computation.230 | convolution fusion | flops 5913968640 | bytes 15728640 | tf_op jit(solution)/shard_map/dot_general | solution.py:797
  326.0 6.7 fusion.1
  333.0 10.8 %all-gather.12.cloned.1.call-done = bf16[704,1024]{1,0:T(8,128)(2,1)} async-done(((bf16[176,1024]{1,0:T(8,128)(2,1)}), bf16[704,1024]{1,0:T(8,128)(2,1)}) %all-gather.12.cloned.1.call-update) | async-done | bytes 1441808 | tf_op jit(solution)/shard_map/all_gather | solution.py:931
  352.8 26.8 %all-gather.10.cloned.1.call-done = bf16[704,1024]{1,0:T(8,128)(2,1)} async-done(((bf16[176,1024]{1,0:T(8,128)(2,1)}), bf16[704,1024]{1,0:T(8,128)(2,1)}) %all-gather.10.cloned.1.call-update) | async-done | bytes 1441808 | tf_op jit(solution)/shard_map/all_gather | solution.py:928
  379.6 7.2 %multiply_convert_fusion = (bf16[1024,704]{0,1:T(8,128)(2,1)S(1)}, bf16[1024,704]{0,1:T(8,128)(2,1)S(1)}) fusion(f32[1024,1408]{0,1:T(8,128)} %copy-done.10, f32[1024,704]{0,1:T(8,128)} %fusion.11, bf16[704,1024]{1,0:T(8,128)(2,1)} %all-gather.10.cloned.1.call-done, bf16[512,2048]{1,0:T(8,128)(2,1)} %bitcast.31, bf16[512,2048]{1,0:T(8,128)(2,1)} %bitcast.32), kind=kOutput, calls=%fused_computation.35 | convolution fusion | flops 1491402752 | bytes 17170432 | tf_op jit(solution)/shard_map/dot_general | solution.py:805
  386.8 7.6 %convolution_convert_fusion.8 = bf16[512,2048]{1,0:T(8,128)(2,1)} fusion(bf16[2048,1408]{1,0:T(8,128)(2,1)} %bitcast.394, bf16[1024,704]{0,1:T(8,128)(2,1)S(1)} %get-tuple-element.140, bf16[1024,704]{0,1:T(8,128)(2,1)S(1)} %get-tuple-element.139), kind=kOutput, calls=%fused_computation.30 | convolution fusion | flops 2956722176 | bytes 10747904 | tf_op jit(solution)/shard_map/dot_general | solution.py:805
  394.5 6.6 convolution_convert_fusion.9
  401.1 8.5 %convolution_convert_fusion = bf16[2048,1408]{1,0:T(8,128)(2,1)} fusion(bf16[1024,2048]{1,0:T(8,128)(2,1)S(1)} %copy-done.13, bf16[1024,704]{0,1:T(8,128)(2,1)S(1)} %get-tuple-element.139, bf16[1024,704]{0,1:T(8,128)(2,1)S(1)} %get-tuple-element.140), kind=kOutput, calls=%fused_computation.3 | convolution fusion | flops 5914230784 | bytes 12845056 | tf_op jit(solution)/shard_map/dot_general | solution.py:801
  421.2 7.5 %collective-permute-done.26.refs_2_ = bf16[2,64,2048]{2,1,0:T(8,128)(2,1)S(1)} collective-permute-done((bf16[2,64,2048]{2,1,0:T(8,128)(2,1)S(1)}, bf16[2,64,2048]{2,1,0:T(8,128)(2,1)S(1)}, u32[]{:S(2)}, u32[]{:S(2)}) %collective-permute-start.26) | collective-permute-done | bytes 524320 | tf_op jit(solution)/shard_map/ppermute | solution.py:715
  457.3 8.2 %collective-permute-done.31 = bf16[2,64,2048]{2,1,0:T(8,128)(2,1)S(1)} collective-permute-done((bf16[2,64,2048]{2,1,0:T(8,128)(2,1)S(1)}, bf16[2,64,2048]{2,1,0:T(8,128)(2,1)S(1)}, u32[]{:S(2)}, u32[]{:S(2)}) %collective-permute-start.31) | collective-permute-done | bytes 524320 | tf_op jit(solution)/shard_map/ppermute | solution.py:715
  478.3 5.9 gated_norm_back.1
  499.1 12.1 %collective-permute-done.41.refs_2_ = bf16[2,64,2048]{2,1,0:T(8,128)(2,1)S(1)} collective-permute-done((bf16[2,64,2048]{2,1,0:T(8,128)(2,1)S(1)}, bf16[2,64,2048]{2,1,0:T(8,128)(2,1)S(1)}, u32[]{:S(2)}, u32[]{:S(2)}) %collective-permute-start.41) | collective-permute-done | bytes 524320 | tf_op jit(solution)/shard_map/ppermute | solution.py:715
  519.7 39.3 %delta_backward.1 = (bf16[2,2,4,64,1024]{4,3,2,1,0:T(8,128)(2,1)}, bf16[2,2,4,64,128]{4,3,2,1,0:T(8,128)(2,1)}, f32[8,1024]{1,0:T(8,128)}, f32[8,128]{1,0:T(8,128)}) custom-call(s32[8]{0:T(128)} %iota_xor_fusion.pos_ref, s32[2]{0:T(128)} %reset_ref.3, f32[2,2,4,64,1536]{4,3,2,1,0:T(8,128)} %bitcast.298, f32[2,2,4,64,128]{4,3,2,1,0:T(8,128)} %bitcast.404, ...), custom_call_target="tpu_custom_call" | custom-call | flops 30000001024 | bytes 40000000 | tf_op jit(solution)/shard_map/delta_backward/pallas_call | solution.py:464
  559.0 7.5 %convolution_convert_fusion.1 = bf16[2048,1024]{1,0:T(8,128)(2,1)S(1)} fusion(bf16[1024,1024]{1,0:T(8,128)(2,1)} %bitcast.331, bf16[512,2048]{1,0:T(8,128)(2,1)} %bitcast.6, bf16[512,2048]{1,0:T(8,128)(2,1)} %bitcast.4), kind=kOutput, calls=%fused_computation.17 | convolution fusion | flops 4305453056 | bytes 10485760 | tf_op jit(solution)/shard_map/dot_general | solution.py:801
  587.4 6.2 fusion.16
  601.1 5.5 collective-permute-done.51
  608.5 14.3 %all-to-all-done.2 = bf16[4,8,64,1024]{3,2,0,1:T(8,128)(2,1)} async-done(((bf16[4,8,64,1024]{3,2,0,1:T(8,128)(2,1)}), bf16[4,8,64,1024]{3,2,0,1:T(8,128)(2,1)}, u32[]{:S(2)}, u32[]{:S(2)}) %all-to-all-start.2) | async-done | bytes 4194336 | tf_op jit(solution)/shard_map/all_to_all | solution.py:977
  635.9 8.1 %collective-permute-done.38.refs_4_ = bf16[2,64,2048]{2,1,0:T(8,128)(2,1)S(1)} collective-permute-done((bf16[2,64,2048]{2,1,0:T(8,128)(2,1)S(1)}, bf16[2,64,2048]{2,1,0:T(8,128)(2,1)S(1)}, u32[]{:S(2)}, u32[]{:S(2)}) %collective-permute-start.38) | collective-permute-done | bytes 524320 | tf_op jit(solution)/shard_map/ppermute | solution.py:715
  666.6 6.4 collective-permute-done.46
  679.7 5.9 collective-permute-done.48
  694.7 9.6 %reduce-scatter.9.cloned.1.call-done = bf16[1,8,64,1024]{3,2,1,0:T(8,128)(2,1)} async-done(((bf16[4,8,64,1024]{3,2,1,0:T(8,128)(2,1)}), bf16[1,8,64,1024]{3,2,1,0:T(8,128)(2,1)}) %reduce-scatter.9.cloned.1.call-update) | async-done | bytes 1048592 | tf_op jit(solution)/shard_map/reduce_scatter | solution.py:982
  (451 shorter events, 303.1 us)
Async XLA Ops:
  7.2 51.9 %all-gather.8.cloned.1.call-start = ((), (), s32[]{:S(2)}) async-start(), calls=%async_computation.10 | async-start | bytes 2621440 | tf_op jit(solution)/shard_map/all_gather | solution.py:867
  9.4 165.6 %all-gather.14.cloned.1.call-start = ((), (), s32[]{:S(2)}) async-start(), calls=%async_computation.17 | async-start | bytes 7864320 | tf_op jit(solution)/shard_map/all_gather | solution.py:821
  88.1 36.8 %collective-permute-start.4 = (bf16[2,4,64,2048]{3,2,1,0:T(8,128)(2,1)}, bf16[2,4,64,2048]{3,2,1,0:T(8,128)(2,1)}, u32[]{:S(2)}, u32[]{:S(2)}) collective-permute-start(bf16[2,4,64,2048]{3,2,1,0:T(8,128)(2,1)} %bitcast.5), channel_id=1, source_target_pairs={{0,4},{4,0},{8,12},{12,8},{16,20},{20,16},{24,28},{28,24},{1,5},{5... | collective-permute-start | bytes 6291464 | tf_op jit(solution)/shard_map/ppermute | solution.py:715
  119.9 83.0 %all-to-all-start.1 = ((bf16[8,64,1408]{2,1,0:T(8,128)(2,1)}), bf16[8,64,1408]{2,1,0:T(8,128)(2,1)S(1)}, u32[]{:S(2)}, u32[]{:S(2)}) async-start(bf16[8,64,1408]{2,1,0:T(8,128)(2,1)} %reshape.473), calls=%async_computation.1 | async-start | bytes 2883584 | tf_op jit(solution)/shard_map/all_to_all | solution.py:817
  123.5 185.6 %all-gather.16.cloned.1.call-start = ((), (), s32[]{:S(2)}) async-start(), calls=%async_computation.18 | async-start | bytes 7208960 | tf_op jit(solution)/shard_map/all_gather | solution.py:821
  204.0 139.7 %all-gather.12.cloned.1.call-start = ((), (), s32[]{:S(2)}) async-start(), calls=%async_computation.12 | async-start | bytes 1802240 | tf_op jit(solution)/shard_map/all_gather | solution.py:931
  226.5 16.6 %collective-permute-start.15 = (bf16[2,4,64,2048]{3,2,1,0:T(8,128)(2,1)}, bf16[2,4,64,2048]{3,2,1,0:T(8,128)(2,1)S(1)}, u32[]{:S(2)}, u32[]{:S(2)}) collective-permute-start(bf16[2,4,64,2048]{3,2,1,0:T(8,128)(2,1)} %bitcast.30), channel_id=1, source_target_pairs={{0,4},{4,0},{8,12},{12,8},{16,20},{20,16},{24,28},{28,24},{1,5},{5... | collective-permute-start | bytes 6291464 | tf_op jit(solution)/shard_map/ppermute | solution.py:715
  229.6 15.9 %collective-permute-start.12 = (bf16[1,64,2048]{2,1,0:T(8,128)(2,1)S(1)}, bf16[1,64,2048]{2,1,0:T(8,128)(2,1)}, u32[]{:S(2)}, u32[]{:S(2)}) collective-permute-start(bf16[1,64,2048]{2,1,0:T(8,128)(2,1)S(1)} %get-tuple-element.162), channel_id=1, source_target_pairs={{0,16},{4,20},{8,24},{12,28},{16,0},{20,4},{24,8},{28,12},{1,17},{... | collective-permute-start | bytes 786440 | tf_op jit(solution)/shard_map/ppermute | solution.py:715
  235.2 144.5 %all-gather.10.cloned.1.call-start = ((), (), s32[]{:S(2)}) async-start(), calls=%async_computation.11 | async-start | bytes 1802240 | tf_op jit(solution)/shard_map/all_gather | solution.py:928
  238.2 29.4 %collective-permute-start.11 = (bf16[2,64,2048]{2,1,0:T(8,128)(2,1)S(1)}, bf16[2,64,2048]{2,1,0:T(8,128)(2,1)S(1)}, u32[]{:S(2)}, u32[]{:S(2)}) collective-permute-start(bf16[2,64,2048]{2,1,0:T(8,128)(2,1)S(1)} %pad_maximum_fusion.14), channel_id=1, source_target_pairs={{0,16},{4,20},{8,24},{12,28},{16,0},{20,4},{24,8},{28,12},{1,17},{... | collective-permute-start | bytes 1572872 | tf_op jit(solution)/shard_map/ppermute | solution.py:715
  243.3 14.9 %collective-permute-start.18 = (bf16[2,64,2048]{2,1,0:T(8,128)(2,1)S(1)}, bf16[2,64,2048]{2,1,0:T(8,128)(2,1)S(1)}, u32[]{:S(2)}, u32[]{:S(2)}) collective-permute-start(bf16[2,64,2048]{2,1,0:T(8,128)(2,1)S(1)} %fusion.34), channel_id=1, source_target_pairs={{0,8},{4,12},{8,0},{12,4},{16,24},{20,28},{24,16},{28,20},{1,9},{5... | collective-permute-start | bytes 1572872 | tf_op jit(solution)/shard_map/ppermute | solution.py:715
  244.9 19.4 %collective-permute-start.16 = (bf16[2,64,2048]{2,1,0:T(8,128)(2,1)S(1)}, bf16[2,64,2048]{2,1,0:T(8,128)(2,1)S(1)}, u32[]{:S(2)}, u32[]{:S(2)}) collective-permute-start(bf16[2,64,2048]{2,1,0:T(8,128)(2,1)S(1)} %fusion.31), channel_id=1, source_target_pairs={{0,16},{4,20},{8,24},{12,28},{16,0},{20,4},{24,8},{28,12},{1,17},{... | collective-permute-start | bytes 1572872 | tf_op jit(solution)/shard_map/ppermute | solution.py:715
  247.3 38.6 %collective-permute-start.13 = (bf16[2,64,2048]{2,1,0:T(8,128)(2,1)}, bf16[2,64,2048]{2,1,0:T(8,128)(2,1)}, u32[]{:S(2)}, u32[]{:S(2)}) collective-permute-start(bf16[2,64,2048]{2,1,0:T(8,128)(2,1)} %pad_maximum_fusion.15), channel_id=1, source_target_pairs={{0,8},{4,12},{8,0},{12,4},{16,24},{20,28},{24,16},{28,20},{1,9},{5... | collective-permute-start | bytes 1572872 | tf_op jit(solution)/shard_map/ppermute | solution.py:715
  285.3 14.8 %collective-permute-start.21 = (bf16[2,64,2048]{2,1,0:T(8,128)(2,1)S(1)}, bf16[2,64,2048]{2,1,0:T(8,128)(2,1)S(1)}, u32[]{:S(2)}, u32[]{:S(2)}) collective-permute-start(bf16[2,64,2048]{2,1,0:T(8,128)(2,1)S(1)} %pad_maximum_fusion.16), channel_id=1, source_target_pairs={{0,16},{4,20},{8,24},{12,28},{16,0},{20,4},{24,8},{28,12},{1,17},{... | collective-permute-start | bytes 1572872 | tf_op jit(solution)/shard_map/ppermute | solution.py:715
  287.8 22.3 %collective-permute-start.14 = (bf16[2,4,64,2048]{3,2,1,0:T(8,128)(2,1)}, bf16[2,4,64,2048]{3,2,1,0:T(8,128)(2,1)}, u32[]{:S(2)}, u32[]{:S(2)}) collective-permute-start(bf16[2,4,64,2048]{3,2,1,0:T(8,128)(2,1)} %bitcast.25), channel_id=1, source_target_pairs={{0,4},{4,0},{8,12},{12,8},{16,20},{20,16},{24,28},{28,24},{1,5},{5... | collective-permute-start | bytes 6291464 | tf_op jit(solution)/shard_map/ppermute | solution.py:715
  310.1 133.6 %reduce-scatter.5.cloned.1.call-start = ((), (), s32[]{:S(2)}) async-start(), calls=%async_computation.13 | async-start | bytes 3604480 | tf_op jit(solution)/shard_map/reduce_scatter | solution.py:826
  332.8 226.3 %reduce-scatter.7.cloned.1.call-start = ((), (), s32[]{:S(2)}) async-start(), calls=%async_computation.14 | async-start | bytes 7208960 | tf_op jit(solution)/shard_map/reduce_scatter | solution.py:826
  409.6 246.4 %reduce-scatter.11.cloned.1.call-start = ((), (), s32[]{:S(2)}) async-start(), calls=%async_computation.16 | async-start | bytes 5242880 | tf_op jit(solution)/shard_map/reduce_scatter | solution.py:826
  414.7 14.0 %collective-permute-start.26 = (bf16[2,64,2048]{2,1,0:T(8,128)(2,1)S(1)}, bf16[2,64,2048]{2,1,0:T(8,128)(2,1)S(1)}, u32[]{:S(2)}, u32[]{:S(2)}) collective-permute-start(bf16[2,64,2048]{2,1,0:T(8,128)(2,1)S(1)} %get-tuple-element.150), channel_id=1, source_target_pairs={{0,16},{4,20},{8,24},{12,28},{16,0},{20,4},{24,8},{28,12},{1,17},{... | collective-permute-start | bytes 1572872 | tf_op jit(solution)/shard_map/ppermute | solution.py:715
  454.5 14.7 %collective-permute-start.40 = (bf16[2,4,64,2048]{3,2,1,0:T(8,128)(2,1)S(1)}, bf16[2,4,64,2048]{3,2,1,0:T(8,128)(2,1)}, u32[]{:S(2)}, u32[]{:S(2)}) collective-permute-start(bf16[2,4,64,2048]{3,2,1,0:T(8,128)(2,1)S(1)} %bitcast.396), channel_id=1, source_target_pairs={{0,4},{4,0},{8,12},{12,8},{16,20},{20,16},{24,28},{28,24},{1,5},{5... | collective-permute-start | bytes 6291464 | tf_op jit(solution)/shard_map/ppermute | solution.py:715
  497.2 14.1 %collective-permute-start.41 = (bf16[2,64,2048]{2,1,0:T(8,128)(2,1)S(1)}, bf16[2,64,2048]{2,1,0:T(8,128)(2,1)S(1)}, u32[]{:S(2)}, u32[]{:S(2)}) collective-permute-start(bf16[2,64,2048]{2,1,0:T(8,128)(2,1)S(1)} %get-tuple-element.146), channel_id=1, source_target_pairs={{0,16},{4,20},{8,24},{12,28},{16,0},{20,4},{24,8},{28,12},{1,17},{... | collective-permute-start | bytes 1572872 | tf_op jit(solution)/shard_map/ppermute | solution.py:715
  514.4 60.2 %collective-permute-start.42 = (bf16[64,2048]{1,0:T(8,128)(2,1)}, bf16[64,2048]{1,0:T(8,128)(2,1)S(1)}, u32[]{:S(2)}, u32[]{:S(2)}) collective-permute-start(bf16[64,2048]{1,0:T(8,128)(2,1)} %get-tuple-element.142), channel_id=1, source_target_pairs={{0,8},{4,12},{8,0},{12,4},{16,24},{20,28},{24,16},{28,20},{1,9},{5... | collective-permute-start | bytes 786440 | tf_op jit(solution)/shard_map/ppermute | solution.py:715
  514.9 59.7 %collective-permute-start.44 = (bf16[64,2048]{1,0:T(8,128)(2,1)S(1)}, bf16[64,2048]{1,0:T(8,128)(2,1)S(1)}, u32[]{:S(2)}, u32[]{:S(2)}) collective-permute-start(bf16[64,2048]{1,0:T(8,128)(2,1)S(1)} %get-tuple-element.141), channel_id=1, source_target_pairs={{0,16},{4,20},{8,24},{12,28},{16,0},{20,4},{24,8},{28,12},{1,17},{... | collective-permute-start | bytes 786440 | tf_op jit(solution)/shard_map/ppermute | solution.py:715
  515.6 53.4 %all-to-all-start.5 = ((bf16[8,64,704]{2,1,0:T(8,128)(2,1)}), bf16[8,64,704]{2,1,0:T(8,128)(2,1)S(1)}, u32[]{:S(2)}, u32[]{:S(2)}) async-start(bf16[8,64,704]{2,1,0:T(8,128)(2,1)} %bitcast.62), calls=%async_computation.9 | async-start | bytes 1572864 | tf_op jit(solution)/shard_map/all_to_all | solution.py:817
  569.0 53.9 %all-to-all-start.2 = ((bf16[4,8,64,1024]{3,2,0,1:T(8,128)(2,1)}), bf16[4,8,64,1024]{3,2,0,1:T(8,128)(2,1)}, u32[]{:S(2)}, u32[]{:S(2)}) async-start(bf16[4,8,64,1024]{3,2,0,1:T(8,128)(2,1)} %copy.124), calls=%async_computation.4 | async-start | bytes 8388608 | tf_op jit(solution)/shard_map/all_to_all | solution.py:977
  573.7 130.6 %reduce-scatter.9.cloned.1.call-start = ((), (), s32[]{:S(2)}) async-start(), calls=%async_computation.15 | async-start | bytes 5242880 | tf_op jit(solution)/shard_map/reduce_scatter | solution.py:982
  595.7 32.9 %collective-permute-start.35 = (bf16[2,4,64,2048]{3,2,1,0:T(8,128)(2,1)}, bf16[2,4,64,2048]{3,2,1,0:T(8,128)(2,1)}, u32[]{:S(2)}, u32[]{:S(2)}) collective-permute-start(bf16[2,4,64,2048]{3,2,1,0:T(8,128)(2,1)} %bitcast.75), channel_id=1, source_target_pairs={{0,4},{4,0},{8,12},{12,8},{16,20},{20,16},{24,28},{28,24},{1,5},{5... | collective-permute-start | bytes 6291464 | tf_op jit(solution)/shard_map/ppermute | solution.py:715
  606.6 21.3 %collective-permute-start.52 = (f32[1,12292]{1,0:T(1,128)S(1)}, f32[1,12292]{1,0:T(1,128)S(1)}, u32[]{:S(2)}, u32[]{:S(2)}) collective-permute-start(f32[1,12292]{1,0:T(1,128)S(1)} %broadcast_in_dim.15), channel_id=1, source_target_pairs={{0,4},{4,0},{8,12},{12,8},{16,20},{20,16},{24,28},{28,24},{1,5},{5... | collective-permute-start | bytes 147512 | tf_op jit(solution)/shard_map/ppermute | solution.py:715
  632.9 14.9 %collective-permute-start.36 = (bf16[2,64,2048]{2,1,0:T(8,128)(2,1)S(1)}, bf16[2,64,2048]{2,1,0:T(8,128)(2,1)S(1)}, u32[]{:S(2)}, u32[]{:S(2)}) collective-permute-start(bf16[2,64,2048]{2,1,0:T(8,128)(2,1)S(1)} %fusion.28), channel_id=1, source_target_pairs={{0,16},{4,20},{8,24},{12,28},{16,0},{20,4},{24,8},{28,12},{1,17},{... | collective-permute-start | bytes 1572872 | tf_op jit(solution)/shard_map/ppermute | solution.py:715
  634.3 19.7 %collective-permute-start.54 = (f32[4,12292]{1,0:T(4,128)}, f32[4,12292]{1,0:T(4,128)}, u32[]{:S(2)}, u32[]{:S(2)}) collective-permute-start(f32[4,12292]{1,0:T(4,128)} %pad_maximum_fusion.22), channel_id=1, source_target_pairs={{0,16},{4,20},{8,24},{12,28},{16,0},{20,4},{24,8},{28,12},{1,17},{... | collective-permute-start | bytes 590024 | tf_op jit(solution)/shard_map/ppermute | solution.py:715
  650.2 24.4 %all-to-all-start.4 = ((bf16[8,64,1408]{2,1,0:T(8,128)(2,1)}), bf16[8,64,1408]{2,1,0:T(8,128)(2,1)S(1)}, u32[]{:S(2)}, u32[]{:S(2)}) async-start(bf16[8,64,1408]{2,1,0:T(8,128)(2,1)} %bitcast.341), calls=%async_computation.8 | async-start | bytes 2883584 | tf_op jit(solution)/shard_map/all_to_all | solution.py:817
  674.5 18.9 %all-to-all-start.3 = ((bf16[8,64,1024]{2,1,0:T(8,128)(2,1)}), bf16[8,64,1024]{2,1,0:T(8,128)(2,1)S(1)}, u32[]{:S(2)}, u32[]{:S(2)}) async-start(bf16[8,64,1024]{2,1,0:T(8,128)(2,1)} %bitcast.87), calls=%async_computation.7 | async-start | bytes 2097152 | tf_op jit(solution)/shard_map/all_to_all | solution.py:817
  (104 other events, 1223.3 us)
Sparse Core Ops, SparseCore 0:
  10.2 48.9 all-gather.7
  60.7 114.2 all-gather.13
  204.2 104.8 all-gather.15
  310.5 33.2 all-gather.11
  345.8 33.8 all-gather.9
  382.4 55.0 reduce-scatter.4
  439.8 102.1 reduce-scatter.6
  544.2 79.5 reduce-scatter.10
  628.0 76.2 reduce-scatter.8
